TPU v7x, 32 devices: a whole 2x2x4 slice. The times are simulated.
32 devices in a mesh: blk: 8 (over z, y), head: 4 (over x, core).
Axes of the slice: x: 2, y: 2, z: 4, core: 2. Of those that a mesh axis runs over, the one named last changes fastest.
Arguments:
- layer_entry_vectors: bfloat16 [64, 16, 2048], P('blk', None, 'head'), may hold values from -6 to 6
- guessed_lookup_vectors: bfloat16 [64, 16, 2048], P('blk', None, 'head'), may hold values from -3 to 3
- guessed_content_vectors: bfloat16 [64, 16, 2048], P('blk', None, 'head'), may hold values from -6 to 6
- gating_query: bfloat16 [64, 16, 2048], P('blk', 'head'), may hold values from -6 to 6
- lane_memory_store: float32 [4, 1024, 2048], P('head', 'blk'), may hold values from -3 to 3
- prior_step_store: float32 [4, 1024, 32], P('head', 'blk'), may hold values from -6 to 6
- fading_blend_ratio: float32 [2048], P('head'), may hold values from 0 to 1
- learning_speed_blend: float32 [2048], P('head'), may hold values from 0 to 1
- fading_left_factor: bfloat16 [2048, 96], P('head'), may hold values from -0.125 to 0.125
- fading_right_factor: bfloat16 [96, 2048], P(None, 'head'), may hold values from -0.625 to 0.625
- fading_offset: float32 [2048], P('head'), may hold values from -6 to 1
- learning_speed_left: bfloat16 [2048, 96], P('head'), may hold values from -0.125 to 0.125
- learning_speed_right: bfloat16 [96, 2048], P(None, 'head'), may hold values from -0.625 to 0.625
- learning_speed_offset: float32 [2048], P('head'), may hold values from -2 to 2
- erasing_lookup_factor: float32 [2048], P('head'), may hold values from 0.1 to 1.9
- written_lookup_factor: float32 [2048], P('head'), may hold values from 0 to 1
- present_reward_factors: float32 [2048], P('head'), may hold values from -3 to 3
- lane_standard_factor: float32 [2048], P('head'), may hold values from 0.1 to 1.9
- lane_standard_offset: float32 [2048], P('head'), may hold values from -2 to 2
- caller_memory_directory: int32 [64, 32, 2], P(None, 'head'), may hold values from 0 to 1023, as said below
- kept_target_place: int32 [64, 32, 2], P(None, 'head'), may hold values from 0 to 1023, as said below
- caller_sequence: int32 [64], replicated, may hold values from 0 to 63, as said below
- approved_guesses: int32 [64], replicated, may hold values from 0 to 16
Outputs:
- temporal_blend_result: bfloat16 [64, 16, 2048], P('blk', None, 'head')
- new_states: float32 [4, 1024, 2048], P('head', 'blk')
- new_edges: float32 [4, 1024, 32], P('head', 'blk')
Inputs may be any that keep to these rules, and one draw needn't show every extreme that they name: `caller_memory_directory`: every entry names a slot of the pool of head group h // 8; all entries of one head group are distinct and cover its 1024 slots. For the positions p of one blk index, taken through q = caller_sequence[p], exactly 16 of the slots of each head group lie on each blk index (slot // 128). `kept_target_place`: same rules as the page table: every slot of a head group is written exactly once, and one blk index's positions write exactly 16 slots of each head group on each blk index. `caller_sequence`: A permutation of the 64 requests.
All inputs are finite; a program needn't handle non-finite values.
Results may differ from a plain program's by a relative error of at most 0.006.
Values may be sent and summed in bfloat16 or wider, within the bound.
No kernel may reach another device: no remote copies, remote signals or barrier semaphores. Data moves between devices by JAX's collectives and lax.ppermute only.
A program may use at most 64 MiB of HBM per device.

v0:
```python
import jax
import jax.numpy as jnp
from jax import lax
from jax.sharding import PartitionSpec as P

EPSILON = 1e-05
NORM_EPSILON = 0.00064


def local(
    layer_entry_vectors,
    guessed_lookup_vectors,
    guessed_content_vectors,
    gating_query,
    lane_memory_store,
    prior_step_store,
    fading_blend_ratio,
    learning_speed_blend,
    fading_left_factor,
    fading_right_factor,
    fading_offset,
    learning_speed_left,
    learning_speed_right,
    learning_speed_offset,
    erasing_lookup_factor,
    written_lookup_factor,
    present_reward_factors,
    lane_standard_factor,
    lane_standard_offset,
    caller_memory_directory,
    kept_target_place,
    caller_sequence,
    approved_guesses,
):
    blocks = lax.axis_size("blk")
    me_block = lax.axis_index("blk")
    requests_on_device = layer_entry_vectors.shape[0]
    draft_length = layer_entry_vectors.shape[1]
    width_on_device = layer_entry_vectors.shape[2]
    heads_on_device = caller_memory_directory.shape[1]
    halves = caller_memory_directory.shape[2]
    slot_dev = lane_memory_store.shape[1]
    per_peer = slot_dev // blocks
    head_width = width_on_device // heads_on_device
    slot_rows = head_width // halves
    slot_base = me_block * slot_dev
    requests = lax.dynamic_slice_in_dim(
        caller_sequence, me_block * requests_on_device, requests_on_device
    )
    counts = approved_guesses[requests]
    wanted = caller_memory_directory[requests].reshape(slot_dev)
    targets = kept_target_place[requests].reshape(slot_dev)
    item_ids = jnp.arange(slot_dev, dtype=jnp.int32)
    fetch_sort = jnp.argsort(wanted // slot_dev * slot_dev + item_ids)
    fetch_back = jnp.argsort(fetch_sort)
    asked_for = lax.all_to_all(
        wanted[fetch_sort].reshape(blocks, per_peer), "blk", split_axis=0, concat_axis=0, tiled=True
    )
    local_slots = asked_for.reshape(slot_dev) - slot_base
    got_states, got_edges = (
        lax.all_to_all(
            lane_memory_store[0][local_slots]
            .reshape(blocks, per_peer, slot_rows * head_width)
            .astype(jnp.bfloat16),
            "blk",
            split_axis=0,
            concat_axis=0,
            tiled=True,
        ).astype(jnp.float32),
        lax.all_to_all(
            prior_step_store[0][local_slots]
            .reshape(blocks, per_peer, slot_rows)
            .astype(jnp.bfloat16),
            "blk",
            split_axis=0,
            concat_axis=0,
            tiled=True,
        ).astype(jnp.float32),
    )
    recept_rows = lax.all_to_all(gating_query, "head", split_axis=2, concat_axis=1, tiled=True)
    current = layer_entry_vectors.astype(jnp.float32)
    row_count = requests_on_device * draft_length
    edge_first = got_edges.reshape(slot_dev, slot_rows)[fetch_back].reshape(
        requests_on_device, width_on_device
    )
    previous = jnp.concatenate([edge_first[:, None, :], current[:, :-1]], axis=1)
    shift_delta = previous - current
    mixed_decay = (
        (current + shift_delta * fading_blend_ratio)
        .astype(jnp.bfloat16)
        .reshape(row_count, width_on_device)
    )
    mixed_rate = (
        (current + shift_delta * learning_speed_blend)
        .astype(jnp.bfloat16)
        .reshape(row_count, width_on_device)
    )
    partial_terms = jnp.concatenate(
        [
            jnp.dot(mixed_decay, fading_left_factor, preferred_element_type=jnp.float32),
            jnp.dot(mixed_rate, learning_speed_left, preferred_element_type=jnp.float32),
        ],
        axis=1,
    )
    summed_rows = lax.psum(partial_terms.astype(jnp.bfloat16), "head").astype(jnp.float32)
    low_rank_weight = fading_left_factor.shape[1]
    decay_inner = jnp.tanh(summed_rows[:, :low_rank_weight]).astype(jnp.bfloat16)
    rate_inner = summed_rows[:, low_rank_weight:].astype(jnp.bfloat16)
    decay_term = jnp.dot(
        decay_inner, fading_right_factor, preferred_element_type=jnp.float32
    ).reshape(requests_on_device, draft_length, width_on_device)
    rate_term = jnp.dot(
        rate_inner, learning_speed_right, preferred_element_type=jnp.float32
    ).reshape(requests_on_device, draft_length, width_on_device)
    forget = jnp.exp(-jnp.exp(-jax.nn.softplus(-(fading_offset + decay_term)) - 0.5))
    in_rate = jax.nn.sigmoid(learning_speed_offset + rate_term)
    key_full = guessed_lookup_vectors.astype(jnp.float32)
    grouped = (key_full * erasing_lookup_factor).reshape(
        requests_on_device, draft_length, heads_on_device, head_width
    )
    unit_key = grouped * lax.rsqrt(jnp.sum(grouped * grouped, axis=-1, keepdims=True) + EPSILON)
    adjusted_lookup = key_full * (1.0 + (in_rate - 1.0) * written_lookup_factor)
    content_lines = guessed_content_vectors.astype(jnp.float32)
    gating_query_lines = recept_rows.astype(jnp.float32)
    start_states = got_states.reshape(slot_dev, slot_rows * head_width)[fetch_back].reshape(
        requests_on_device, heads_on_device, head_width, head_width
    )

    def by_step(array):
        return jnp.moveaxis(
            array.reshape(requests_on_device, draft_length, heads_on_device, head_width), 1, 0
        )

    def advance(carried, per_step):
        carry_state, accepted_state = carried
        step_index, forget_t, unit_t, rate_t, key_t, value_t, recept_t = per_step
        projected = jnp.sum(carry_state * unit_t[:, :, None, :], axis=-1)
        carry_state = (
            carry_state * forget_t[:, :, None, :]
            - projected[..., None] * (rate_t * unit_t)[:, :, None, :]
            + value_t[..., None] * key_t[:, :, None, :]
        )
        output = jnp.sum(carry_state * recept_t[:, :, None, :], axis=-1)
        accepted_state = jnp.where(
            (counts == step_index + 1)[:, None, None, None], carry_state, accepted_state
        )
        return ((carry_state, accepted_state), output)

    step_ids = jnp.arange(draft_length, dtype=jnp.int32)
    carried, outputs = lax.scan(
        advance,
        (start_states, start_states),
        (
            step_ids,
            by_step(forget),
            by_step(unit_key),
            by_step(in_rate),
            by_step(adjusted_lookup),
            by_step(content_lines),
            by_step(gating_query_lines),
        ),
    )
    outputs = jnp.moveaxis(outputs, 0, 1)
    average = jnp.mean(outputs, axis=-1, keepdims=True)
    centered = outputs - average
    variance = jnp.mean(centered * centered, axis=-1, keepdims=True)
    standardized_lines = centered * lax.rsqrt(
        variance + NORM_EPSILON
    ) * lane_standard_factor.reshape(heads_on_device, head_width) + lane_standard_offset.reshape(
        heads_on_device, head_width
    )
    present_reward_term = jnp.sum(
        (gating_query_lines * adjusted_lookup * present_reward_factors).reshape(
            requests_on_device, draft_length, heads_on_device, head_width
        ),
        axis=-1,
        keepdims=True,
    ) * content_lines.reshape(requests_on_device, draft_length, heads_on_device, head_width)
    temporal_blend_result = (
        (standardized_lines + present_reward_term)
        .astype(jnp.bfloat16)
        .reshape(requests_on_device, draft_length, width_on_device)
    )
    last_token = jnp.maximum(counts - 1, 0)
    picked = jnp.take_along_axis(current, last_token[:, None, None], axis=1)[:, 0]
    new_edge_rows = jnp.where((counts > 0)[:, None], picked, edge_first)
    return_sort = jnp.argsort(targets // slot_dev * slot_dev + item_ids)
    send_states = (
        carried[1]
        .reshape(slot_dev, slot_rows * head_width)[return_sort]
        .reshape(blocks, per_peer, slot_rows * head_width)
    )
    send_edges = new_edge_rows.reshape(slot_dev, slot_rows)[return_sort].reshape(
        blocks, per_peer, slot_rows
    )
    back_states, back_edges, back_slots = (
        lax.all_to_all(send_states, "blk", split_axis=0, concat_axis=0, tiled=True),
        lax.all_to_all(send_edges, "blk", split_axis=0, concat_axis=0, tiled=True),
        lax.all_to_all(
            targets[return_sort].reshape(blocks, per_peer),
            "blk",
            split_axis=0,
            concat_axis=0,
            tiled=True,
        ),
    )
    placing = jnp.argsort(back_slots.reshape(slot_dev) - slot_base)
    new_states = back_states.reshape(slot_dev, slot_rows * head_width)[placing][None]
    new_edges = back_edges.reshape(slot_dev, slot_rows)[placing][None]
    return (temporal_blend_result, new_states, new_edges)


def solution(mesh):
    return jax.shard_map(
        local,
        mesh=mesh,
        in_specs=(
            P("blk", None, "head"),
            P("blk", None, "head"),
            P("blk", None, "head"),
            P("blk", "head", None),
            P("head", "blk", None),
            P("head", "blk", None),
            P("head"),
            P("head"),
            P("head", None),
            P(None, "head"),
            P("head"),
            P("head", None),
            P(None, "head"),
            P("head"),
            P("head"),
            P("head"),
            P("head"),
            P("head"),
            P("head"),
            P(None, "head", None),
            P(None, "head", None),
            P(),
            P(),
        ),
        out_specs=(P("blk", None, "head"), P("head", "blk", None), P("head", "blk", None)),
        check_vma=False,
    )
```

profile of v0, /device:TPU:0, one launch (start us, length us, event | category | flops | bytes accessed | tf_op | source)
XLA Modules:
  0.0 382.0 jit_solution(14699735648283972944)
XLA Ops:
  3.2 2.5 sort.59
  5.8 1.2 gather_fusion.1
  7.7 7.3 %all-to-all-start = ((s32[8,1,16]{2,1,0:T(1,128)}), s32[8,1,16]{2,1,0:T(1,128)S(1)}, u32[]{:S(2)}, u32[]{:S(2)}) async-start(s32[8,1,16]{2,1,0:T(1,128)} %bitcast.9), calls=%async_computation | async-start | bytes 8192 | tf_op jit(solution)/shard_map/all_to_all | solution.py:56
  14.9 1.3 gather_fusion.6
  18.5 2.5 sort.61
  21.0 2.5 sort.60
  23.6 1.2 gather_fusion.9
  25.5 6.0 %all-to-all-start.5 = ((s32[8,1,16]{2,1,0:T(1,128)}), s32[8,1,16]{2,1,0:T(1,128)S(1)}, u32[]{:S(2)}, u32[]{:S(2)}) async-start(s32[8,1,16]{2,1,0:T(1,128)} %bitcast.31), calls=%async_computation.5 | async-start | bytes 8192 | tf_op jit(solution)/shard_map/all_to_all | solution.py:199
  31.6 6.2 %all-to-all-done.5 = s32[8,1,16]{2,1,0:T(1,128)S(1)} async-done(((s32[8,1,16]{2,1,0:T(1,128)}), s32[8,1,16]{2,1,0:T(1,128)S(1)}, u32[]{:S(2)}, u32[]{:S(2)}) %all-to-all-start.5) | async-done | bytes 544 | tf_op jit(solution)/shard_map/all_to_all | solution.py:199
  40.0 3.9 %all-to-all-start.2 = ((bf16[8,2,256]{2,1,0:T(2,128)(2,1)}), bf16[8,2,256]{2,1,0:T(2,128)(2,1)}, u32[]{:S(2)}, u32[]{:S(2)}) async-start(bf16[8,2,256]{2,1,0:T(2,128)(2,1)} %reshape.393), calls=%async_computation.2 | async-start | bytes 16384 | tf_op jit(solution)/shard_map/all_to_all | solution.py:70
  46.9 0.9 reshape.251
  49.1 2.8 copy.83
  51.9 2.8 reshape.395
  54.8 2.0 gather_fusion.2
  56.8 3.5 all-to-all-start.3
  62.5 12.2 %psum.7 = bf16[128,192]{0,1:T(8,128)(2,1)S(1)} all-reduce(bf16[128,192]{0,1:T(8,128)(2,1)S(1)} %pad_maximum_fusion), channel_id=1, replica_groups=mesh['blk'=8,'head'=4] {'head'}, use_global_device_ids=true, to_apply=%region_2.3 | all-reduce | flops 24576 | bytes 98304 | tf_op jit(solution)/shard_map/psum | solution.py:105
  75.4 1.2 fusion.10
  76.7 1.0 fusion.15
  79.9 5.9 %all-to-all-start.1 = ((bf16[8,16,2048]{2,1,0:T(8,128)(2,1)}), bf16[8,16,2048]{2,1,0:T(8,128)(2,1)}, u32[]{:S(2)}, u32[]{:S(2)}) async-start(bf16[8,16,2048]{2,1,0:T(8,128)(2,1)} %bitcast.11), calls=%async_computation.1 | async-start | bytes 1048576 | tf_op jit(solution)/shard_map/all_to_all | solution.py:61
  85.8 3.3 reshape.396
  89.1 2.2 convert_bitcast_fusion
  91.3 3.5 copy.85
  94.8 3.5 copy.84
  98.4 0.9 reshape.253
  100.4 0.9 reshape.237
  101.8 1.0 multiply_bitcast_fusion
  102.9 6.0 %all-to-all-start.6 = ((f32[8,1,512]{2,1,0:T(1,128)}), f32[8,1,512]{2,1,0:T(1,128)S(1)}, u32[]{:S(2)}, u32[]{:S(2)}) async-start(f32[8,1,512]{2,1,0:T(1,128)} %reshape.397), calls=%async_computation.6 | async-start | bytes 32768 | tf_op jit(solution)/shard_map/all_to_all | solution.py:198
  108.9 1.1 bitcast_convert_fusion
  110.0 2.0 gather_fusion.3
  112.0 2.0 reshape.226
  114.0 1.4 copy.112
  115.4 230.6 %while.14 = (s32[]{:T(128)}, f32[8,8,64,64]{3,2,1,0:T(8,128)S(1)}, f32[8,8,64,64]{3,2,1,0:T(8,128)}, f32[16,8,8,64]{3,2,1,0:T(8,128)}, f32[16,8,8,64]{3,2,1,0:T(...) while((s32[]{:T(128)}, f32[8,8,64,64]{3,2,1,0:T(8,128)S(1)}, ...), condition=%wide.region_7.8_spmd, body=%wide.region_4.7_spmd.sunk | while | flops 2363466 | bytes 15057189 | solution.py:150
  116.8 0.9 bitcast_multiply_fusion.2
  120.0 8.4 %multiply_reduce_fusion.5 = (f32[8,8,64]{2,1,0:T(8,128)S(1)}, f32[8,8,64,64]{3,2,1,0:T(8,128)S(1)}, f32[8,8,64,64]{3,2,1,0:T(8,128)S(1)}) fusion(f32[8,8,64]{2,1,0:T(8,128)S(1)} %get-tuple-element.208, f32[8,8,64,64]{3,2,1,0:T(8,128)S(1)} %copy-done.1, pred[8]{0:T(512)(128)(4,1)S(1)} %broadcast_compare_fusion.4, ...), kind=kOutput, calls=%fused_computation.15.clone.1 | output fusion | flops 2359359 | bytes 4309000 | tf_op jit(solution)/shard_map/while/body/eval_jaxpr/mul | solution.py:140
  134.4 8.4 %multiply_reduce_fusion.5 = (f32[8,8,64]{2,1,0:T(8,128)S(1)}, f32[8,8,64,64]{3,2,1,0:T(8,128)S(1)}, f32[8,8,64,64]{3,2,1,0:T(8,128)S(1)}) fusion(f32[8,8,64]{2,1,0:T(8,128)S(1)} %get-tuple-element.208, f32[8,8,64,64]{3,2,1,0:T(8,128)S(1)} %copy-done.1, pred[8]{0:T(512)(128)(4,1)S(1)} %broadcast_compare_fusion.4, ...), kind=kOutput, calls=%fused_computation.15.clone.1 | output fusion | flops 2359359 | bytes 4309000 | tf_op jit(solution)/shard_map/while/body/eval_jaxpr/mul | solution.py:140
  145.6 0.9 bitcast_multiply_fusion.2
  148.9 8.4 %multiply_reduce_fusion.5 = (f32[8,8,64]{2,1,0:T(8,128)S(1)}, f32[8,8,64,64]{3,2,1,0:T(8,128)S(1)}, f32[8,8,64,64]{3,2,1,0:T(8,128)S(1)}) fusion(f32[8,8,64]{2,1,0:T(8,128)S(1)} %get-tuple-element.208, f32[8,8,64,64]{3,2,1,0:T(8,128)S(1)} %copy-done.1, pred[8]{0:T(512)(128)(4,1)S(1)} %broadcast_compare_fusion.4, ...), kind=kOutput, calls=%fused_computation.15.clone.1 | output fusion | flops 2359359 | bytes 4309000 | tf_op jit(solution)/shard_map/while/body/eval_jaxpr/mul | solution.py:140
  163.3 8.4 %multiply_reduce_fusion.5 = (f32[8,8,64]{2,1,0:T(8,128)S(1)}, f32[8,8,64,64]{3,2,1,0:T(8,128)S(1)}, f32[8,8,64,64]{3,2,1,0:T(8,128)S(1)}) fusion(f32[8,8,64]{2,1,0:T(8,128)S(1)} %get-tuple-element.208, f32[8,8,64,64]{3,2,1,0:T(8,128)S(1)} %copy-done.1, pred[8]{0:T(512)(128)(4,1)S(1)} %broadcast_compare_fusion.4, ...), kind=kOutput, calls=%fused_computation.15.clone.1 | output fusion | flops 2359359 | bytes 4309000 | tf_op jit(solution)/shard_map/while/body/eval_jaxpr/mul | solution.py:140
  177.7 8.4 %multiply_reduce_fusion.5 = (f32[8,8,64]{2,1,0:T(8,128)S(1)}, f32[8,8,64,64]{3,2,1,0:T(8,128)S(1)}, f32[8,8,64,64]{3,2,1,0:T(8,128)S(1)}) fusion(f32[8,8,64]{2,1,0:T(8,128)S(1)} %get-tuple-element.208, f32[8,8,64,64]{3,2,1,0:T(8,128)S(1)} %copy-done.1, pred[8]{0:T(512)(128)(4,1)S(1)} %broadcast_compare_fusion.4, ...), kind=kOutput, calls=%fused_computation.15.clone.1 | output fusion | flops 2359359 | bytes 4309000 | tf_op jit(solution)/shard_map/while/body/eval_jaxpr/mul | solution.py:140
  188.9 0.9 bitcast_multiply_fusion.2
  192.1 8.4 %multiply_reduce_fusion.5 = (f32[8,8,64]{2,1,0:T(8,128)S(1)}, f32[8,8,64,64]{3,2,1,0:T(8,128)S(1)}, f32[8,8,64,64]{3,2,1,0:T(8,128)S(1)}) fusion(f32[8,8,64]{2,1,0:T(8,128)S(1)} %get-tuple-element.208, f32[8,8,64,64]{3,2,1,0:T(8,128)S(1)} %copy-done.1, pred[8]{0:T(512)(128)(4,1)S(1)} %broadcast_compare_fusion.4, ...), kind=kOutput, calls=%fused_computation.15.clone.1 | output fusion | flops 2359359 | bytes 4309000 | tf_op jit(solution)/shard_map/while/body/eval_jaxpr/mul | solution.py:140
  206.5 8.4 %multiply_reduce_fusion.5 = (f32[8,8,64]{2,1,0:T(8,128)S(1)}, f32[8,8,64,64]{3,2,1,0:T(8,128)S(1)}, f32[8,8,64,64]{3,2,1,0:T(8,128)S(1)}) fusion(f32[8,8,64]{2,1,0:T(8,128)S(1)} %get-tuple-element.208, f32[8,8,64,64]{3,2,1,0:T(8,128)S(1)} %copy-done.1, pred[8]{0:T(512)(128)(4,1)S(1)} %broadcast_compare_fusion.4, ...), kind=kOutput, calls=%fused_computation.15.clone.1 | output fusion | flops 2359359 | bytes 4309000 | tf_op jit(solution)/shard_map/while/body/eval_jaxpr/mul | solution.py:140
  217.7 0.9 bitcast_multiply_fusion.2
  220.9 8.4 %multiply_reduce_fusion.5 = (f32[8,8,64]{2,1,0:T(8,128)S(1)}, f32[8,8,64,64]{3,2,1,0:T(8,128)S(1)}, f32[8,8,64,64]{3,2,1,0:T(8,128)S(1)}) fusion(f32[8,8,64]{2,1,0:T(8,128)S(1)} %get-tuple-element.208, f32[8,8,64,64]{3,2,1,0:T(8,128)S(1)} %copy-done.1, pred[8]{0:T(512)(128)(4,1)S(1)} %broadcast_compare_fusion.4, ...), kind=kOutput, calls=%fused_computation.15.clone.1 | output fusion | flops 2359359 | bytes 4309000 | tf_op jit(solution)/shard_map/while/body/eval_jaxpr/mul | solution.py:140
  232.1 0.9 bitcast_multiply_fusion.2
  235.3 8.4 %multiply_reduce_fusion.5 = (f32[8,8,64]{2,1,0:T(8,128)S(1)}, f32[8,8,64,64]{3,2,1,0:T(8,128)S(1)}, f32[8,8,64,64]{3,2,1,0:T(8,128)S(1)}) fusion(f32[8,8,64]{2,1,0:T(8,128)S(1)} %get-tuple-element.208, f32[8,8,64,64]{3,2,1,0:T(8,128)S(1)} %copy-done.1, pred[8]{0:T(512)(128)(4,1)S(1)} %broadcast_compare_fusion.4, ...), kind=kOutput, calls=%fused_computation.15.clone.1 | output fusion | flops 2359359 | bytes 4309000 | tf_op jit(solution)/shard_map/while/body/eval_jaxpr/mul | solution.py:140
  249.7 8.4 %multiply_reduce_fusion.5 = (f32[8,8,64]{2,1,0:T(8,128)S(1)}, f32[8,8,64,64]{3,2,1,0:T(8,128)S(1)}, f32[8,8,64,64]{3,2,1,0:T(8,128)S(1)}) fusion(f32[8,8,64]{2,1,0:T(8,128)S(1)} %get-tuple-element.208, f32[8,8,64,64]{3,2,1,0:T(8,128)S(1)} %copy-done.1, pred[8]{0:T(512)(128)(4,1)S(1)} %broadcast_compare_fusion.4, ...), kind=kOutput, calls=%fused_computation.15.clone.1 | output fusion | flops 2359359 | bytes 4309000 | tf_op jit(solution)/shard_map/while/body/eval_jaxpr/mul | solution.py:140
  260.9 0.9 bitcast_multiply_fusion.2
  264.1 8.4 %multiply_reduce_fusion.5 = (f32[8,8,64]{2,1,0:T(8,128)S(1)}, f32[8,8,64,64]{3,2,1,0:T(8,128)S(1)}, f32[8,8,64,64]{3,2,1,0:T(8,128)S(1)}) fusion(f32[8,8,64]{2,1,0:T(8,128)S(1)} %get-tuple-element.208, f32[8,8,64,64]{3,2,1,0:T(8,128)S(1)} %copy-done.1, pred[8]{0:T(512)(128)(4,1)S(1)} %broadcast_compare_fusion.4, ...), kind=kOutput, calls=%fused_computation.15.clone.1 | output fusion | flops 2359359 | bytes 4309000 | tf_op jit(solution)/shard_map/while/body/eval_jaxpr/mul | solution.py:140
  278.6 8.4 %multiply_reduce_fusion.5 = (f32[8,8,64]{2,1,0:T(8,128)S(1)}, f32[8,8,64,64]{3,2,1,0:T(8,128)S(1)}, f32[8,8,64,64]{3,2,1,0:T(8,128)S(1)}) fusion(f32[8,8,64]{2,1,0:T(8,128)S(1)} %get-tuple-element.208, f32[8,8,64,64]{3,2,1,0:T(8,128)S(1)} %copy-done.1, pred[8]{0:T(512)(128)(4,1)S(1)} %broadcast_compare_fusion.4, ...), kind=kOutput, calls=%fused_computation.15.clone.1 | output fusion | flops 2359359 | bytes 4309000 | tf_op jit(solution)/shard_map/while/body/eval_jaxpr/mul | solution.py:140
  293.0 8.4 %multiply_reduce_fusion.5 = (f32[8,8,64]{2,1,0:T(8,128)S(1)}, f32[8,8,64,64]{3,2,1,0:T(8,128)S(1)}, f32[8,8,64,64]{3,2,1,0:T(8,128)S(1)}) fusion(f32[8,8,64]{2,1,0:T(8,128)S(1)} %get-tuple-element.208, f32[8,8,64,64]{3,2,1,0:T(8,128)S(1)} %copy-done.1, pred[8]{0:T(512)(128)(4,1)S(1)} %broadcast_compare_fusion.4, ...), kind=kOutput, calls=%fused_computation.15.clone.1 | output fusion | flops 2359359 | bytes 4309000 | tf_op jit(solution)/shard_map/while/body/eval_jaxpr/mul | solution.py:140
  304.1 0.9 bitcast_multiply_fusion.2
  307.4 8.4 %multiply_reduce_fusion.5 = (f32[8,8,64]{2,1,0:T(8,128)S(1)}, f32[8,8,64,64]{3,2,1,0:T(8,128)S(1)}, f32[8,8,64,64]{3,2,1,0:T(8,128)S(1)}) fusion(f32[8,8,64]{2,1,0:T(8,128)S(1)} %get-tuple-element.208, f32[8,8,64,64]{3,2,1,0:T(8,128)S(1)} %copy-done.1, pred[8]{0:T(512)(128)(4,1)S(1)} %broadcast_compare_fusion.4, ...), kind=kOutput, calls=%fused_computation.15.clone.1 | output fusion | flops 2359359 | bytes 4309000 | tf_op jit(solution)/shard_map/while/body/eval_jaxpr/mul | solution.py:140
  321.8 8.4 %multiply_reduce_fusion.5 = (f32[8,8,64]{2,1,0:T(8,128)S(1)}, f32[8,8,64,64]{3,2,1,0:T(8,128)S(1)}, f32[8,8,64,64]{3,2,1,0:T(8,128)S(1)}) fusion(f32[8,8,64]{2,1,0:T(8,128)S(1)} %get-tuple-element.208, f32[8,8,64,64]{3,2,1,0:T(8,128)S(1)} %copy-done.1, pred[8]{0:T(512)(128)(4,1)S(1)} %broadcast_compare_fusion.4, ...), kind=kOutput, calls=%fused_computation.15.clone.1 | output fusion | flops 2359359 | bytes 4309000 | tf_op jit(solution)/shard_map/while/body/eval_jaxpr/mul | solution.py:140
  333.0 0.9 bitcast_multiply_fusion.2
  336.2 8.4 %multiply_reduce_fusion.5 = (f32[8,8,64]{2,1,0:T(8,128)S(1)}, f32[8,8,64,64]{3,2,1,0:T(8,128)S(1)}, f32[8,8,64,64]{3,2,1,0:T(8,128)S(1)}) fusion(f32[8,8,64]{2,1,0:T(8,128)S(1)} %get-tuple-element.208, f32[8,8,64,64]{3,2,1,0:T(8,128)S(1)} %copy-done.1, pred[8]{0:T(512)(128)(4,1)S(1)} %broadcast_compare_fusion.4, ...), kind=kOutput, calls=%fused_computation.15.clone.1 | output fusion | flops 2359359 | bytes 4309000 | tf_op jit(solution)/shard_map/while/body/eval_jaxpr/mul | solution.py:140
  346.0 2.1 reshape.240
  348.1 2.0 gather_fusion.8
  350.1 6.1 %all-to-all-start.4 = ((f32[8,16,2048]{2,1,0:T(8,128)}), f32[8,16,2048]{2,1,0:T(8,128)S(1)}, u32[]{:S(2)}, u32[]{:S(2)}) async-start(f32[8,16,2048]{2,1,0:T(8,128)} %bitcast.113), calls=%async_computation.4 | async-start | bytes 2097152 | tf_op jit(solution)/shard_map/all_to_all | solution.py:197
  356.5 2.5 sort.62
  361.7 1.0 reshape.238
  362.7 1.2 reduce_sum.57
  366.0 14.0 %all-to-all-done.4 = f32[8,16,2048]{2,1,0:T(8,128)S(1)} async-done(((f32[8,16,2048]{2,1,0:T(8,128)}), f32[8,16,2048]{2,1,0:T(8,128)S(1)}, u32[]{:S(2)}, u32[]{:S(2)}) %all-to-all-start.4) | async-done | bytes 1048608 | tf_op jit(solution)/shard_map/all_to_all | solution.py:197
  380.0 1.9 gather_fusion.10
  (342 shorter events, 101.8 us)
Async XLA Ops:
  0.6 54.1 %copy-start = (f32[1,128,2048]{2,1,0:T(8,128)S(1)}, f32[1,128,2048]{2,1,0:T(8,128)}, u32[]{:S(2)}) copy-start(f32[1,128,2048]{2,1,0:T(8,128)} %param.29) | copy-start | bytes 3145732
  0.6 30.8 %copy-start.17 = (f32[1,128,32]{1,2,0:T(8,128)S(1)}, f32[1,128,32]{1,2,0:T(8,128)}, u32[]{:S(2)}) copy-start(f32[1,128,32]{1,2,0:T(8,128)} %param.30) | copy-start | bytes 49156
  0.7 43.9 %copy-start.5 = (bf16[8,16,512]{2,1,0:T(8,128)(2,1)S(1)}, bf16[8,16,512]{2,1,0:T(8,128)(2,1)}, u32[]{:S(2)}) copy-start(bf16[8,16,512]{2,1,0:T(8,128)(2,1)} %param.25) | copy-start | bytes 393220
  0.7 44.6 %copy-start.28 = (f32[512]{0:T(512)S(1)}, f32[512]{0:T(512)}, u32[]{:S(2)}) copy-start(f32[512]{0:T(512)} %param.35) | copy-start | bytes 6148
  0.7 45.3 %copy-start.19 = (f32[512]{0:T(512)S(1)}, f32[512]{0:T(512)}, u32[]{:S(2)}) copy-start(f32[512]{0:T(512)} %param.38) | copy-start | bytes 6148
  0.7 46.1 %copy-start.9 = (bf16[8,16,512]{2,1,0:T(8,128)(2,1)S(1)}, bf16[8,16,512]{2,1,0:T(8,128)(2,1)}, u32[]{:S(2)}) copy-start(bf16[8,16,512]{2,1,0:T(8,128)(2,1)} %param.27) | copy-start | bytes 393220
  7.7 17.8 %all-to-all-start = ((s32[8,1,16]{2,1,0:T(1,128)}), s32[8,1,16]{2,1,0:T(1,128)S(1)}, u32[]{:S(2)}, u32[]{:S(2)}) async-start(s32[8,1,16]{2,1,0:T(1,128)} %bitcast.9), calls=%async_computation | async-start | bytes 8192 | tf_op jit(solution)/shard_map/all_to_all | solution.py:56
  21.0 10.5 %copy-start.21 = (s32[1024]{0:T(1024)}, s32[1024]{0:T(1024)S(1)}, u32[]{:S(2)}) copy-start(s32[1024]{0:T(1024)S(1)} %pad_clamp_fusion.1) | copy-start | bytes 12292
  25.5 12.4 %all-to-all-start.5 = ((s32[8,1,16]{2,1,0:T(1,128)}), s32[8,1,16]{2,1,0:T(1,128)S(1)}, u32[]{:S(2)}, u32[]{:S(2)}) async-start(s32[8,1,16]{2,1,0:T(1,128)} %bitcast.31), calls=%async_computation.5 | async-start | bytes 8192 | tf_op jit(solution)/shard_map/all_to_all | solution.py:199
  38.6 8.1 %copy-start.22 = (s32[1024]{0:T(1024)}, s32[1024]{0:T(1024)S(1)}, u32[]{:S(2)}) copy-start(s32[1024]{0:T(1024)S(1)} %pad_clamp_fusion.3) | copy-start | bytes 12292
  40.0 16.8 %all-to-all-start.2 = ((bf16[8,2,256]{2,1,0:T(2,128)(2,1)}), bf16[8,2,256]{2,1,0:T(2,128)(2,1)}, u32[]{:S(2)}, u32[]{:S(2)}) async-start(bf16[8,2,256]{2,1,0:T(2,128)(2,1)} %reshape.393), calls=%async_computation.2 | async-start | bytes 16384 | tf_op jit(solution)/shard_map/all_to_all | solution.py:70
  54.8 7.2 %copy-start.23 = (f32[512]{0:T(512)S(1)}, f32[512]{0:T(512)}, u32[]{:S(2)}) copy-start(f32[512]{0:T(512)} %param.31) | copy-start | bytes 6148
  54.8 7.2 %copy-start.24 = (f32[512]{0:T(512)S(1)}, f32[512]{0:T(512)}, u32[]{:S(2)}) copy-start(f32[512]{0:T(512)} %param.32) | copy-start | bytes 6148
  54.8 7.3 %copy-start.11 = (bf16[512,96]{0,1:T(8,128)(2,1)S(1)}, bf16[512,96]{0,1:T(8,128)(2,1)}, u32[]{:S(2)}) copy-start(bf16[512,96]{0,1:T(8,128)(2,1)} %param.33) | copy-start | bytes 294916
  54.8 7.5 %copy-start.12 = (bf16[512,96]{0,1:T(8,128)(2,1)S(1)}, bf16[512,96]{0,1:T(8,128)(2,1)}, u32[]{:S(2)}) copy-start(bf16[512,96]{0,1:T(8,128)(2,1)} %param.36) | copy-start | bytes 294916
  56.8 17.9 %copy-start.13 = (bf16[96,512]{1,0:T(8,128)(2,1)S(1)}, bf16[96,512]{1,0:T(8,128)(2,1)}, u32[]{:S(2)}) copy-start(bf16[96,512]{1,0:T(8,128)(2,1)} %param.37) | copy-start | bytes 294916
  56.8 18.1 %copy-start.14 = (bf16[96,512]{1,0:T(8,128)(2,1)S(1)}, bf16[96,512]{1,0:T(8,128)(2,1)}, u32[]{:S(2)}) copy-start(bf16[96,512]{1,0:T(8,128)(2,1)} %param.34) | copy-start | bytes 294916
  56.8 22.4 %all-to-all-start.3 = ((bf16[4,2,8192]{2,1,0:T(2,128)(2,1)}), bf16[4,2,8192]{2,1,0:T(2,128)(2,1)S(1)}, u32[]{:S(2)}, u32[]{:S(2)}) async-start(bf16[4,2,8192]{2,1,0:T(2,128)(2,1)} %reshape.395), calls=%async_computation.3 | async-start | bytes 262144 | tf_op jit(solution)/shard_map/all_to_all | solution.py:80
  61.1 14.3 %copy-start.16 = (f32[8,64]{1,0:T(8,128)S(1)}, f32[8,64]{1,0:T(8,128)}, u32[]{:S(2)}) copy-start(f32[8,64]{1,0:T(8,128)} %add.166) | copy-start | bytes 6148
  62.1 14.6 %copy-start.15 = (f32[8,64]{1,0:T(8,128)S(1)}, f32[8,64]{1,0:T(8,128)}, u32[]{:S(2)}) copy-start(f32[8,64]{1,0:T(8,128)} %add.174) | copy-start | bytes 6148
  74.9 2.7 copy-start.8
  74.9 2.7 copy-start.31
  79.9 23.0 %all-to-all-start.1 = ((bf16[8,16,2048]{2,1,0:T(8,128)(2,1)}), bf16[8,16,2048]{2,1,0:T(8,128)(2,1)}, u32[]{:S(2)}, u32[]{:S(2)}) async-start(bf16[8,16,2048]{2,1,0:T(8,128)(2,1)} %bitcast.11), calls=%async_computation.1 | async-start | bytes 1048576 | tf_op jit(solution)/shard_map/all_to_all | solution.py:61
  94.7 4.6 %copy-start.10 = (bf16[8,16,512]{2,1,0:T(8,128)(2,1)S(1)}, bf16[8,16,512]{2,1,0:T(8,128)(2,1)}, u32[]{:S(2)}) copy-start(bf16[8,16,512]{2,1,0:T(8,128)(2,1)} %param.26) | copy-start | bytes 393220
  94.7 4.6 %copy-start.20 = (f32[512]{0:T(512)S(1)}, f32[512]{0:T(512)}, u32[]{:S(2)}) copy-start(f32[512]{0:T(512)} %param.38) | copy-start | bytes 6148
  94.8 4.6 %copy-start.25 = (f32[512]{0:T(512)S(1)}, f32[512]{0:T(512)}, u32[]{:S(2)}) copy-start(f32[512]{0:T(512)} %param.41) | copy-start | bytes 6148
  94.8 4.6 %copy-start.26 = (f32[512]{0:T(512)S(1)}, f32[512]{0:T(512)}, u32[]{:S(2)}) copy-start(f32[512]{0:T(512)} %param.40) | copy-start | bytes 6148
  94.8 4.6 %copy-start.27 = (f32[512]{0:T(512)S(1)}, f32[512]{0:T(512)}, u32[]{:S(2)}) copy-start(f32[512]{0:T(512)} %param.39) | copy-start | bytes 6148
  102.9 247.3 %all-to-all-start.6 = ((f32[8,1,512]{2,1,0:T(1,128)}), f32[8,1,512]{2,1,0:T(1,128)S(1)}, u32[]{:S(2)}, u32[]{:S(2)}) async-start(f32[8,1,512]{2,1,0:T(1,128)} %reshape.397), calls=%async_computation.6 | async-start | bytes 32768 | tf_op jit(solution)/shard_map/all_to_all | solution.py:198
  114.0 1.4 copy-start.33
  116.6 3.4 copy-start.1
  128.4 1.4 copy-start.2
  131.1 3.4 copy-start.1
  142.9 1.4 copy-start.2
  145.5 3.4 copy-start.1
  157.3 1.4 copy-start.2
  159.9 3.4 copy-start.1
  171.7 1.4 copy-start.2
  174.3 3.4 copy-start.1
  186.1 1.4 copy-start.2
  188.7 3.4 copy-start.1
  200.5 1.4 copy-start.2
  203.1 3.4 copy-start.1
  214.9 1.4 copy-start.2
  217.5 3.4 copy-start.1
  229.3 1.4 copy-start.2
  231.9 3.4 copy-start.1
  243.7 1.4 copy-start.2
  246.3 3.4 copy-start.1
  260.8 3.4 copy-start.1
  275.2 3.4 copy-start.1
  287.0 1.4 copy-start.2
  289.6 3.4 copy-start.1
  304.0 3.4 copy-start.1
  318.4 3.4 copy-start.1
  330.2 1.4 copy-start.2
  332.8 3.4 copy-start.1
  350.1 6.2 %copy-start.29 = (f32[512]{0:T(512)S(1)}, f32[512]{0:T(512)}, u32[]{:S(2)}) copy-start(f32[512]{0:T(512)} %param.42) | copy-start | bytes 6148
  350.1 6.3 %copy-start.30 = (f32[512]{0:T(512)S(1)}, f32[512]{0:T(512)}, u32[]{:S(2)}) copy-start(f32[512]{0:T(512)} %param.43) | copy-start | bytes 6148
  350.1 6.3 %copy-start.18 = (s32[8,16]{1,0:T(8,128)S(1)}, s32[8,16]{1,0:T(8,128)}, u32[]{:S(2)}) copy-start(s32[8,16]{1,0:T(8,128)} %get-tuple-element.126) | copy-start | bytes 1540
  350.1 11.6 %copy-start.6 = (f32[8,16,512]{2,1,0:T(8,128)S(1)}, f32[8,16,512]{2,1,0:T(8,128)}, u32[]{:S(2)}) copy-start(f32[8,16,512]{2,1,0:T(8,128)} %get-tuple-element.112) | copy-start | bytes 786436
  350.1 13.8 %copy-start.3 = (f32[16,8,8,64]{3,2,1,0:T(8,128)S(1)}, f32[16,8,8,64]{3,2,1,0:T(8,128)}, u32[]{:S(2)}) copy-start(f32[16,8,8,64]{3,2,1,0:T(8,128)} %get-tuple-element.72) | copy-start | bytes 786436
  350.1 29.9 %all-to-all-start.4 = ((f32[8,16,2048]{2,1,0:T(8,128)}), f32[8,16,2048]{2,1,0:T(8,128)S(1)}, u32[]{:S(2)}, u32[]{:S(2)}) async-start(f32[8,16,2048]{2,1,0:T(8,128)} %bitcast.113), calls=%async_computation.4 | async-start | bytes 2097152 | tf_op jit(solution)/shard_map/all_to_all | solution.py:197
  356.3 8.3 %copy-start.4 = (f32[16,8,8,64]{3,2,1,0:T(8,128)S(1)}, f32[16,8,8,64]{3,2,1,0:T(8,128)}, u32[]{:S(2)}) copy-start(f32[16,8,8,64]{3,2,1,0:T(8,128)} %get-tuple-element.260) | copy-start | bytes 786436
  (7 other events, 8.0 us)
where the time goes:
time: 386 us; the launch traced here: 382 us
  other arithmetic  172 us (45%)
  local copies, waits for them, and re-layouts  125 us (32%)
  starting transfers between devices  38.7 us (10%)
  waiting for transfers between devices  20.3 us (5%)
  blocking collectives  12.2 us (3%)
  loops' own time  11.1 us (3%)
    mul x16, other arithmetic, advance(): projected[..., None] * (rate_t * unit_t)[:, :, None, :]  135 us
    unnamed x77, local copies, waits for them, and re-layouts  16.2 us
    mul x16, other arithmetic, advance(): rate_t * unit_t  14.5 us
    all_to_all x1, waiting for transfers between devices, local(): lax.all_to_all(send_states, 'blk', split_axis=0, concat_axis=0, tiled=True)  14 us
    while x80, local copies, waits for them, and re-layouts  13.4 us
    mul x16, local copies, waits for them, and re-layouts, advance(): output = jnp.sum(carry_state * recept_t[:, :, None, :], axis=-1)  12.5 us
    mul x16, local copies, waits for them, and re-layouts, advance(): value_t[..., None] * key_t[:, :, None, :]  12.5 us
    psum x1, blocking collectives, local(): lax.psum(partial_terms.astype(jnp.bfloat16), 'head').astype(jnp.float32)  12.2 us
  transfers between devices with their start and end apart: 7, of which 2 were waited for; matrix products, arithmetic and copies ran while one was open for 72% of the time, Pallas kernels for 0%

commit v1 on v0

v1 whole, which is shorter than its diff:
```python
import functools

import jax
import jax.numpy as jnp
from jax import lax
from jax.experimental import pallas as pl
from jax.experimental.pallas import tpu as pltpu
from jax.sharding import PartitionSpec as P

EPSILON = 1e-05
NORM_EPSILON = 0.00064
DECAY_SCALE = 0.6065306597126334
F32 = jnp.float32
BF16 = jnp.bfloat16
I32 = jnp.int32
NT = (((1,), (1,)), ((), ()))
NN = (((1,), (0,)), ((), ()))

SMEM = functools.partial(pl.BlockSpec, memory_space=pltpu.SMEM)
VMEM = functools.partial(pl.BlockSpec, memory_space=pltpu.VMEM)


def call(kernel, out_shape, in_specs, scratch=(), flops=1 << 20, moved=1 << 20):
    return pl.pallas_call(
        kernel,
        out_shape=out_shape,
        in_specs=in_specs,
        out_specs=jax.tree.map(lambda _: VMEM(), out_shape),
        scratch_shapes=list(scratch),
        compiler_params=pltpu.CompilerParams(vmem_limit_bytes=48 * 1024 * 1024),
        cost_estimate=pl.CostEstimate(flops=flops, bytes_accessed=moved, transcendentals=0),
    )


def dot(a, b, dims=NN):
    return lax.dot_general(a, b, dims, preferred_element_type=F32)


def split(x):
    high = x.astype(BF16)
    return high, (x - high.astype(F32)).astype(BF16)


def group_sum(x, width):
    rows, lanes = x.shape
    block = max(width, 128)
    ones = (
        lax.broadcasted_iota(I32, (block, block), 0) // width
        == lax.broadcasted_iota(I32, (block, block), 1) // width
    ).astype(BF16)
    high, low = split(x)
    parts = []
    for start in range(0, lanes, block):
        cut = slice(start, start + block)
        parts.append(dot(high[:, cut], ones) + dot(low[:, cut], ones))
    return jnp.concatenate(parts, axis=1)


def positions(seq_ref, count):
    lane = lax.broadcasted_iota(I32, (1, count), 1)

    def block(b, acc):
        for k in range(8):
            acc = jnp.where(lane == seq_ref[b * 8 + k], b * 8 + k, acc)
        return acc

    return lax.fori_loop(0, count // 8, block, jnp.zeros((1, count), I32))


def place_of_slot(table_ref, position, base, blocks, per_peer, requests, slot_dev):
    heads, halves, count = table_ref.shape
    slot = lax.broadcasted_iota(I32, (slot_dev, count), 0) + base
    named = jnp.zeros((slot_dev, count), F32)
    for h in range(heads):
        for c in range(halves):
            named = jnp.where(table_ref[h, c : c + 1, :] == slot, 1.0, named)
    other_of = jnp.broadcast_to(position // requests, (16, count)).astype(F32).astype(BF16)
    other = dot(other_of, named.astype(BF16), NT)[0:1, :].astype(I32)
    rows = max(16, blocks)
    mask = other == lax.broadcasted_iota(I32, (rows, slot_dev), 0)
    before = (
        lax.broadcasted_iota(I32, (slot_dev, slot_dev), 0)
        < lax.broadcasted_iota(I32, (slot_dev, slot_dev), 1)
    ).astype(F32).astype(BF16)
    ahead = dot(mask.astype(F32).astype(BF16), before)
    rank = jnp.sum(jnp.where(mask, ahead, 0.0), axis=0, keepdims=True).astype(I32)
    return other * per_peer + rank


def place_of_item(table_ref, position, first, requests):
    heads, halves, count = table_ref.shape
    per_item = heads * halves
    items = requests * per_item
    mine = (
        jnp.broadcast_to(position, (16, count)) - first == lax.broadcasted_iota(I32, (16, count), 0)
    ).astype(F32).astype(BF16)
    lane = lax.broadcasted_iota(I32, (16, items), 1)
    owner = lax.broadcasted_iota(I32, (16, items), 0) == lane // per_item
    slots = jnp.zeros((16, items), F32)
    for h in range(heads):
        for c in range(halves):
            line = jnp.broadcast_to(table_ref[h, c : c + 1, :], (items, count))
            high = dot(mine, (line // 128).astype(F32).astype(BF16), NT)
            low = dot(mine, (line % 128).astype(F32).astype(BF16), NT)
            slots = jnp.where(lane % per_item == h * halves + c, high * 128.0 + low, slots)
    row = jnp.sum(jnp.where(owner, slots, 0.0), axis=0, keepdims=True)
    diagonal = lax.broadcasted_iota(I32, (items, items), 0) == lax.broadcasted_iota(I32, (items, items), 1)
    column = jnp.sum(jnp.where(diagonal, row, 0.0), axis=1, keepdims=True)
    return row.astype(I32), jnp.sum((column < row).astype(F32), axis=0, keepdims=True).astype(I32)


def send_kernel(
    blocks, requests, per_peer,
    seq_ref, read_ref, write_ref, state_ref,
    out_ref, index_ref, scratch,
):
    slot_dev = state_ref.shape[0]
    lanes = state_ref.shape[1] // 128
    me = lax.axis_index("blk")
    position = positions(seq_ref, read_ref.shape[2])
    place = place_of_slot(read_ref, position, me * slot_dev, blocks, per_peer, requests, slot_dev)
    pick = (place == lax.broadcasted_iota(I32, (slot_dev, slot_dev), 0)).astype(F32).astype(BF16)
    left = lax.broadcasted_iota(I32, (slot_dev, 128), 1) < 64
    half = lanes // 2
    for b in range(half):
        x = dot(pick, state_ref[:, b * 128 : (b + 1) * 128].astype(BF16))
        y = dot(pick, state_ref[:, (half + b) * 128 : (half + b + 1) * 128].astype(BF16))
        scratch[:, 2 * b, :] = jnp.where(left, x, pltpu.roll(y, 64, 1))
        scratch[:, 2 * b + 1, :] = jnp.where(left, pltpu.roll(x, 64, 1), y)
    out_ref[...] = scratch[...].astype(BF16)
    first = me * requests
    wanted, place = place_of_item(read_ref, position, first, requests)
    index_ref[0:1, :] = place
    index_ref[2:3, :] = wanted
    index_ref[1:2, :] = place_of_item(write_ref, position, first, requests)[1]
    index_ref[3:8, :] = jnp.zeros((5, slot_dev), I32)


def target_kernel(blocks, requests, per_peer, slot_dev, seq_ref, write_ref, out_ref):
    position = positions(seq_ref, write_ref.shape[2])
    base = lax.axis_index("blk") * slot_dev
    place = place_of_slot(write_ref, position, base, blocks, per_peer, requests, slot_dev)
    out_ref[...] = jnp.broadcast_to(place, out_ref.shape)


def shift_kernel(
    requests, heads, halves,
    index_ref, seq_ref, count_ref, edges_ref, layer_ref, mix_decay_ref, mix_rate_ref, left_decay_ref, left_rate_ref,
    out_ref, new_edge_ref, pool_scratch, edge_scratch, line_scratch,
):
    width = layer_ref.shape[1]
    steps = layer_ref.shape[0] // requests
    blocks, rows, slot_dev = edges_ref.shape
    first = lax.axis_index("blk") * requests

    @pl.loop(0, blocks)
    def _(b):
        pool = jnp.concatenate([edges_ref[b], jnp.zeros((slot_dev - rows, slot_dev), F32)], axis=0)
        pool_scratch[pl.ds(pl.multiple_of(b * slot_dev, slot_dev), slot_dev), :] = jnp.transpose(pool)

    for p in range(requests):
        for k in range(heads * halves):
            slot = index_ref[2, p * heads * halves + k]
            edge_scratch[p : p + 1, k * rows : (k + 1) * rows] = pool_scratch[pl.ds(slot, 1), :rows]
    edge = edge_scratch[...]
    line = layer_ref[...].astype(F32)
    line_scratch[...] = line
    step = lax.broadcasted_iota(I32, line.shape, 0) % steps
    edge_lines = jnp.broadcast_to(edge[:, None, :], (requests, steps, width)).reshape(line.shape)
    delta = jnp.where(step == 0, edge_lines, pltpu.roll(line, 1, 0)) - line
    rank = left_decay_ref.shape[0]
    mixed_decay = (line + delta * mix_decay_ref[...]).astype(BF16)
    mixed_rate = (line + delta * mix_rate_ref[...]).astype(BF16)
    partial_decay = dot(mixed_decay, left_decay_ref[...], NT).astype(BF16)
    partial_rate = dot(mixed_rate, left_rate_ref[...], NT).astype(BF16)
    out_ref[:, :rank] = partial_decay
    out_ref[:, rank:] = partial_rate
    for p in range(requests):
        n = count_ref[seq_ref[first + p]]
        picked = line_scratch[pl.ds(p * steps + jnp.maximum(n - 1, 0), 1), :]
        new_edge_ref[p : p + 1, :] = jnp.where(n > 0, picked, edge[p : p + 1, :])


def expand(x, head_width):
    steps, lanes = x.shape
    heads = lanes // head_width
    per_block = 128 // head_width
    lane = lax.broadcasted_iota(I32, (steps, 128), 1) // head_width
    zero = jnp.zeros((steps, 128), x.dtype)
    lines = []
    for h in range(heads):
        own = h // per_block
        block = jnp.where(lane == h % per_block, x[:, own * 128 : (own + 1) * 128], zero)
        lines.append(jnp.concatenate([block if b == own else zero for b in range(lanes // 128)], axis=1))
    return jnp.concatenate(lines, axis=0)


def prepare_kernel(
    requests, heads,
    seq_ref, count_ref, parts_ref, right_decay_ref, right_rate_ref, offset_decay_ref, offset_rate_ref,
    key_ref, value_ref, erase_ref, written_ref,
    a_ref, k_ref, b_ref, cum_ref, key_mod_ref, last_ref, value_t_ref, small_ref, solve_ref,
    cross, compact,
):
    rows, width = key_ref.shape
    steps = rows // requests
    head_width = width // heads
    rank = right_decay_ref.shape[0]
    first = lax.axis_index("blk") * requests
    total = parts_ref[0].astype(F32)
    for g in range(1, parts_ref.shape[0]):
        total = total + parts_ref[g].astype(F32)
    hidden = jnp.tanh(total[:, :rank]).astype(BF16)
    rate_hidden = total[:, rank:].astype(BF16)
    decay = offset_decay_ref[...] + dot(hidden, right_decay_ref[...])
    log_forget = -DECAY_SCALE * jax.nn.sigmoid(decay)
    rate = jax.nn.sigmoid(offset_rate_ref[...] + dot(rate_hidden, right_rate_ref[...]))
    key = key_ref[...].astype(F32)
    u = key * erase_ref[...]
    unit = u * lax.rsqrt(group_sum(u * u, head_width) + EPSILON)
    key_mod = key * (1.0 + (rate - 1.0) * written_ref[...])
    key_mod_ref[...] = key_mod
    step = lax.broadcasted_iota(I32, (rows, width), 0) % steps
    cum = log_forget
    shift = 1
    while shift < steps:
        cum = cum + jnp.where(step >= shift, pltpu.roll(cum, shift, 0), 0.0)
        shift *= 2
    grow = jnp.exp(-cum)
    cum_ref[...] = cum
    a_ref[...] = (unit * jnp.exp(cum - log_forget)).astype(BF16)
    k_ref[...] = (key_mod * grow).astype(BF16)
    b_ref[...] = (rate * unit * grow).astype(BF16)
    ident = (
        lax.broadcasted_iota(I32, (head_width, width), 0)
        == lax.broadcasted_iota(I32, (head_width, width), 1) % head_width
    ).astype(F32).astype(BF16)
    for p in range(requests):
        cut = slice(p * steps, (p + 1) * steps)
        n = count_ref[seq_ref[first + p]]
        at_n = cum_ref[pl.ds(p * steps + jnp.maximum(n - 1, 0), 1), :]
        last_ref[p : p + 1, :] = jnp.where(n > 0, jnp.exp(at_n), 1.0)
        right = jnp.concatenate([expand(k_ref[cut, :], head_width), expand(b_ref[cut, :], head_width)], axis=0)
        cross[p] = dot(a_ref[cut, :], right, NT)
        value_t_ref[p] = dot(ident, expand(value_ref[cut, :], head_width), NT).astype(BF16)
    lanes = heads * steps
    lane = lax.broadcasted_iota(I32, (requests, lanes), 1)
    source = lane % steps
    group = lane - source
    solve, carry = [], []
    for t in range(steps):
        weights = jnp.where(source < t, cross[:, t, lanes:], 0.0)
        solve_t = jnp.where(source == t, 1.0, 0.0)
        carry_t = jnp.where(source < t, cross[:, t, :lanes], 0.0)
        for s in range(t):
            weight = jnp.take_along_axis(weights, group + s, axis=1)
            solve_t = solve_t - weight * solve[s]
            carry_t = carry_t - weight * carry[s]
        solve.append(solve_t)
        carry.append(carry_t)
        compact[0, :, t, :] = solve_t
        compact[1, :, t, :] = carry_t
        solve_ref[0, t] = solve_t
        solve_ref[1, t] = carry_t
    small_ref[...] = compact[...].astype(BF16)


def spread(x, steps):
    lanes = x.shape[1]
    group = lax.broadcasted_iota(I32, x.shape, 1) // steps
    zero = jnp.zeros_like(x)
    return jnp.concatenate([jnp.where(group == h, x, zero) for h in range(lanes // steps)], axis=0)


def state_kernel(
    requests, heads, halves, per_peer,
    index_ref, seq_ref, count_ref, got_ref, a_ref, k_ref, b_ref, last_ref, value_t_ref, small_ref, new_edge_ref,
    send_ref, state_ref, both_ref, edge_scratch,
):
    rows, width = a_ref.shape
    steps = rows // requests
    head_width = width // heads
    pack = got_ref.shape[1]
    first = lax.axis_index("blk") * requests
    edge_rows = head_width // halves
    low = lax.broadcasted_iota(I32, (pack, 128), 1) < head_width

    def sent_at(item):
        place = index_ref[1, item]
        return place + place // per_peer

    for p in range(requests):
        cut = slice(p * steps, (p + 1) * steps)
        n = count_ref[seq_ref[first + p]]
        lines = []
        for c in range(halves):
            tops, bottoms = [], []
            for pair in range(heads // 2):
                at = (p * heads + 2 * pair) * halves + c
                even = got_ref[index_ref[0, at]].astype(F32)
                odd = got_ref[index_ref[0, at + halves]].astype(F32)
                tops.append(jnp.where(low, even, pltpu.roll(odd, head_width, 1)))
                bottoms.append(jnp.where(low, pltpu.roll(even, head_width, 1), odd))
            lines.append(jnp.concatenate(tops, axis=1))
            lines.append(jnp.concatenate(bottoms, axis=1))
        state = jnp.concatenate(lines, axis=0)
        state_b = state.astype(BF16)
        state_ref[p] = state_b
        along = dot(state_b, expand(a_ref[cut, :], head_width), NT).astype(BF16)
        value_t = value_t_ref[p]
        both = jnp.concatenate([along, value_t], axis=1)
        both_ref[p] = both
        weights = jnp.concatenate([spread(small_ref[0, p], steps), spread(small_ref[1, p], steps)], axis=1)
        removed = dot(both, weights, NT)
        update = jnp.concatenate([-removed, value_t.astype(F32)], axis=1)
        step = lax.broadcasted_iota(I32, update.shape, 1) % steps
        update = jnp.where(step < n, update, 0.0).astype(BF16)
        written = jnp.concatenate([expand(b_ref[cut, :], head_width), expand(k_ref[cut, :], head_width)], axis=0)
        kept = (state + dot(update, written)) * last_ref[p : p + 1, :]
        for c in range(halves):
            for pair in range(heads // 2):
                top = kept[(2 * c) * pack : (2 * c + 1) * pack, pair * 128 : (pair + 1) * 128]
                bottom = kept[(2 * c + 1) * pack : (2 * c + 2) * pack, pair * 128 : (pair + 1) * 128]
                at = (p * heads + 2 * pair) * halves + c
                send_ref[sent_at(at)] = jnp.where(low, top, pltpu.roll(bottom, head_width, 1)).astype(BF16)
                send_ref[sent_at(at + halves)] = jnp.where(low, pltpu.roll(top, head_width, 1), bottom).astype(BF16)
        for k in range(heads * halves):
            lane = k * edge_rows
            line = new_edge_ref[p : p + 1, lane // 128 * 128 : lane // 128 * 128 + 128]
            if lane % 128:
                line = pltpu.roll(line, 128 - lane % 128, 1)
            edge_scratch[pl.ds(index_ref[1, p * heads * halves + k], 1), :] = line
    blocks = rows_of(edge_scratch) // per_peer
    for b in range(blocks):
        block = edge_scratch[b * per_peer : (b + 1) * per_peer, :]
        if per_peer < pack:
            block = jnp.concatenate([block, jnp.zeros((pack - per_peer, 128), F32)], axis=0)
        send_ref[b * (per_peer + 1) + per_peer] = block.astype(BF16)


def rows_of(ref):
    return ref.shape[0]


def lines_kernel(gating_ref, *refs):
    *outs, scratch = refs
    requests, part = gating_ref.shape[:2]
    width = scratch.shape[1]
    me = lax.axis_index("head")
    for d, out in enumerate(outs):
        start = pl.multiple_of((me ^ d) * width, 128)
        for p in range(requests):
            scratch[p * part : (p + 1) * part, :] = gating_ref[p, :, pl.ds(start, width)].astype(F32)
        out[...] = scratch[...].astype(BF16)


def read_kernel(
    requests, heads, groups,
    *refs,
):
    return read_body(requests, heads, refs[:groups], *refs[groups:])


def read_body(
    requests, heads,
    recept_refs, cum_ref, key_mod_ref, k_ref, b_ref, solve_ref, state_ref, both_ref, value_ref, reward_ref, gain_ref, offset_ref,
    result_ref, line_scratch, cross, compact, out_scratch,
):
    rows, width = value_ref.shape
    steps = rows // requests
    head_width = width // heads
    lanes = heads * steps
    part = steps // len(recept_refs)
    row = lax.broadcasted_iota(I32, (rows, rows), 0)
    source = (row % steps // part) ^ lax.axis_index("head")
    source_row = source * (requests * part) + row // steps * part + row % part
    order = (source_row == lax.broadcasted_iota(I32, (rows, rows), 1)).astype(F32).astype(BF16)
    recept = dot(order, jnp.concatenate([ref[...] for ref in recept_refs], axis=0))
    bonus = group_sum(recept * key_mod_ref[...] * reward_ref[...], head_width)
    line_scratch[...] = (recept * jnp.exp(cum_ref[...])).astype(BF16)
    for p in range(requests):
        cut = slice(p * steps, (p + 1) * steps)
        right = jnp.concatenate([expand(k_ref[cut, :], head_width), expand(b_ref[cut, :], head_width)], axis=0)
        cross[p] = dot(line_scratch[cut, :], right, NT)
    lane = lax.broadcasted_iota(I32, (requests, lanes), 1)
    source = lane % steps
    group = lane - source
    for t in range(steps):
        weights = jnp.where(source <= t, cross[:, t, lanes:], 0.0)
        from_a = jnp.zeros((requests, lanes), F32)
        from_v = jnp.where(source <= t, cross[:, t, :lanes], 0.0)
        for s in range(t + 1):
            weight = jnp.take_along_axis(weights, group + s, axis=1)
            from_a = from_a - weight * solve_ref[0, s]
            from_v = from_v - weight * solve_ref[1, s]
        compact[0, :, t, :] = from_a
        compact[1, :, t, :] = from_v
    out_low = lax.broadcasted_iota(I32, (steps, 128), 1) < head_width
    for p in range(requests):
        cut = slice(p * steps, (p + 1) * steps)
        read = jnp.concatenate(
            [spread(compact[0, p].astype(BF16), steps), spread(compact[1, p].astype(BF16), steps)], axis=1
        )
        both = both_ref[p]
        state = state_ref[p]
        out = dot(read, jnp.concatenate([both, both], axis=0), NT)
        out = out + dot(expand(line_scratch[cut, :], head_width), jnp.concatenate([state, state], axis=0), NT)
        for pair in range(heads // 2):
            at = 2 * pair * steps
            out_scratch[cut, pair * 128 : (pair + 1) * 128] = jnp.where(
                out_low, out[at : at + steps, :], out[at + steps : at + 2 * steps, :]
            )
    out = out_scratch[...]
    centered = out - group_sum(out, head_width) * (1.0 / head_width)
    variance = group_sum(centered * centered, head_width) * (1.0 / head_width)
    line = centered * lax.rsqrt(variance + NORM_EPSILON) * gain_ref[...] + offset_ref[...]
    result_ref[...] = (line + bonus * value_ref[...].astype(F32)).astype(BF16)


def place_kernel(per_peer, index_ref, back_ref, out_ref, edge_ref, scratch, edge_scratch, edge_placed):
    slot_dev = out_ref.shape[0]
    pack = back_ref.shape[1]
    for b in range(slot_dev // per_peer):
        block = back_ref[b * (per_peer + 1) + per_peer].astype(F32)
        edge_scratch[b * per_peer : (b + 1) * per_peer, :] = block[:per_peer, :]
    for s in range(slot_dev):
        place = index_ref[0, s]
        scratch[s] = back_ref[place + place // per_peer].astype(F32)
        edge_placed[s : s + 1, :] = edge_scratch[pl.ds(place, 1), :]
    left = lax.broadcasted_iota(I32, (slot_dev, 128), 1) < 64
    half = pack // 2
    for b in range(half):
        even = scratch[:, 2 * b, :]
        odd = scratch[:, 2 * b + 1, :]
        out_ref[:, b * 128 : (b + 1) * 128] = jnp.where(left, even, pltpu.roll(odd, 64, 1))
        out_ref[:, (half + b) * 128 : (half + b + 1) * 128] = jnp.where(left, pltpu.roll(even, 64, 1), odd)
    edge_ref[...] = jnp.transpose(edge_placed[...])[: edge_ref.shape[0], :]


def local(
    layer_entry_vectors,
    guessed_lookup_vectors,
    guessed_content_vectors,
    gating_query,
    lane_memory_store,
    prior_step_store,
    fading_blend_ratio,
    learning_speed_blend,
    fading_left_factor,
    fading_right_factor,
    fading_offset,
    learning_speed_left,
    learning_speed_right,
    learning_speed_offset,
    erasing_lookup_factor,
    written_lookup_factor,
    present_reward_factors,
    lane_standard_factor,
    lane_standard_offset,
    caller_memory_directory,
    kept_target_place,
    caller_sequence,
    approved_guesses,
):
    blocks = lax.axis_size("blk")
    groups = lax.axis_size("head")
    requests, steps, width = layer_entry_vectors.shape
    heads, halves = caller_memory_directory.shape[1:]
    slot_dev = lane_memory_store.shape[1]
    slot_width = lane_memory_store.shape[2]
    pack = slot_width // 128
    per_peer = slot_dev // blocks
    edge_rows = prior_step_store.shape[2]
    rows = requests * steps
    rank = fading_left_factor.shape[1]
    sds = jax.ShapeDtypeStruct

    def line(x):
        return x.reshape(1, width)

    def exchange(x, axis):
        return lax.all_to_all(x, axis, split_axis=0, concat_axis=0, tiled=True)

    read_table = caller_memory_directory.transpose(1, 2, 0)
    write_table = kept_target_place.transpose(1, 2, 0)
    pool = jnp.broadcast_to(prior_step_store[0].T, (blocks, edge_rows, slot_dev))
    edges = exchange(pool, "blk")
    sent, index = call(
        functools.partial(send_kernel, blocks, requests, per_peer),
        (sds((slot_dev, pack, 128), BF16), sds((8, slot_dev), I32)),
        [SMEM()] + [VMEM()] * 3,
        [pltpu.VMEM((slot_dev, pack, 128), F32)],
    )(caller_sequence, read_table, write_table, lane_memory_store[0])
    got = exchange(sent.reshape(blocks, per_peer * pack, 128), "blk").reshape(slot_dev, pack, 128)

    layer = layer_entry_vectors.reshape(rows, width)
    key = guessed_lookup_vectors.reshape(rows, width)
    value = guessed_content_vectors.reshape(rows, width)
    partial_sums, new_edge = call(
        functools.partial(shift_kernel, requests, heads, halves),
        (sds((rows, 2 * rank), BF16), sds((requests, width), F32)),
        [SMEM(), SMEM(), SMEM()] + [VMEM()] * 6,
        [
            pltpu.VMEM((blocks * slot_dev, slot_dev), F32),
            pltpu.VMEM((requests, width), F32),
            pltpu.VMEM((rows, width), F32),
        ],
    )(
        index, caller_sequence, approved_guesses, edges, layer, line(fading_blend_ratio), line(learning_speed_blend),
        fading_left_factor.T, learning_speed_left.T,
    )
    parts = lax.all_gather(partial_sums, "head", axis=0)

    wide = sds((rows, width), BF16)
    full = sds((rows, width), F32)
    a_lines, k_lines, b_lines, cum, key_mod, last, value_t, small, solve = call(
        functools.partial(prepare_kernel, requests, heads),
        (
            wide, wide, wide, full, full,
            sds((requests, width), F32),
            sds((requests, width // heads, heads * steps), BF16),
            sds((2, requests, steps, heads * steps), BF16),
            sds((2, steps, requests, heads * steps), F32),
        ),
        [SMEM(), SMEM()] + [VMEM()] * 9,
        [
            pltpu.VMEM((requests, steps, 2 * heads * steps), F32),
            pltpu.VMEM((2, requests, steps, heads * steps), F32),
        ],
    )(
        caller_sequence, approved_guesses, parts, fading_right_factor, learning_speed_right,
        line(fading_offset), line(learning_speed_offset), key, value,
        line(erasing_lookup_factor), line(written_lookup_factor),
    )
    back, state, both = call(
        functools.partial(state_kernel, requests, heads, halves, per_peer),
        (
            sds((blocks * (per_peer + 1), pack, 128), BF16),
            sds((requests, width // heads, width), BF16),
            sds((requests, width // heads, 2 * heads * steps), BF16),
        ),
        [SMEM(), SMEM(), SMEM()] + [VMEM()] * 8,
        [pltpu.VMEM((slot_dev, 128), F32)],
    )(
        index, caller_sequence, approved_guesses, got, a_lines, k_lines, b_lines, last, value_t, small, new_edge,
    )
    back = exchange(back.reshape(blocks, (per_peer + 1) * pack, 128), "blk")
    back = back.reshape(blocks * (per_peer + 1), pack, 128)
    recept = call(
        lines_kernel,
        (sds((rows // groups, width), BF16),) * groups,
        [VMEM()],
        [pltpu.VMEM((rows // groups, width), F32)],
    )(gating_query)
    recept = [recept[0]] + [
        lax.ppermute(recept[d], "head", [(g, g ^ d) for g in range(groups)]) for d in range(1, groups)
    ]
    result = call(
        functools.partial(read_kernel, requests, heads, groups),
        wide,
        [VMEM()] * (11 + groups),
        [
            pltpu.VMEM((rows, width), BF16),
            pltpu.VMEM((requests, steps, 2 * heads * steps), F32),
            pltpu.VMEM((2, requests, steps, heads * steps), F32),
            pltpu.VMEM((rows, width), F32),
        ],
    )(
        *recept, cum, key_mod, k_lines, b_lines, solve, state, both, value,
        line(present_reward_factors), line(lane_standard_factor), line(lane_standard_offset),
    )
    target = call(
        functools.partial(target_kernel, blocks, requests, per_peer, slot_dev),
        sds((8, slot_dev), I32),
        [SMEM(), VMEM()],
    )(caller_sequence, write_table)
    new_states, new_edges = call(
        functools.partial(place_kernel, per_peer),
        (sds((slot_dev, slot_width), F32), sds((edge_rows, slot_dev), F32)),
        [SMEM(), VMEM()],
        [
            pltpu.VMEM((slot_dev, pack, 128), F32),
            pltpu.VMEM((slot_dev, 128), F32),
            pltpu.VMEM((slot_dev, 128), F32),
        ],
    )(target, back)
    return (result.reshape(requests, steps, width), new_states[None], new_edges.T[None])


def solution(mesh):
    return jax.shard_map(
        local,
        mesh=mesh,
        in_specs=(
            P("blk", None, "head"),
            P("blk", None, "head"),
            P("blk", None, "head"),
            P("blk", "head", None),
            P("head", "blk", None),
            P("head", "blk", None),
            P("head"),
            P("head"),
            P("head", None),
            P(None, "head"),
            P("head"),
            P("head", None),
            P(None, "head"),
            P("head"),
            P("head"),
            P("head"),
            P("head"),
            P("head"),
            P("head"),
            P(None, "head", None),
            P(None, "head", None),
            P(),
            P(),
        ),
        out_specs=(P("blk", None, "head"), P("head", "blk", None), P("head", "blk", None)),
        check_vma=False,
    )
```

time: 386 us -> 62.2 us (0.16)
  other arithmetic: 172 us -> 0 us
  local copies, waits for them, and re-layouts: 125 us -> 5.29 us
  starting transfers between devices: 38.7 us -> 17.5 us
  Pallas kernels: 0 us -> 18.7 us
  loops' own time: 11.1 us -> 0 us
  waiting for transfers between devices: 20.3 us -> 13.4 us
  blocking collectives: 12.2 us -> 5.92 us
    mul x33 -> x0, other arithmetic: 150 us -> none  [the longest x16 135 us: advance(): projected[..., None] * (rate_t * unit_t)[:, :, None, :]]
    mul x51 -> x0, local copies, waits for them, and re-layouts: 37.5 us -> none  [the longest x16 12.5 us: advance(): output = jnp.sum(carry_state * recept_t[:, :, None, :], axis=-1)]
    all_to_all x7 -> x3, starting transfers between devices: 38.7 us -> 15.5 us  [exchange(): return lax.all_to_all(x, axis, split_axis=0, concat_axis=0, tiled=True)]
    pallas_call x0 -> x8, Pallas kernels: none -> 18.7 us  [the longest x1 4.04 us: local(): call(functools.partial(state_kernel, requests, heads, halves, per_peer),...]
    gather x17 -> x0, local copies, waits for them, and re-layouts: 17.3 us -> none  [the longest x1 2.04 us: local(): carried[1].reshape(slot_dev, slot_rows * head_width)[return_sort]]
    while x80 -> x0, local copies, waits for them, and re-layouts: 13.4 us -> none
    unnamed x77 -> x44, local copies, waits for them, and re-layouts: 16.2 us -> 3.91 us
    psum x1 -> x0, blocking collectives: 12.2 us -> none  [local(): lax.psum(partial_terms.astype(jnp.bfloat16), 'head').astype(jnp.float32)]
  transfers between devices with their start and end apart: 7 -> 6, of which waited for: 2 -> 5; matrix products, arithmetic and copies ran while one was open for 72% -> 0% of each run, Pallas kernels for 0% -> 19%
where the time goes in v1:
time: 62.2 us; the launch traced here: 61.6 us
  Pallas kernels  18.7 us (30%)
  starting transfers between devices  17.5 us (28%)
  waiting for transfers between devices  13.4 us (22%)
  blocking collectives  5.92 us (10%)
  local copies, waits for them, and re-layouts  5.29 us (9%)
  between operations  0.82 us (1%)
    all_to_all x3, starting transfers between devices, exchange(): return lax.all_to_all(x, axis, split_axis=0, concat_axis=0, tiled=True)  15.5 us
    all_to_all x3, waiting for transfers between devices, exchange(): return lax.all_to_all(x, axis, split_axis=0, concat_axis=0, tiled=True)  11.3 us
    all_gather x1, blocking collectives, local(): parts = lax.all_gather(partial_sums, 'head', axis=0)  5.92 us
    pallas_call x1, Pallas kernels, local(): call(functools.partial(state_kernel, requests, heads, halves, per_peer),...  4.04 us
    unnamed x44, local copies, waits for them, and re-layouts  3.91 us
    pallas_call x1, Pallas kernels, local(): call(functools.partial(send_kernel, blocks, requests, per_peer), (sds((sl...  3.66 us
    pallas_call x1, Pallas kernels, local(): call(functools.partial(place_kernel, per_peer), (sds((slot_dev, slot_widt...  3.01 us
    pallas_call x1, Pallas kernels, local(): call(functools.partial(read_kernel, requests, heads, groups), wide, [VMEM...  2.8 us
  transfers between devices with their start and end apart: 6, of which 5 were waited for; matrix products, arithmetic and copies ran while one was open for 0% of the time, Pallas kernels for 19%

profile of v1, /device:TPU:0, one launch (start us, length us, event | category | flops | bytes accessed | tf_op | source)
XLA Modules:
  0.0 61.6 jit_solution(5130633344149949859)
XLA Ops:
  0.6 1.4 %broadcast_in_dim.9 = f32[8,32,128]{2,1,0:T(8,128)} broadcast(f32[32,128]{1,0:T(8,128)} %bitcast.53), dimensions={1,2} | broadcast | bytes 147456 | tf_op jit(solution)/shard_map/broadcast_in_dim | solution.py:486
  2.0 0.0 copy-start.9
  2.0 7.4 %all-to-all-start = ((f32[8,32,128]{2,1,0:T(8,128)}), f32[8,32,128]{2,1,0:T(8,128)S(1)}, u32[]{:S(2)}, u32[]{:S(2)}) async-start(f32[8,32,128]{2,1,0:T(8,128)} %broadcast_in_dim.9), calls=%async_computation | async-start | bytes 262144 | tf_op jit(solution)/shard_map/all_to_all | solution.py:482
  9.4 0.0 copy-start.10
  9.4 0.0 copy-done.9
  9.4 0.0 copy-done.11
  9.5 0.6 %copy-done.10 = s32[64]{0:T(128)S(1)} copy-done((s32[64]{0:T(128)S(1)}, s32[64]{0:T(128)}, u32[]{:S(2)}) %copy-start.10) | copy-done | bytes 280
  10.1 0.0 copy-start
  10.1 1.2 %copy-done = f32[1,128,2048]{2,1,0:T(8,128)S(1)} copy-done((f32[1,128,2048]{2,1,0:T(8,128)S(1)}, f32[1,128,2048]{2,1,0:T(8,128)}, u32[]{:S(2)}) %copy-start) | copy-done | bytes 1048600
  11.3 3.7 %shard_map.239 = (bf16[128,16,128]{2,1,0:T(8,128)(2,1)}, s32[8,128]{1,0:T(8,128)S(1)}) custom-call(s32[64]{0:T(128)S(1)} %copy-done.10, s32[8,2,64]{2,1,0:T(2,128)S(1)} %bitcast.42, s32[8,2,64]{2,1,0:T(2,128)S(1)} %bitcast.40, f32[128,2048]{1,0:T(8,128)S(1)} %bitcast.33), custom_call_target="tpu_custom_call" | custom-call | flops 1048576 | bytes 1048576 | tf_op jit(solution)/shard_map/pallas_call | solution.py:488
  15.0 1.8 %all-to-all-done.edges_ref = f32[8,32,128]{2,1,0:T(8,128)S(1)} async-done(((f32[8,32,128]{2,1,0:T(8,128)}), f32[8,32,128]{2,1,0:T(8,128)S(1)}, u32[]{:S(2)}, u32[]{:S(2)}) %all-to-all-start) | async-done | bytes 131104 | tf_op jit(solution)/shard_map/all_to_all | solution.py:482
  16.8 0.0 copy-start.2
  16.8 0.0 copy-start.5
  16.8 0.0 copy-start.6
  16.8 4.3 %all-to-all-start.1 = ((bf16[8,256,128]{2,1,0:T(8,128)(2,1)}), bf16[8,256,128]{2,1,0:T(8,128)(2,1)S(1)}, u32[]{:S(2)}, u32[]{:S(2)}) async-start(bf16[8,256,128]{2,1,0:T(8,128)(2,1)} %bitcast.17), calls=%async_computation.1 | async-start | bytes 1048576 | tf_op jit(solution)/shard_map/all_to_all | solution.py:482
  21.1 0.0 copy-start.14
  21.1 0.0 copy-start.13
  21.1 0.0 copy-start.12
  21.2 0.0 copy-done.2
  21.2 0.0 copy-done.5
  21.2 0.0 copy-done.6
  21.2 0.6 %copy-done.14 = f32[512]{0:T(512)S(1)} copy-done((f32[512]{0:T(512)S(1)}, f32[512]{0:T(512)}, u32[]{:S(2)}) %copy-start.14) | copy-done | bytes 2072
  21.8 0.0 copy-done.13
  21.8 0.0 copy-done.12
  21.8 0.0 copy-start.7
  21.8 0.0 copy-start.8
  21.8 1.9 %shard_map.240 = (bf16[128,192]{1,0:T(8,128)(2,1)S(1)}, f32[8,512]{1,0:T(8,128)S(1)}) custom-call(s32[8,128]{1,0:T(8,128)S(1)} %get-tuple-element.29.index_ref, s32[64]{0:T(128)S(1)} %copy-done.10, s32[64]{0:T(128)S(1)} %copy-done.12, f32[8,32,128]{2,1,0:T(8,128)S(1)} %all-to-all-done.edges_ref, bf16[128,512]{1,0:T(8,128)(2,1)S(1)} %bitcast.36, ...), custom_call_target="tpu_custom_call" | custom-call | flops 1048576 | bytes 1048576 | tf_op jit(solution)/shard_map/pallas_call | solution.py:499
  23.7 0.0 copy-start.1
  23.7 0.0 copy-start.4
  23.7 0.0 copy-start.17
  23.8 0.0 copy-start.18
  23.8 5.9 %all-gather = bf16[512,192]{1,0:T(8,128)(2,1)S(1)} all-gather(bf16[128,192]{1,0:T(8,128)(2,1)S(1)} %get-tuple-element.30), channel_id=2, replica_groups=mesh['blk'=8,'head'=4] {'head'}, dimensions={0}, use_global_device_ids=true | all-gather | bytes 245760 | tf_op jit(solution)/shard_map/all_gather | solution.py:512
  29.7 0.0 copy-start.16
  29.7 0.0 copy-start.15
  29.7 0.0 copy-done.7
  29.7 0.0 copy-done.8
  29.7 0.0 copy-done.1
  29.7 0.0 copy-done.4
  29.7 0.0 copy-done.17
  29.7 0.0 copy-done.18
  29.7 0.6 %copy-done.16 = f32[512]{0:T(512)S(1)} copy-done((f32[512]{0:T(512)S(1)}, f32[512]{0:T(512)}, u32[]{:S(2)}) %copy-start.16) | copy-done | bytes 2072
  30.4 0.0 copy-done.15
  30.4 2.3 %shard_map.241 = (bf16[128,512]{1,0:T(8,128)(2,1)S(1)}, bf16[128,512]{1,0:T(8,128)(2,1)S(1)}, bf16[128,512]{1,0:T(8,128)(2,1)S(1)}, f32[128,512]{1,0:T(8,128)S(1...) custom-call(s32[64]{0:T(128)S(1)} %copy-done.10, ...), custom_call_target="tpu_custom_call" | custom-call | flops 1048576 | bytes 1048576 | tf_op jit(solution)/shard_map/pallas_call | solution.py:516
  32.7 2.5 %all-to-all-done.1 = bf16[8,256,128]{2,1,0:T(8,128)(2,1)S(1)} async-done(((bf16[8,256,128]{2,1,0:T(8,128)(2,1)}), bf16[8,256,128]{2,1,0:T(8,128)(2,1)S(1)}, u32[]{:S(2)}, u32[]{:S(2)}) %all-to-all-start.1) | async-done | bytes 524320 | tf_op jit(solution)/shard_map/all_to_all | solution.py:482
  35.1 4.0 %shard_map.242 = (bf16[136,16,128]{2,1,0:T(8,128)(2,1)}, bf16[8,64,512]{2,1,0:T(8,128)(2,1)S(1)}, bf16[8,64,256]{2,1,0:T(8,128)(2,1)S(1)}) custom-call(s32[8,128]{1,0:T(8,128)S(1)} %get-tuple-element.29.index_ref, s32[64]{0:T(128)S(1)} %copy-done.10, s32[64]{0:T(128)S(1)} %copy-done.12, bf16[128,16,128]{2,1,0:T(8,128)(2,1)S(1)} %bitcast.31, ...), custom_call_target="tpu_custom_call" | custom-call | flops 1048576 | bytes 1048576 | tf_op jit(solution)/shard_map/pallas_call | solution.py:535
  39.2 3.8 %all-to-all-start.2 = ((bf16[8,272,128]{2,1,0:T(8,128)(2,1)}), bf16[8,272,128]{2,1,0:T(8,128)(2,1)S(1)}, u32[]{:S(2)}, u32[]{:S(2)}) async-start(bf16[8,272,128]{2,1,0:T(8,128)(2,1)} %bitcast.23), calls=%async_computation.2 | async-start | bytes 1114112 | tf_op jit(solution)/shard_map/all_to_all | solution.py:482
  42.9 0.0 copy-done.3
  42.9 0.0 copy-start.21
  42.9 0.1 shard_map.238
  43.0 0.1 collective-permute-start
  43.1 1.6 %collective-permute-start.1 = (bf16[32,512]{1,0:T(8,128)(2,1)S(1)}, bf16[32,512]{1,0:T(8,128)(2,1)S(1)}, u32[]{:S(2)}, u32[]{:S(2)}) collective-permute-start(bf16[32,512]{1,0:T(8,128)(2,1)S(1)} %get-tuple-element.27), channel_id=1, source_target_pairs={{0,2},{1,3},{2,0},{3,1},{4,6},{5,7},{6,4},{7,5},{8,10},{9,11},{10,... | collective-permute-start | bytes 98312 | tf_op jit(solution)/shard_map/ppermute | solution.py:556
  44.7 0.3 collective-permute-start.2
  45.0 0.9 %shard_map.244.index_ref = s32[8,128]{1,0:T(8,128)S(1)} custom-call(s32[64]{0:T(128)S(1)} %copy-done.10, s32[8,2,64]{2,1,0:T(2,128)S(1)} %bitcast.41), custom_call_target="tpu_custom_call" | custom-call | flops 1048576 | bytes 1048576 | tf_op jit(solution)/shard_map/pallas_call | solution.py:572
  45.9 0.0 collective-permute-done.refs_1_
  45.9 1.2 %collective-permute-done.1.refs_2_ = bf16[32,512]{1,0:T(8,128)(2,1)S(1)} collective-permute-done((bf16[32,512]{1,0:T(8,128)(2,1)S(1)}, bf16[32,512]{1,0:T(8,128)(2,1)S(1)}, u32[]{:S(2)}, u32[]{:S(2)}) %collective-permute-start.1) | collective-permute-done | bytes 32800 | tf_op jit(solution)/shard_map/ppermute | solution.py:556
  47.1 0.9 %collective-permute-done.2.refs_3_ = bf16[32,512]{1,0:T(8,128)(2,1)S(1)} collective-permute-done((bf16[32,512]{1,0:T(8,128)(2,1)S(1)}, bf16[32,512]{1,0:T(8,128)(2,1)S(1)}, u32[]{:S(2)}, u32[]{:S(2)}) %collective-permute-start.2) | collective-permute-done | bytes 32800 | tf_op jit(solution)/shard_map/ppermute | solution.py:556
  48.0 0.0 copy-start.20
  48.0 0.0 copy-start.19
  48.0 0.0 copy-done.21
  48.0 0.7 %copy-done.20 = f32[512]{0:T(512)S(1)} copy-done((f32[512]{0:T(512)S(1)}, f32[512]{0:T(512)}, u32[]{:S(2)}) %copy-start.20) | copy-done | bytes 2072
  48.7 0.0 copy-done.19
  48.7 2.8 %shard_map.243 = bf16[128,512]{1,0:T(8,128)(2,1)} custom-call(bf16[32,512]{1,0:T(8,128)(2,1)S(1)} %get-tuple-element.25.refs_0_, bf16[32,512]{1,0:T(8,128)(2,1)S(1)} %collective-permute-done.refs_1_, bf16[32,512]{1,0:T(8,128)(2,1)S(1)} %collective-permute-done.1.refs_2_, bf16[32,512]{1,0:T(8,128)(2,1)S(1)} %collective-permute-done.2.refs_3_, ...), custom_call_target="tpu_custom_call" | custom-call | flops 1048576 | bytes 1048576 | tf_op jit(solution)/shard_map/pallas_call | solution.py:558
  51.5 7.1 %all-to-all-done.2 = bf16[8,272,128]{2,1,0:T(8,128)(2,1)S(1)} async-done(((bf16[8,272,128]{2,1,0:T(8,128)(2,1)}), bf16[8,272,128]{2,1,0:T(8,128)(2,1)S(1)}, u32[]{:S(2)}, u32[]{:S(2)}) %all-to-all-start.2) | async-done | bytes 557088 | tf_op jit(solution)/shard_map/all_to_all | solution.py:482
  58.6 3.0 %shard_map.245 = (f32[128,2048]{1,0:T(8,128)}, f32[32,128]{1,0:T(8,128)}) custom-call(s32[8,128]{1,0:T(8,128)S(1)} %shard_map.244.index_ref, bf16[136,16,128]{2,1,0:T(8,128)(2,1)S(1)} %bitcast.30), custom_call_target="tpu_custom_call" | custom-call | flops 1048576 | bytes 1048576 | tf_op jit(solution)/shard_map/pallas_call | solution.py:577
  (2 shorter events, 0.0 us)
Async XLA Ops:
  2.0 7.4 %copy-start.9 = (s32[64,8,2]{0,2,1:T(2,128)S(1)}, s32[64,8,2]{0,2,1:T(2,128)}, u32[]{:S(2)}) copy-start(s32[64,8,2]{0,2,1:T(2,128)} %param.43) | copy-start | bytes 12292
  2.0 7.4 %copy-start.11 = (s32[64,8,2]{0,2,1:T(2,128)S(1)}, s32[64,8,2]{0,2,1:T(2,128)}, u32[]{:S(2)}) copy-start(s32[64,8,2]{0,2,1:T(2,128)} %param.42) | copy-start | bytes 12292
  2.0 14.8 %all-to-all-start = ((f32[8,32,128]{2,1,0:T(8,128)}), f32[8,32,128]{2,1,0:T(8,128)S(1)}, u32[]{:S(2)}, u32[]{:S(2)}) async-start(f32[8,32,128]{2,1,0:T(8,128)} %broadcast_in_dim.9), calls=%async_computation | async-start | bytes 262144 | tf_op jit(solution)/shard_map/all_to_all | solution.py:482
  9.4 0.7 %copy-start.10 = (s32[64]{0:T(128)S(1)}, s32[64]{0:T(128)}, u32[]{:S(2)}) copy-start(s32[64]{0:T(128)} %seq_ref.9) | copy-start | bytes 772
  10.1 1.2 %copy-start = (f32[1,128,2048]{2,1,0:T(8,128)S(1)}, f32[1,128,2048]{2,1,0:T(8,128)}, u32[]{:S(2)}) copy-start(f32[1,128,2048]{2,1,0:T(8,128)} %param.27) | copy-start | bytes 3145732
  16.8 4.4 %copy-start.2 = (bf16[8,16,512]{2,1,0:T(8,128)(2,1)S(1)}, bf16[8,16,512]{2,1,0:T(8,128)(2,1)}, u32[]{:S(2)}) copy-start(bf16[8,16,512]{2,1,0:T(8,128)(2,1)} %param.23) | copy-start | bytes 393220
  16.8 4.4 %copy-start.5 = (bf16[512,96]{0,1:T(8,128)(2,1)S(1)}, bf16[512,96]{0,1:T(8,128)(2,1)}, u32[]{:S(2)}) copy-start(bf16[512,96]{0,1:T(8,128)(2,1)} %param.31) | copy-start | bytes 294916
  16.8 4.4 %copy-start.6 = (bf16[512,96]{0,1:T(8,128)(2,1)S(1)}, bf16[512,96]{0,1:T(8,128)(2,1)}, u32[]{:S(2)}) copy-start(bf16[512,96]{0,1:T(8,128)(2,1)} %param.34) | copy-start | bytes 294916
  16.8 18.3 %all-to-all-start.1 = ((bf16[8,256,128]{2,1,0:T(8,128)(2,1)}), bf16[8,256,128]{2,1,0:T(8,128)(2,1)S(1)}, u32[]{:S(2)}, u32[]{:S(2)}) async-start(bf16[8,256,128]{2,1,0:T(8,128)(2,1)} %bitcast.17), calls=%async_computation.1 | async-start | bytes 1048576 | tf_op jit(solution)/shard_map/all_to_all | solution.py:482
  21.1 0.7 %copy-start.14 = (f32[512]{0:T(512)S(1)}, f32[512]{0:T(512)}, u32[]{:S(2)}) copy-start(f32[512]{0:T(512)} %param.30) | copy-start | bytes 6148
  21.1 0.7 %copy-start.13 = (f32[512]{0:T(512)S(1)}, f32[512]{0:T(512)}, u32[]{:S(2)}) copy-start(f32[512]{0:T(512)} %param.29) | copy-start | bytes 6148
  21.1 0.7 %copy-start.12 = (s32[64]{0:T(128)S(1)}, s32[64]{0:T(128)}, u32[]{:S(2)}) copy-start(s32[64]{0:T(128)} %count_ref.5) | copy-start | bytes 772
  21.8 7.9 %copy-start.7 = (bf16[96,512]{1,0:T(8,128)(2,1)S(1)}, bf16[96,512]{1,0:T(8,128)(2,1)}, u32[]{:S(2)}) copy-start(bf16[96,512]{1,0:T(8,128)(2,1)} %right_decay_ref.1) | copy-start | bytes 294916
  21.8 7.9 %copy-start.8 = (bf16[96,512]{1,0:T(8,128)(2,1)S(1)}, bf16[96,512]{1,0:T(8,128)(2,1)}, u32[]{:S(2)}) copy-start(bf16[96,512]{1,0:T(8,128)(2,1)} %right_rate_ref.1) | copy-start | bytes 294916
  23.7 6.0 %copy-start.1 = (bf16[8,16,512]{2,1,0:T(8,128)(2,1)S(1)}, bf16[8,16,512]{2,1,0:T(8,128)(2,1)}, u32[]{:S(2)}) copy-start(bf16[8,16,512]{2,1,0:T(8,128)(2,1)} %param.25) | copy-start | bytes 393220
  23.7 6.0 %copy-start.4 = (bf16[8,16,512]{2,1,0:T(8,128)(2,1)S(1)}, bf16[8,16,512]{2,1,0:T(8,128)(2,1)}, u32[]{:S(2)}) copy-start(bf16[8,16,512]{2,1,0:T(8,128)(2,1)} %param.24) | copy-start | bytes 393220
  23.7 6.0 %copy-start.17 = (f32[512]{0:T(512)S(1)}, f32[512]{0:T(512)}, u32[]{:S(2)}) copy-start(f32[512]{0:T(512)} %param.37) | copy-start | bytes 6148
  23.8 6.0 %copy-start.18 = (f32[512]{0:T(512)S(1)}, f32[512]{0:T(512)}, u32[]{:S(2)}) copy-start(f32[512]{0:T(512)} %param.38) | copy-start | bytes 6148
  29.7 0.7 %copy-start.16 = (f32[512]{0:T(512)S(1)}, f32[512]{0:T(512)}, u32[]{:S(2)}) copy-start(f32[512]{0:T(512)} %param.36) | copy-start | bytes 6148
  29.7 0.7 %copy-start.15 = (f32[512]{0:T(512)S(1)}, f32[512]{0:T(512)}, u32[]{:S(2)}) copy-start(f32[512]{0:T(512)} %param.33) | copy-start | bytes 6148
  39.2 3.8 %copy-start.3 = (bf16[8,4,2048]{2,1,0:T(4,128)(2,1)S(1)}, bf16[8,4,2048]{2,1,0:T(4,128)(2,1)}, u32[]{:S(2)}) copy-start(bf16[8,4,2048]{2,1,0:T(4,128)(2,1)} %gating_ref.1) | copy-start | bytes 393220
  39.2 19.4 %all-to-all-start.2 = ((bf16[8,272,128]{2,1,0:T(8,128)(2,1)}), bf16[8,272,128]{2,1,0:T(8,128)(2,1)S(1)}, u32[]{:S(2)}, u32[]{:S(2)}) async-start(bf16[8,272,128]{2,1,0:T(8,128)(2,1)} %bitcast.23), calls=%async_computation.2 | async-start | bytes 1114112 | tf_op jit(solution)/shard_map/all_to_all | solution.py:482
  42.9 5.1 %copy-start.21 = (f32[512]{0:T(512)S(1)}, f32[512]{0:T(512)}, u32[]{:S(2)}) copy-start(f32[512]{0:T(512)} %param.41) | copy-start | bytes 6148
  43.0 2.9 %collective-permute-start = (bf16[32,512]{1,0:T(8,128)(2,1)S(1)}, bf16[32,512]{1,0:T(8,128)(2,1)S(1)}, u32[]{:S(2)}, u32[]{:S(2)}) collective-permute-start(bf16[32,512]{1,0:T(8,128)(2,1)S(1)} %get-tuple-element.26), channel_id=1, source_target_pairs={{0,1},{1,0},{2,3},{3,2},{4,5},{5,4},{6,7},{7,6},{8,9},{9,8},{10,11... | collective-permute-start | bytes 98312 | tf_op jit(solution)/shard_map/ppermute | solution.py:556
  43.1 4.0 %collective-permute-start.1 = (bf16[32,512]{1,0:T(8,128)(2,1)S(1)}, bf16[32,512]{1,0:T(8,128)(2,1)S(1)}, u32[]{:S(2)}, u32[]{:S(2)}) collective-permute-start(bf16[32,512]{1,0:T(8,128)(2,1)S(1)} %get-tuple-element.27), channel_id=1, source_target_pairs={{0,2},{1,3},{2,0},{3,1},{4,6},{5,7},{6,4},{7,5},{8,10},{9,11},{10,... | collective-permute-start | bytes 98312 | tf_op jit(solution)/shard_map/ppermute | solution.py:556
  44.7 3.3 %collective-permute-start.2 = (bf16[32,512]{1,0:T(8,128)(2,1)S(1)}, bf16[32,512]{1,0:T(8,128)(2,1)S(1)}, u32[]{:S(2)}, u32[]{:S(2)}) collective-permute-start(bf16[32,512]{1,0:T(8,128)(2,1)S(1)} %get-tuple-element.28), channel_id=1, source_target_pairs={{0,3},{1,2},{2,1},{3,0},{4,7},{5,6},{6,5},{7,4},{8,11},{9,10},{10,... | collective-permute-start | bytes 98312 | tf_op jit(solution)/shard_map/ppermute | solution.py:556
  48.0 0.7 %copy-start.20 = (f32[512]{0:T(512)S(1)}, f32[512]{0:T(512)}, u32[]{:S(2)}) copy-start(f32[512]{0:T(512)} %param.40) | copy-start | bytes 6148
  48.0 0.7 %copy-start.19 = (f32[512]{0:T(512)S(1)}, f32[512]{0:T(512)}, u32[]{:S(2)}) copy-start(f32[512]{0:T(512)} %param.39) | copy-start | bytes 6148

commit v2 on v1

v2 whole, which is shorter than its diff:
```python
import functools

import jax
import jax.numpy as jnp
from jax import lax
from jax.experimental import pallas as pl
from jax.experimental.pallas import tpu as pltpu
from jax.sharding import PartitionSpec as P

EPSILON = 1e-05
NORM_EPSILON = 0.00064
DECAY_SCALE = 0.6065306597126334
F32 = jnp.float32
BF16 = jnp.bfloat16
I32 = jnp.int32
NT = (((1,), (1,)), ((), ()))
NN = (((1,), (0,)), ((), ()))


def call(kernel, outs, scalars=(), near=(), far=(), raw=(), held=(), scratch=(), vmem=16):
    reads = len(scalars) + len(near) + len(far) + len(raw)

    def body(*refs):
        kernel(*refs[:reads], *refs[reads + len(held) :])

    args = [*scalars]
    args += [*near]
    args += [pltpu.with_memory_space_constraint(x, pltpu.HBM) for x in (*far, *raw)]
    specs = [pl.BlockSpec(memory_space=pltpu.SMEM)] * len(scalars)
    specs += [pl.BlockSpec(memory_space=pltpu.VMEM)] * (len(near) + len(far))
    specs += [pl.BlockSpec(memory_space=pltpu.HBM)] * (len(raw) + len(held))
    return pl.pallas_call(
        body,
        out_shape=outs,
        in_specs=specs,
        out_specs=jax.tree.map(lambda _: pl.BlockSpec(memory_space=pltpu.VMEM), outs),
        scratch_shapes=list(scratch),
        compiler_params=pltpu.CompilerParams(vmem_limit_bytes=vmem * 1024 * 1024),
        cost_estimate=pl.CostEstimate(flops=1 << 20, bytes_accessed=1 << 20, transcendentals=0),
    )(*args, *held)


def dot(a, b, dims=NN):
    return lax.dot_general(a, b, dims, preferred_element_type=F32)


def split(x):
    high = x.astype(BF16)
    return high, (x - high.astype(F32)).astype(BF16)


def group_sum(x, width):
    rows, lanes = x.shape
    block = max(width, 128)
    ones = (
        lax.broadcasted_iota(I32, (block, block), 0) // width
        == lax.broadcasted_iota(I32, (block, block), 1) // width
    ).astype(BF16)
    high, low = split(x)
    parts = []
    for start in range(0, lanes, block):
        cut = slice(start, start + block)
        parts.append(dot(high[:, cut], ones) + dot(low[:, cut], ones))
    return jnp.concatenate(parts, axis=1)


def positions(seq_ref, count):
    lane = lax.broadcasted_iota(I32, (1, count), 1)

    def block(b, acc):
        for k in range(8):
            acc = jnp.where(lane == seq_ref[b * 8 + k], b * 8 + k, acc)
        return acc

    return lax.fori_loop(0, count // 8, block, jnp.zeros((1, count), I32))


def place_of_slot(table_ref, position, base, blocks, per_peer, requests, slot_dev):
    heads, halves, count = table_ref.shape
    slot = lax.broadcasted_iota(I32, (slot_dev, count), 0) + base
    named = jnp.zeros((slot_dev, count), F32)
    for h in range(heads):
        for c in range(halves):
            named = jnp.where(table_ref[h, c : c + 1, :] == slot, 1.0, named)
    other_of = jnp.broadcast_to(position // requests, (16, count)).astype(F32).astype(BF16)
    other = dot(other_of, named.astype(BF16), NT)[0:1, :].astype(I32)
    rows = max(16, blocks)
    mask = other == lax.broadcasted_iota(I32, (rows, slot_dev), 0)
    before = (
        lax.broadcasted_iota(I32, (slot_dev, slot_dev), 0)
        < lax.broadcasted_iota(I32, (slot_dev, slot_dev), 1)
    ).astype(F32).astype(BF16)
    ahead = dot(mask.astype(F32).astype(BF16), before)
    rank = jnp.sum(jnp.where(mask, ahead, 0.0), axis=0, keepdims=True).astype(I32)
    return other * per_peer + rank


def place_of_item(table_ref, lines_ref, position, first, requests):
    heads, halves, count = table_ref.shape
    per_item = heads * halves
    items = requests * per_item
    mine = (
        jnp.broadcast_to(position, (16, count)) - first == lax.broadcasted_iota(I32, (16, count), 0)
    ).astype(F32).astype(BF16)
    for h in range(heads):
        lines_ref[h * halves : (h + 1) * halves, :] = table_ref[h]
    lines = lines_ref[...]
    lane = lax.broadcasted_iota(I32, (16, items), 1)
    owner = lax.broadcasted_iota(I32, (16, items), 0) == lane // per_item
    of_item = (
        lax.broadcasted_iota(I32, (per_item, items), 0) == lax.broadcasted_iota(I32, (per_item, items), 1) % per_item
    ).astype(F32).astype(BF16)
    high = dot(dot(mine, (lines // 128).astype(F32).astype(BF16), NT).astype(BF16), of_item)
    low = dot(dot(mine, (lines % 128).astype(F32).astype(BF16), NT).astype(BF16), of_item)
    slots = high * 128.0 + low
    row = jnp.sum(jnp.where(owner, slots, 0.0), axis=0, keepdims=True)
    diagonal = lax.broadcasted_iota(I32, (items, items), 0) == lax.broadcasted_iota(I32, (items, items), 1)
    column = jnp.sum(jnp.where(diagonal, row, 0.0), axis=1, keepdims=True)
    return jnp.sum((column < row).astype(F32), axis=0, keepdims=True).astype(I32)


def send_kernel(
    blocks, requests, per_peer,
    seq_hbm, read_hbm, state_hbm, edge_hbm,
    out_ref,
    seq_ref, read_ref, state_ref, edge_ref, scratch, edge_scratch, sems,
):
    slot_dev = state_ref.shape[0]
    pack = out_ref.shape[1]
    me = lax.axis_index("blk")
    sources = (seq_hbm, read_hbm, state_hbm, edge_hbm)
    targets = (seq_ref, read_ref, state_ref, edge_ref)
    copies = [pltpu.make_async_copy(a, b, sems.at[i]) for i, (a, b) in enumerate(zip(sources, targets))]
    for copy in copies:
        copy.start()
    copies[0].wait()
    copies[1].wait()
    position = positions(seq_ref, read_ref.shape[2])
    place = place_of_slot(read_ref, position, me * slot_dev, blocks, per_peer, requests, slot_dev)
    pick = (place == lax.broadcasted_iota(I32, (slot_dev, slot_dev), 0)).astype(F32).astype(BF16)
    left = lax.broadcasted_iota(I32, (slot_dev, 128), 1) < 64
    copies[3].wait()
    edge_rows = edge_ref.shape[0]
    edges = jnp.concatenate([edge_ref[...], jnp.zeros((slot_dev - edge_rows, slot_dev), F32)], axis=0)
    edge_scratch[...] = dot(pick, edges.astype(BF16), NT)
    half = pack // 2
    copies[2].wait()
    for b in range(half):
        x = dot(pick, state_ref[:, b * 128 : (b + 1) * 128].astype(BF16))
        y = dot(pick, state_ref[:, (half + b) * 128 : (half + b + 1) * 128].astype(BF16))
        scratch[:, 2 * b, :] = jnp.where(left, x, pltpu.roll(y, 64, 1))
        scratch[:, 2 * b + 1, :] = jnp.where(left, pltpu.roll(x, 64, 1), y)
    for b in range(blocks):
        at = b * (per_peer + 1)
        out_ref[at : at + per_peer] = scratch[b * per_peer : (b + 1) * per_peer].astype(BF16)
        block = edge_scratch[b * per_peer : (b + 1) * per_peer, :]
        if per_peer < pack:
            block = jnp.concatenate([block, jnp.zeros((pack - per_peer, 128), F32)], axis=0)
        out_ref[at + per_peer] = block.astype(BF16)


def early_kernel(blocks, requests, per_peer, lines, *refs):
    scalars_hbm, refs = refs[:2], refs[2:]
    tables_hbm, refs = refs[:2], refs[2:]
    vectors_hbm, refs = refs[:lines], refs[lines:]
    arrays_hbm, refs = refs[:5], refs[5:]
    index_ref, partial_ref, first_ref, picked_ref, vector_ref = refs[:5]
    arrays, refs = refs[5:9], refs[9:]
    seq_ref, count_ref, read_ref, write_ref, layer_ref, line_scratch, lines_ref, sems, line_sem, array_sem = refs
    pairs = list(zip((*scalars_hbm, *tables_hbm, arrays_hbm[0]), (seq_ref, count_ref, read_ref, write_ref, layer_ref)))
    copies = [pltpu.make_async_copy(a, b, sems.at[i]) for i, (a, b) in enumerate(pairs)]
    line_copies = [
        pltpu.make_async_copy(a, vector_ref.at[pl.ds(i, 1)], line_sem.at[i]) for i, a in enumerate(vectors_hbm)
    ]
    array_copies = [
        pltpu.make_async_copy(a, b, array_sem.at[i]) for i, (a, b) in enumerate(zip(arrays_hbm[1:], arrays))
    ]
    for copy in (*copies, *line_copies, *array_copies):
        copy.start()
    for copy in copies[:4]:
        copy.wait()
    slot_dev = index_ref.shape[1]
    me = lax.axis_index("blk")
    first = me * requests
    position = positions(seq_ref, read_ref.shape[2])
    place_in = place_of_item(read_ref, lines_ref, position, first, requests)
    place_out = place_of_item(write_ref, lines_ref, position, first, requests)
    target = place_of_slot(write_ref, position, me * slot_dev, blocks, per_peer, requests, slot_dev)
    lane = lax.broadcasted_iota(I32, (1, slot_dev), 1)
    counts = jnp.zeros((1, slot_dev), I32)
    for p in range(requests):
        counts = jnp.where(lane == p, count_ref[seq_ref[first + p]], counts)
    index_ref[0:1, :] = place_in
    index_ref[1:2, :] = place_out
    index_ref[2:3, :] = place_in + place_in // per_peer
    index_ref[3:4, :] = counts
    index_ref[4:5, :] = place_out + place_out // per_peer
    index_ref[5:6, :] = target
    index_ref[6:7, :] = target + target // per_peer
    index_ref[7:8, :] = jnp.zeros((1, slot_dev), I32)
    copies[4].wait()
    for copy in (*line_copies, *array_copies):
        copy.wait()
    steps = layer_ref.shape[0] // requests
    line = layer_ref[...].astype(F32)
    line_scratch[...] = line
    delta = pltpu.roll(line, 1, 0) - line
    left_decay_ref, left_rate_ref = arrays[:2]
    rank = left_decay_ref.shape[0]
    mixed_decay = (line + delta * vector_ref[0:1, :]).astype(BF16)
    mixed_rate = (line + delta * vector_ref[1:2, :]).astype(BF16)
    partial_ref[:, :rank] = dot(mixed_decay, left_decay_ref[...], NT).astype(BF16)
    partial_ref[:, rank:] = dot(mixed_rate, left_rate_ref[...], NT).astype(BF16)
    for p in range(requests):
        first_ref[p : p + 1, :] = line_scratch[p * steps : p * steps + 1, :]
        n = count_ref[seq_ref[first + p]]
        picked_ref[p : p + 1, :] = line_scratch[pl.ds(p * steps + jnp.maximum(n - 1, 0), 1), :]


def first_kernel(
    requests, heads, halves, per_peer,
    index_ref, got_ref, first_ref, vector_ref, left_decay_ref, left_rate_ref,
    out_ref, edge_ref, pool_scratch,
):
    slot_dev = pool_scratch.shape[0]
    rows = first_ref.shape[1] // (heads * halves)
    for b in range(slot_dev // per_peer):
        block = got_ref[b * (per_peer + 1) + per_peer].astype(F32)
        pool_scratch[b * per_peer : (b + 1) * per_peer, :] = block[:per_peer, :]
    for p in range(requests):
        for k in range(heads * halves):
            place = index_ref[0, p * heads * halves + k]
            edge_ref[p : p + 1, k * rows : (k + 1) * rows] = pool_scratch[pl.ds(place, 1), :rows]
    line = first_ref[...]
    delta = edge_ref[...] - line
    rank = left_decay_ref.shape[0]
    mixed_decay = (line + delta * vector_ref[0:1, :]).astype(BF16)
    mixed_rate = (line + delta * vector_ref[1:2, :]).astype(BF16)
    out_ref[:, :rank] = dot(mixed_decay, left_decay_ref[...], NT)
    out_ref[:, rank:] = dot(mixed_rate, left_rate_ref[...], NT)


def expand(x, head_width):
    steps, lanes = x.shape
    heads = lanes // head_width
    per_block = 128 // head_width
    lane = lax.broadcasted_iota(I32, (steps, 128), 1) // head_width
    zero = jnp.zeros((steps, 128), x.dtype)
    lines = []
    for h in range(heads):
        own = h // per_block
        block = jnp.where(lane == h % per_block, x[:, own * 128 : (own + 1) * 128], zero)
        lines.append(jnp.concatenate([block if b == own else zero for b in range(lanes // 128)], axis=1))
    return jnp.concatenate(lines, axis=0)


def ident_of(head_width, width):
    return (
        lax.broadcasted_iota(I32, (head_width, width), 0)
        == lax.broadcasted_iota(I32, (head_width, width), 1) % head_width
    ).astype(F32).astype(BF16)


def head_rows(line, heads, head_width, shift):
    shape = (2 * heads, line.shape[1])
    own = lax.broadcasted_iota(I32, shape, 1) // head_width + shift
    return jnp.where(own == lax.broadcasted_iota(I32, shape, 0), jnp.broadcast_to(line, shape), 0.0)


def prepare_kernel(
    requests, heads,
    index_ref, parts_ref, vector_ref, right_decay_ref, right_rate_ref, key_ref, value_ref,
    a_ref, k_ref, b_ref, scale_ref, key_mod_ref, last_ref, value_t_ref, solve_ref,
    unit_first_ref, key_first_ref, value_first_ref, through_ref, added_ref,
    cross, compact, unit_scratch, cum_ref,
):
    rows, width = key_ref.shape
    steps = rows // requests
    head_width = width // heads
    rank = right_decay_ref.shape[0]
    total = parts_ref[0].astype(F32)
    for g in range(1, parts_ref.shape[0]):
        total = total + parts_ref[g].astype(F32)
    hidden = jnp.tanh(total[:, :rank]).astype(BF16)
    rate_hidden = total[:, rank:].astype(BF16)
    decay = vector_ref[2:3, :] + dot(hidden, right_decay_ref[...])
    step = lax.broadcasted_iota(I32, (rows, width), 0) % steps
    later = step > 0
    log_forget = jnp.where(later, -DECAY_SCALE * jax.nn.sigmoid(decay), 0.0)
    rate = jax.nn.sigmoid(vector_ref[3:4, :] + dot(rate_hidden, right_rate_ref[...]))
    key = key_ref[...].astype(F32)
    u = key * vector_ref[4:5, :]
    unit = u * lax.rsqrt(group_sum(u * u, head_width) + EPSILON)
    unit_scratch[...] = unit
    key_mod = key * (1.0 + (rate - 1.0) * vector_ref[5:6, :])
    key_mod_ref[...] = key_mod.astype(BF16)
    cum = log_forget
    shift = 1
    while shift < steps:
        cum = cum + jnp.where(step >= shift, pltpu.roll(cum, shift, 0), 0.0)
        shift *= 2
    grow = jnp.where(later, jnp.exp(-cum), 0.0)
    cum_ref[...] = cum
    scale_ref[...] = jnp.exp(cum).astype(BF16)
    a_ref[...] = jnp.where(later, unit * jnp.exp(cum - log_forget), 0.0).astype(BF16)
    k_ref[...] = (key_mod * grow).astype(BF16)
    b_ref[...] = (rate * unit * grow).astype(BF16)
    ident = ident_of(head_width, width)
    lanes = heads * steps
    for p in range(requests):
        cut = slice(p * steps, (p + 1) * steps)
        n = index_ref[3, p]
        at_n = cum_ref[pl.ds(p * steps + jnp.maximum(n - 1, 0), 1), :]
        last_ref[p : p + 1, :] = jnp.where(n > 0, jnp.exp(at_n), 1.0)
        unit_first_ref[p : p + 1, :] = unit_scratch[p * steps : p * steps + 1, :]
        key_first_ref[p : p + 1, :] = key_ref[cut, :].astype(F32)[0:1, :]
        value_first_ref[p : p + 1, :] = value_ref[cut, :].astype(F32)[0:1, :]
        right = jnp.concatenate([expand(k_ref[cut, :], head_width), expand(b_ref[cut, :], head_width)], axis=0)
        cross[p] = dot(a_ref[cut, :], right, NT)
        value_t_ref[p] = dot(ident, expand(value_ref[cut, :], head_width), NT).astype(BF16)
    lane = lax.broadcasted_iota(I32, (requests, lanes), 1)
    source = lane % steps
    group = lane - source
    solve, carry = [], []
    for t in range(steps):
        weights = jnp.where(source < t, cross[:, t, lanes:], 0.0)
        solve_t = jnp.where(source == t, 1.0, 0.0)
        carry_t = jnp.where(source < t, cross[:, t, :lanes], 0.0)
        for s in range(t):
            weight = jnp.take_along_axis(weights, group + s, axis=1)
            solve_t = solve_t - weight * solve[s]
            carry_t = carry_t - weight * carry[s]
        solve.append(solve_t)
        carry.append(carry_t)
        compact[0, :, t, :] = solve_t
        compact[1, :, t, :] = carry_t
        solve_ref[0, t] = solve_t
        solve_ref[1, t] = carry_t
    for p in range(requests):
        cut = slice(p * steps, (p + 1) * steps)
        n = index_ref[3, p]
        a_t = dot(ident, expand(a_ref[cut, :], head_width), NT).astype(BF16)
        value_t = value_t_ref[p]
        reach = dot(a_t, spread(compact[0, p].astype(BF16), steps), NT)
        removed = dot(value_t, spread(compact[1, p].astype(BF16), steps), NT)
        left = jnp.concatenate(
            [
                jnp.concatenate([-reach, jnp.zeros_like(reach)], axis=1),
                jnp.concatenate([-removed, value_t.astype(F32)], axis=1),
            ],
            axis=0,
        )
        at = lax.broadcasted_iota(I32, left.shape, 1) % steps
        left = jnp.where(at < n, left, 0.0).astype(BF16)
        right = jnp.concatenate([expand(b_ref[cut, :], head_width), expand(k_ref[cut, :], head_width)], axis=0)
        both = dot(left, right) * last_ref[p : p + 1, :]
        added_ref[p] = both[head_width:, :].astype(BF16)
        through_ref[p] = both[:head_width, :].astype(BF16)


def spread(x, steps):
    lanes = x.shape[1]
    group = lax.broadcasted_iota(I32, x.shape, 1) // steps
    zero = jnp.zeros_like(x)
    return jnp.concatenate([jnp.where(group == h, x, zero) for h in range(lanes // steps)], axis=0)


def layout_kernel(
    requests, heads, halves, per_peer,
    index_ref, got_ref, unit_first_ref, value_first_ref, edge_ref, picked_ref,
    state_ref, change_ref, edge_out_ref, edge_scratch,
):
    width = unit_first_ref.shape[1]
    head_width = width // heads
    pack = got_ref.shape[1]
    edge_rows = head_width // halves
    ident = ident_of(head_width, width)
    low = lax.broadcasted_iota(I32, (pack, 128), 1) < head_width
    for p in range(requests):
        for c in range(halves):
            for pair in range(heads // 2):
                at = (p * heads + 2 * pair) * halves + c
                even = got_ref[index_ref[2, at]].astype(F32)
                odd = got_ref[index_ref[2, at + halves]].astype(F32)
                top = jnp.where(low, even, pltpu.roll(odd, head_width, 1))
                bottom = jnp.where(low, pltpu.roll(even, head_width, 1), odd)
                lanes = slice(pair * 128, (pair + 1) * 128)
                state_ref[p, 2 * c * pack : (2 * c + 1) * pack, lanes] = top.astype(BF16)
                state_ref[p, (2 * c + 1) * pack : (2 * c + 2) * pack, lanes] = bottom.astype(BF16)
        unit = head_rows(unit_first_ref[p : p + 1, :], heads, head_width, 0).astype(BF16)
        value = head_rows(value_first_ref[p : p + 1, :], heads, head_width, heads).astype(BF16)
        change_ref[p] = (dot(ident, value, NT) - dot(state_ref[p], unit, NT)).astype(BF16)
        new_edge = jnp.where(index_ref[3, p] > 0, picked_ref[p : p + 1, :], edge_ref[p : p + 1, :])
        for k in range(heads * halves):
            lane = k * edge_rows
            line = new_edge[:, lane // 128 * 128 : lane // 128 * 128 + 128]
            if lane % 128:
                line = pltpu.roll(line, 128 - lane % 128, 1)
            edge_scratch[pl.ds(index_ref[1, p * heads * halves + k], 1), :] = line
    for b in range(edge_out_ref.shape[0]):
        block = edge_scratch[b * per_peer : (b + 1) * per_peer, :]
        if per_peer < pack:
            block = jnp.concatenate([block, jnp.zeros((pack - per_peer, 128), F32)], axis=0)
        edge_out_ref[b] = block.astype(BF16)


def state_kernel(
    requests, heads, halves, per_peer, groups,
    index_ref, *refs,
):
    parts_refs = refs[:groups]
    (
        state_ref, change_ref, edge_blocks_ref, unit_first_ref, key_first_ref, last_ref, through_ref, added_ref,
        vector_ref, right_decay_ref, right_rate_ref,
        send_ref, after_ref, key_mod_first_ref,
    ) = refs[groups:]
    width = unit_first_ref.shape[1]
    head_width = width // heads
    pack = send_ref.shape[1]
    rank = right_decay_ref.shape[0]
    total = parts_refs[0][...]
    for ref in parts_refs[1:]:
        total = total + ref[...]
    decay = vector_ref[2:3, :] + dot(jnp.tanh(total[:, :rank]).astype(BF16), right_decay_ref[...])
    forget = jnp.exp(-DECAY_SCALE * jax.nn.sigmoid(decay))
    rate = jax.nn.sigmoid(vector_ref[3:4, :] + dot(total[:, rank:].astype(BF16), right_rate_ref[...]))
    key_mod = key_first_ref[...] * (1.0 + (rate - 1.0) * vector_ref[5:6, :])
    key_mod_first_ref[...] = key_mod
    removal = rate * unit_first_ref[...]
    low = lax.broadcasted_iota(I32, (pack, 128), 1) < head_width
    own = lax.broadcasted_iota(I32, (head_width, 128), 1) < head_width
    for b in range(edge_blocks_ref.shape[0]):
        send_ref[b * (per_peer + 1) + per_peer] = edge_blocks_ref[b]
    for p in range(requests):
        n = index_ref[3, p]
        line = slice(p, p + 1)
        written = head_rows(removal[line, :], heads, head_width, 0) + head_rows(key_mod[line, :], heads, head_width, heads)
        start = state_ref[p].astype(F32)
        change = dot(change_ref[p], written.astype(BF16))
        after = start * forget[line, :] + change
        after_b = after.astype(BF16)
        after_ref[p] = after_b
        parts = []
        for pair in range(heads // 2):
            lanes = slice(pair * 128, (pair + 1) * 128)
            through = through_ref[p, :, lanes]
            zero = jnp.zeros_like(through)
            through = jnp.concatenate([jnp.where(own, through, zero), jnp.where(own, zero, through)], axis=0)
            parts.append(dot(after_b[:, lanes], through))
        kept = after * last_ref[line, :] + jnp.concatenate(parts, axis=1) + added_ref[p].astype(F32)
        kept = jnp.where(n > 0, kept, start)
        for c in range(halves):
            for pair in range(heads // 2):
                top = kept[(2 * c) * pack : (2 * c + 1) * pack, pair * 128 : (pair + 1) * 128]
                bottom = kept[(2 * c + 1) * pack : (2 * c + 2) * pack, pair * 128 : (pair + 1) * 128]
                at = (p * heads + 2 * pair) * halves + c
                even = jnp.where(low, top, pltpu.roll(bottom, head_width, 1))
                odd = jnp.where(low, pltpu.roll(top, head_width, 1), bottom)
                send_ref[index_ref[4, at]] = even.astype(BF16)
                send_ref[index_ref[4, at + halves]] = odd.astype(BF16)


def lines_kernel(gating_ref, *refs):
    *outs, scratch = refs
    requests, part = gating_ref.shape[:2]
    width = scratch.shape[1]
    me = lax.axis_index("head")
    for d, out in enumerate(outs):
        start = pl.multiple_of((me ^ d) * width, 128)
        for p in range(requests):
            scratch[p * part : (p + 1) * part, :] = gating_ref[p, :, pl.ds(start, width)].astype(F32)
        out[...] = scratch[...].astype(BF16)


def read_kernel(
    requests, heads, groups,
    *refs,
):
    return read_body(requests, heads, refs[:groups], *refs[groups:])


def read_body(
    requests, heads,
    recept_refs, scale_ref, key_mod_ref, key_mod_first_ref, a_ref, k_ref, b_ref, solve_ref, state_ref, value_t_ref,
    vector_ref, value_ref,
    result_ref, line_scratch, cross, compact, out_scratch,
):
    rows, width = value_ref.shape
    steps = rows // requests
    head_width = width // heads
    lanes = heads * steps
    part = steps // len(recept_refs)
    row = lax.broadcasted_iota(I32, (rows, rows), 0)
    source = (row % steps // part) ^ lax.axis_index("head")
    source_row = source * (requests * part) + row // steps * part + row % part
    order = (source_row == lax.broadcasted_iota(I32, (rows, rows), 1)).astype(F32).astype(BF16)
    recept = dot(order, jnp.concatenate([ref[...] for ref in recept_refs], axis=0))
    key_mod_first = jnp.broadcast_to(key_mod_first_ref[...][:, None, :], (requests, steps, width)).reshape(rows, width)
    first = lax.broadcasted_iota(I32, (rows, width), 0) % steps == 0
    key_mod = jnp.where(first, key_mod_first, key_mod_ref[...].astype(F32))
    bonus = group_sum(recept * key_mod * vector_ref[6:7, :], head_width)
    line_scratch[...] = (recept * scale_ref[...].astype(F32)).astype(BF16)
    for p in range(requests):
        cut = slice(p * steps, (p + 1) * steps)
        right = jnp.concatenate([expand(k_ref[cut, :], head_width), expand(b_ref[cut, :], head_width)], axis=0)
        cross[p] = dot(line_scratch[cut, :], right, NT)
    lane = lax.broadcasted_iota(I32, (requests, lanes), 1)
    source = lane % steps
    group = lane - source
    for t in range(steps):
        weights = jnp.where(source <= t, cross[:, t, lanes:], 0.0)
        from_a = jnp.zeros((requests, lanes), F32)
        from_v = jnp.where(source <= t, cross[:, t, :lanes], 0.0)
        for s in range(t + 1):
            weight = jnp.take_along_axis(weights, group + s, axis=1)
            from_a = from_a - weight * solve_ref[0, s]
            from_v = from_v - weight * solve_ref[1, s]
        compact[0, :, t, :] = from_a
        compact[1, :, t, :] = from_v
    out_low = lax.broadcasted_iota(I32, (steps, 128), 1) < head_width
    for p in range(requests):
        cut = slice(p * steps, (p + 1) * steps)
        read = jnp.concatenate(
            [spread(compact[0, p].astype(BF16), steps), spread(compact[1, p].astype(BF16), steps)], axis=1
        )
        state = state_ref[p]
        along = dot(state, expand(a_ref[cut, :], head_width), NT).astype(BF16)
        both = jnp.concatenate([along, value_t_ref[p]], axis=1)
        out = dot(read, jnp.concatenate([both, both], axis=0), NT)
        out = out + dot(expand(line_scratch[cut, :], head_width), jnp.concatenate([state, state], axis=0), NT)
        for pair in range(heads // 2):
            at = 2 * pair * steps
            out_scratch[cut, pair * 128 : (pair + 1) * 128] = jnp.where(
                out_low, out[at : at + steps, :], out[at + steps : at + 2 * steps, :]
            )
    out = out_scratch[...]
    centered = out - group_sum(out, head_width) * (1.0 / head_width)
    variance = group_sum(centered * centered, head_width) * (1.0 / head_width)
    line = centered * lax.rsqrt(variance + NORM_EPSILON) * vector_ref[7:8, :] + vector_ref[8:9, :]
    result_ref[...] = (line + bonus * value_ref[...].astype(F32)).astype(BF16)


def place_kernel(per_peer, index_ref, back_ref, out_ref, edge_ref, scratch, edge_scratch, edge_placed):
    slot_dev = out_ref.shape[0]
    pack = back_ref.shape[1]
    for b in range(slot_dev // per_peer):
        block = back_ref[b * (per_peer + 1) + per_peer].astype(F32)
        edge_scratch[b * per_peer : (b + 1) * per_peer, :] = block[:per_peer, :]
    for s in range(slot_dev):
        scratch[s] = back_ref[index_ref[6, s]].astype(F32)
        edge_placed[s : s + 1, :] = edge_scratch[pl.ds(index_ref[5, s], 1), :]
    left = lax.broadcasted_iota(I32, (slot_dev, 128), 1) < 64
    half = pack // 2
    for b in range(half):
        even = scratch[:, 2 * b, :]
        odd = scratch[:, 2 * b + 1, :]
        out_ref[:, b * 128 : (b + 1) * 128] = jnp.where(left, even, pltpu.roll(odd, 64, 1))
        out_ref[:, (half + b) * 128 : (half + b + 1) * 128] = jnp.where(left, pltpu.roll(even, 64, 1), odd)
    edge_ref[...] = jnp.transpose(edge_placed[...])[: edge_ref.shape[0], :]


def local(
    layer_entry_vectors,
    guessed_lookup_vectors,
    guessed_content_vectors,
    gating_query,
    lane_memory_store,
    prior_step_store,
    fading_blend_ratio,
    learning_speed_blend,
    fading_left_factor,
    fading_right_factor,
    fading_offset,
    learning_speed_left,
    learning_speed_right,
    learning_speed_offset,
    erasing_lookup_factor,
    written_lookup_factor,
    present_reward_factors,
    lane_standard_factor,
    lane_standard_offset,
    caller_memory_directory,
    kept_target_place,
    caller_sequence,
    approved_guesses,
):
    blocks = lax.axis_size("blk")
    groups = lax.axis_size("head")
    requests, steps, width = layer_entry_vectors.shape
    heads, halves = caller_memory_directory.shape[1:]
    slot_dev = lane_memory_store.shape[1]
    slot_width = lane_memory_store.shape[2]
    pack = slot_width // 128
    per_peer = slot_dev // blocks
    edge_rows = prior_step_store.shape[2]
    rows = requests * steps
    rank = fading_left_factor.shape[1]
    sds = jax.ShapeDtypeStruct

    def exchange(x, axis):
        return lax.all_to_all(x, axis, split_axis=0, concat_axis=0, tiled=True)

    read_table = caller_memory_directory.transpose(1, 2, 0)
    write_table = kept_target_place.transpose(1, 2, 0)
    sent = call(
        functools.partial(send_kernel, blocks, requests, per_peer),
        pltpu.HBM((blocks * (per_peer + 1), pack, 128), BF16),
        raw=(caller_sequence, read_table, lane_memory_store[0], prior_step_store[0].T),
        scratch=[
            pltpu.SMEM(caller_sequence.shape, I32),
            pltpu.VMEM(read_table.shape, I32),
            pltpu.VMEM((slot_dev, slot_width), F32),
            pltpu.VMEM((edge_rows, slot_dev), F32),
            pltpu.VMEM((slot_dev, pack, 128), F32),
            pltpu.VMEM((slot_dev, slot_dev), F32),
            pltpu.SemaphoreType.DMA((4,)),
        ],
    )
    got = exchange(sent.reshape(blocks, (per_peer + 1) * pack, 128), "blk")
    got = got.reshape(blocks * (per_peer + 1), pack, 128)
    layer = layer_entry_vectors.reshape(rows, width)
    key = guessed_lookup_vectors.reshape(rows, width)
    value = guessed_content_vectors.reshape(rows, width)
    vectors = (
        fading_blend_ratio, learning_speed_blend, fading_offset, learning_speed_offset, erasing_lookup_factor,
        written_lookup_factor, present_reward_factors, lane_standard_factor, lane_standard_offset,
    )
    arrays = (fading_left_factor.T, learning_speed_left.T, fading_right_factor, learning_speed_right)
    one = sds((requests, width), F32)
    wide = sds((rows, width), BF16)
    left = sds((rank, width), BF16)
    (
        index, partial_sums, first_lines, picked, vector,
        left_decay, left_rate, right_decay, right_rate,
    ) = call(
        functools.partial(early_kernel, blocks, requests, per_peer, len(vectors)),
        (
            sds((8, slot_dev), I32), sds((rows, 2 * rank), BF16), one, one,
            sds((16, width), F32), left, left, left, left,
        ),
        raw=(
            caller_sequence, approved_guesses, read_table, write_table,
            *(x.reshape(1, width) for x in vectors), layer, *arrays,
        ),
        scratch=[
            pltpu.SMEM(caller_sequence.shape, I32),
            pltpu.SMEM(approved_guesses.shape, I32),
            pltpu.VMEM(read_table.shape, I32),
            pltpu.VMEM(write_table.shape, I32),
            pltpu.VMEM((rows, width), BF16),
            pltpu.VMEM((rows, width), F32),
            pltpu.VMEM((heads * halves, write_table.shape[2]), I32),
            pltpu.SemaphoreType.DMA((5,)),
            pltpu.SemaphoreType.DMA((len(vectors),)),
            pltpu.SemaphoreType.DMA((len(arrays),)),
        ],
    )
    parts = lax.all_gather(partial_sums, "head", axis=0)

    head_width = width // heads
    (
        a_lines, k_lines, b_lines, scale, key_mod, last, value_t, solve,
        unit_first, key_first, value_first, through, added,
    ) = call(
        functools.partial(prepare_kernel, requests, heads),
        (
            wide, wide, wide, wide, wide, one,
            sds((requests, head_width, heads * steps), BF16),
            sds((2, steps, requests, heads * steps), F32),
            one, one, one,
            sds((requests, head_width, width), BF16),
            sds((requests, head_width, width), BF16),
        ),
        scalars=(index,),
        near=(parts, vector, right_decay, right_rate),
        far=(key, value),
        held=(first_lines, picked, left_decay, left_rate),
        scratch=[
            pltpu.VMEM((requests, steps, 2 * heads * steps), F32),
            pltpu.VMEM((2, requests, steps, heads * steps), F32),
            pltpu.VMEM((rows, width), F32),
            pltpu.VMEM((rows, width), F32),
        ],
    )
    read_later = (scale, key_mod, a_lines, k_lines, b_lines, solve, value_t)
    state_later = (vector, right_decay, right_rate, key_first, last, through, added)
    first_sums, edge = call(
        functools.partial(first_kernel, requests, heads, halves, per_peer),
        (sds((requests, 2 * rank), F32), one),
        scalars=(index,),
        near=(got, first_lines, vector, left_decay, left_rate),
        held=(unit_first, value_first, picked, *state_later[1:], *read_later),
        scratch=[pltpu.VMEM((slot_dev, 128), F32)],
    )
    first_parts = [first_sums] + [
        lax.ppermute(first_sums, "head", [(g, g ^ d) for g in range(groups)]) for d in range(1, groups)
    ]
    state, change, edge_blocks = call(
        functools.partial(layout_kernel, requests, heads, halves, per_peer),
        (
            sds((requests, head_width, width), BF16),
            sds((requests, head_width, 2 * heads), BF16),
            sds((blocks, pack, 128), BF16),
        ),
        scalars=(index,),
        near=(got, unit_first, value_first, edge, picked),
        held=(*state_later, *read_later),
        scratch=[pltpu.VMEM((slot_dev, 128), F32)],
    )
    back, after, key_mod_first = call(
        functools.partial(state_kernel, requests, heads, halves, per_peer, groups),
        (
            pltpu.HBM((blocks * (per_peer + 1), pack, 128), BF16),
            sds((requests, head_width, width), BF16),
            one,
        ),
        scalars=(index,),
        near=(
            *first_parts, state, change, edge_blocks, unit_first, key_first, last, through, added,
            vector, right_decay, right_rate,
        ),
        held=read_later,
    )
    back = exchange(back.reshape(blocks, (per_peer + 1) * pack, 128), "blk")
    back = back.reshape(blocks * (per_peer + 1), pack, 128)
    recept = call(
        lines_kernel,
        (sds((rows // groups, width), BF16),) * groups,
        far=(gating_query,),
        held=(index, vector, after, key_mod_first, *read_later),
        scratch=[pltpu.VMEM((rows // groups, width), F32)],
    )
    recept = [recept[0]] + [
        lax.ppermute(recept[d], "head", [(g, g ^ d) for g in range(groups)]) for d in range(1, groups)
    ]
    result = call(
        functools.partial(read_kernel, requests, heads, groups),
        pltpu.HBM((rows, width), BF16),
        near=(*recept, scale, key_mod, key_mod_first, a_lines, k_lines, b_lines, solve, after, value_t, vector),
        far=(value,),
        held=(index,),
        scratch=[
            pltpu.VMEM((rows, width), BF16),
            pltpu.VMEM((requests, steps, 2 * heads * steps), F32),
            pltpu.VMEM((2, requests, steps, heads * steps), F32),
            pltpu.VMEM((rows, width), F32),
        ],
    )
    new_states, new_edges = call(
        functools.partial(place_kernel, per_peer),
        (pltpu.HBM((slot_dev, slot_width), F32), pltpu.HBM((edge_rows, slot_dev), F32)),
        scalars=(index,),
        near=(back,),
        scratch=[
            pltpu.VMEM((slot_dev, pack, 128), F32),
            pltpu.VMEM((slot_dev, 128), F32),
            pltpu.VMEM((slot_dev, 128), F32),
        ],
    )
    return (result.reshape(requests, steps, width), new_states[None], new_edges.T[None])


def solution(mesh):
    return jax.shard_map(
        local,
        mesh=mesh,
        in_specs=(
            P("blk", None, "head"),
            P("blk", None, "head"),
            P("blk", None, "head"),
            P("blk", "head", None),
            P("head", "blk", None),
            P("head", "blk", None),
            P("head"),
            P("head"),
            P("head", None),
            P(None, "head"),
            P("head"),
            P("head", None),
            P(None, "head"),
            P("head"),
            P("head"),
            P("head"),
            P("head"),
            P("head"),
            P("head"),
            P(None, "head", None),
            P(None, "head", None),
            P(),
            P(),
        ),
        out_specs=(P("blk", None, "head"), P("head", "blk", None), P("head", "blk", None)),
        check_vma=False,
    )
```

time: 62.2 us -> 56.4 us (0.907)
  local copies, waits for them, and re-layouts: 5.29 us -> 0 us
  Pallas kernels: 18.7 us -> 22.8 us
  waiting for transfers between devices: 13.4 us -> 10.7 us
  starting transfers between devices: 17.5 us -> 16.1 us
    pallas_call x8 -> x9, Pallas kernels: 18.7 us -> 22.8 us  [call(): pl.pallas_call(body, out_shape=outs, in_specs=specs, out_specs=jax.tree.m...]
    unnamed x44 -> x0, local copies, waits for them, and re-layouts: 3.91 us -> none
    all_to_all x3 -> x2, waiting for transfers between devices: 11.3 us -> 7.55 us  [exchange(): return lax.all_to_all(x, axis, split_axis=0, concat_axis=0, tiled=True)]
    all_to_all x3 -> x2, starting transfers between devices: 15.5 us -> 12.3 us  [exchange(): return lax.all_to_all(x, axis, split_axis=0, concat_axis=0, tiled=True)]
    ppermute x0 -> x3, starting transfers between devices: none -> 1.86 us  [local(): lax.ppermute(first_sums, 'head', [(g, g ^ d) for g in range(groups)])]
    broadcast_in_dim x1 -> x0, local copies, waits for them, and re-layouts: 1.38 us -> none  [local(): jnp.broadcast_to(prior_step_store[0].T, (blocks, edge_rows, slot_dev))]
    ppermute x0 -> x3, waiting for transfers between devices: none -> 0.68 us  [local(): lax.ppermute(first_sums, 'head', [(g, g ^ d) for g in range(groups)])]
  transfers between devices with their start and end apart: 6 -> 8, of which waited for: 5 -> 5; matrix products, arithmetic and copies ran while one was open for 0% -> 0% of each run, Pallas kernels for 19% -> 24%
where the time goes in v2:
time: 56.4 us; the launch traced here: 56 us
  Pallas kernels  22.8 us (40%)
  starting transfers between devices  16.1 us (29%)
  waiting for transfers between devices  10.7 us (19%)
  blocking collectives  5.79 us (10%)
  between operations  0.68 us (1%)
    pallas_call x9, Pallas kernels, call(): pl.pallas_call(body, out_shape=outs, in_specs=specs, out_specs=jax.tree.m...  22.8 us
    all_to_all x2, starting transfers between devices, exchange(): return lax.all_to_all(x, axis, split_axis=0, concat_axis=0, tiled=True)  12.3 us
    all_to_all x2, waiting for transfers between devices, exchange(): return lax.all_to_all(x, axis, split_axis=0, concat_axis=0, tiled=True)  7.55 us
    all_gather x1, blocking collectives, local(): parts = lax.all_gather(partial_sums, 'head', axis=0)  5.79 us
    ppermute x3, waiting for transfers between devices, local(): lax.ppermute(recept[d], 'head', [(g, g ^ d) for g in range(groups)])  2.42 us
    ppermute x3, starting transfers between devices, local(): lax.ppermute(recept[d], 'head', [(g, g ^ d) for g in range(groups)])  1.93 us
    ppermute x3, starting transfers between devices, local(): lax.ppermute(first_sums, 'head', [(g, g ^ d) for g in range(groups)])  1.86 us
  transfers between devices with their start and end apart: 8, of which 5 were waited for; matrix products, arithmetic and copies ran while one was open for 0% of the time, Pallas kernels for 24%

profile of v2, /device:TPU:0, one launch (start us, length us, event | category | flops | bytes accessed | tf_op | source)
XLA Modules:
  0.0 56.0 jit_solution(2690134090138836356)
XLA Ops:
  0.6 3.1 %shard_map.239 = bf16[136,16,128]{2,1,0:T(8,128)(2,1)} custom-call(s32[64]{0:T(128)} %refs_0_.4, s32[8,2,64]{2,1,0:T(2,128)} %bitcast.44, f32[128,2048]{1,0:T(8,128)} %bitcast.35, f32[32,128]{1,0:T(8,128)} %bitcast.46), custom_call_target="tpu_custom_call" | custom-call | flops 1048576 | bytes 1048576 | tf_op jit(solution)/shard_map/pallas_call | solution.py:32
  3.8 7.3 %all-to-all-start = ((bf16[8,272,128]{2,1,0:T(8,128)(2,1)}), bf16[8,272,128]{2,1,0:T(8,128)(2,1)S(1)}, u32[]{:S(2)}, u32[]{:S(2)}) async-start(bf16[8,272,128]{2,1,0:T(8,128)(2,1)} %bitcast.34), calls=%async_computation | async-start | bytes 1114112 | tf_op jit(solution)/shard_map/all_to_all | solution.py:601
  11.1 2.0 %shard_map.238 = (s32[8,128]{1,0:T(8,128)S(1)}, bf16[128,192]{1,0:T(8,128)(2,1)S(1)}, f32[8,512]{1,0:T(8,128)S(1)}, f32[8,512]{1,0:T(8,128)S(1)}, f32[16,512]{1,...) custom-call(s32[64]{0:T(128)} %refs_0_.4, ...), custom_call_target="tpu_custom_call" | custom-call | flops 1048576 | bytes 1048576 | tf_op jit(solution)/shard_map/pallas_call | solution.py:32
  13.1 5.8 %all-gather = bf16[512,192]{1,0:T(8,128)(2,1)S(1)} all-gather(bf16[128,192]{1,0:T(8,128)(2,1)S(1)} %get-tuple-element.44), channel_id=2, replica_groups=mesh['blk'=8,'head'=4] {'head'}, dimensions={0}, use_global_device_ids=true | all-gather | bytes 245760 | tf_op jit(solution)/shard_map/all_gather | solution.py:658
  18.9 4.9 %shard_map.240 = (bf16[128,512]{1,0:T(8,128)(2,1)S(1)}, bf16[128,512]{1,0:T(8,128)(2,1)S(1)}, bf16[128,512]{1,0:T(8,128)(2,1)S(1)}, bf16[128,512]{1,0:T(8,128)(2...) custom-call(s32[8,128]{1,0:T(8,128)S(1)} %get-tuple-element.39.refs_, ...), custom_call_target="tpu_custom_call" | custom-call | flops 1048576 | bytes 1048576 | tf_op jit(solution)/shard_map/pallas_call | solution.py:32
  23.8 2.4 %all-to-all-done = bf16[8,272,128]{2,1,0:T(8,128)(2,1)S(1)} async-done(((bf16[8,272,128]{2,1,0:T(8,128)(2,1)}), bf16[8,272,128]{2,1,0:T(8,128)(2,1)S(1)}, u32[]{:S(2)}, u32[]{:S(2)}) %all-to-all-start) | async-done | bytes 557088 | tf_op jit(solution)/shard_map/all_to_all | solution.py:601
  26.2 1.0 %shard_map.241 = (f32[8,192]{1,0:T(8,128)S(1)}, f32[8,512]{1,0:T(8,128)S(1)}) custom-call(s32[8,128]{1,0:T(8,128)S(1)} %get-tuple-element.39.refs_0_.refs_1_.refs_15_, bf16[136,16,128]{2,1,0:T(8,128)(2,1)S(1)} %bitcast.30, f32[8,512]{1,0:T(8,128)S(1)} %get-tuple-element.41.refs_7_.refs_2_, f32[16,512]{1,0:T(8,128)S(1)} %get-tuple-element.40.refs_2_.refs_3_.refs_6_.refs_13_, ...), custom_call_target="tpu_custom_call" | custom-call | flops 1048576 | bytes 1048576 | tf_op jit(solution)/shard_map/pallas_call | solution.py:32
  27.2 0.0 collective-permute-start.2
  27.2 1.5 %collective-permute-start.1 = (f32[8,192]{1,0:T(8,128)S(1)}, f32[8,192]{1,0:T(8,128)S(1)}, u32[]{:S(2)}, u32[]{:S(2)}) collective-permute-start(f32[8,192]{1,0:T(8,128)S(1)} %get-tuple-element.61.refs_1_), channel_id=1, source_target_pairs={{0,2},{1,3},{2,0},{3,1},{4,6},{5,7},{6,4},{7,5},{8,10},{9,11},{10,... | collective-permute-start | bytes 18440 | tf_op jit(solution)/shard_map/ppermute | solution.py:696
  28.7 0.3 collective-permute-start
  29.1 1.1 %shard_map.242 = (bf16[8,64,512]{2,1,0:T(8,128)(2,1)S(1)}, bf16[8,64,16]{2,1,0:T(8,128)(2,1)S(1)}, bf16[8,16,128]{2,1,0:T(8,128)(2,1)S(1)}) custom-call(s32[8,128]{1,0:T(8,128)S(1)} %get-tuple-element.39.refs_0_.refs_1_.refs_15_, bf16[136,16,128]{2,1,0:T(8,128)(2,1)S(1)} %bitcast.31, f32[8,512]{1,0:T(8,128)S(1)} %get-tuple-element.48.refs_6_.refs_2_.refs_8_, ...), custom_call_target="tpu_custom_call" | custom-call | flops 1048576 | bytes 1048576 | tf_op jit(solution)/shard_map/pallas_call | solution.py:32
  30.2 0.1 collective-permute-done.2.refs_4_
  30.3 0.6 %collective-permute-done.1.refs_3_ = f32[8,192]{1,0:T(8,128)S(1)} collective-permute-done((f32[8,192]{1,0:T(8,128)S(1)}, f32[8,192]{1,0:T(8,128)S(1)}, u32[]{:S(2)}, u32[]{:S(2)}) %collective-permute-start.1) | collective-permute-done | bytes 6176 | tf_op jit(solution)/shard_map/ppermute | solution.py:696
  30.9 0.0 collective-permute-done.refs_2_
  30.9 3.1 %shard_map.243 = (bf16[136,16,128]{2,1,0:T(8,128)(2,1)}, bf16[8,64,512]{2,1,0:T(8,128)(2,1)S(1)}, f32[8,512]{1,0:T(8,128)S(1)}) custom-call(s32[8,128]{1,0:T(8,128)S(1)} %get-tuple-element.39.refs_0_.refs_1_.refs_15_, f32[8,192]{1,0:T(8,128)S(1)} %get-tuple-element.61.refs_1_, f32[8,192]{1,0:T(8,128)S(1)} %collective-permute-done.refs_2_, ...), custom_call_target="tpu_custom_call" | custom-call | flops 1048576 | bytes 1048576 | tf_op jit(solution)/shard_map/pallas_call | solution.py:32
  34.0 5.0 %all-to-all-start.1 = ((bf16[8,272,128]{2,1,0:T(8,128)(2,1)}), bf16[8,272,128]{2,1,0:T(8,128)(2,1)S(1)}, u32[]{:S(2)}, u32[]{:S(2)}) async-start(bf16[8,272,128]{2,1,0:T(8,128)(2,1)} %bitcast.36), calls=%async_computation.1 | async-start | bytes 1114112 | tf_op jit(solution)/shard_map/all_to_all | solution.py:601
  39.0 1.0 %shard_map.244 = (bf16[32,512]{1,0:T(8,128)(2,1)S(1)}, bf16[32,512]{1,0:T(8,128)(2,1)S(1)}, bf16[32,512]{1,0:T(8,128)(2,1)S(1)}, bf16[32,512]{1,0:T(8,128)(2,1)S(1)}) custom-call(bf16[8,4,2048]{2,1,0:T(4,128)(2,1)} %refs_0_.5, s32[8,128]{1,0:T(8,128)S(1)} %get-tuple-element.39.refs_0_.refs_1_.refs_15_, ...), custom_call_target="tpu_custom_call" | custom-call | flops 1048576 | bytes 1048576 | tf_op jit(solution)/shard_map/pallas_call | solution.py:32
  39.9 0.1 collective-permute-start.3
  40.0 0.6 %collective-permute-start.4 = (bf16[32,512]{1,0:T(8,128)(2,1)S(1)}, bf16[32,512]{1,0:T(8,128)(2,1)S(1)}, u32[]{:S(2)}, u32[]{:S(2)}) collective-permute-start(bf16[32,512]{1,0:T(8,128)(2,1)S(1)} %get-tuple-element.70), channel_id=1, source_target_pairs={{0,2},{1,3},{2,0},{3,1},{4,6},{5,7},{6,4},{7,5},{8,10},{9,11},{10,... | collective-permute-start | bytes 98312 | tf_op jit(solution)/shard_map/ppermute | solution.py:734
  40.6 1.3 %collective-permute-start.5 = (bf16[32,512]{1,0:T(8,128)(2,1)S(1)}, bf16[32,512]{1,0:T(8,128)(2,1)S(1)}, u32[]{:S(2)}, u32[]{:S(2)}) collective-permute-start(bf16[32,512]{1,0:T(8,128)(2,1)S(1)} %get-tuple-element.71), channel_id=1, source_target_pairs={{0,3},{1,2},{2,1},{3,0},{4,7},{5,6},{6,5},{7,4},{8,11},{9,10},{10,... | collective-permute-start | bytes 98312 | tf_op jit(solution)/shard_map/ppermute | solution.py:734
  41.9 0.0 collective-permute-done.3.refs_1_
  41.9 2.4 %collective-permute-done.4.refs_2_ = bf16[32,512]{1,0:T(8,128)(2,1)S(1)} collective-permute-done((bf16[32,512]{1,0:T(8,128)(2,1)S(1)}, bf16[32,512]{1,0:T(8,128)(2,1)S(1)}, u32[]{:S(2)}, u32[]{:S(2)}) %collective-permute-start.4) | collective-permute-done | bytes 32800 | tf_op jit(solution)/shard_map/ppermute | solution.py:734
  44.3 0.0 collective-permute-done.5.refs_3_
  44.3 4.1 %shard_map.245 = bf16[128,512]{1,0:T(8,128)(2,1)} custom-call(bf16[32,512]{1,0:T(8,128)(2,1)S(1)} %get-tuple-element.68.refs_0_, bf16[32,512]{1,0:T(8,128)(2,1)S(1)} %collective-permute-done.3.refs_1_, bf16[32,512]{1,0:T(8,128)(2,1)S(1)} %collective-permute-done.4.refs_2_, bf16[32,512]{1,0:T(8,128)(2,1)S(1)} %collective-permute-done.5.refs_3_, ...), custom_call_target="tpu_custom_call" | custom-call | flops 1048576 | bytes 1048576 | tf_op jit(solution)/shard_map/pallas_call | solution.py:32
  48.5 5.1 %all-to-all-done.1 = bf16[8,272,128]{2,1,0:T(8,128)(2,1)S(1)} async-done(((bf16[8,272,128]{2,1,0:T(8,128)(2,1)}), bf16[8,272,128]{2,1,0:T(8,128)(2,1)S(1)}, u32[]{:S(2)}, u32[]{:S(2)}) %all-to-all-start.1) | async-done | bytes 557088 | tf_op jit(solution)/shard_map/all_to_all | solution.py:601
  53.6 2.4 %shard_map.246 = (f32[128,2048]{1,0:T(8,128)}, f32[32,128]{1,0:T(8,128)}) custom-call(s32[8,128]{1,0:T(8,128)S(1)} %get-tuple-element.39.refs_0_.refs_1_.refs_15_, bf16[136,16,128]{2,1,0:T(8,128)(2,1)S(1)} %bitcast.32), custom_call_target="tpu_custom_call" | custom-call | flops 1048576 | bytes 1048576 | tf_op jit(solution)/shard_map/pallas_call | solution.py:32
Async XLA Ops:
  3.8 22.5 %all-to-all-start = ((bf16[8,272,128]{2,1,0:T(8,128)(2,1)}), bf16[8,272,128]{2,1,0:T(8,128)(2,1)S(1)}, u32[]{:S(2)}, u32[]{:S(2)}) async-start(bf16[8,272,128]{2,1,0:T(8,128)(2,1)} %bitcast.34), calls=%async_computation | async-start | bytes 1114112 | tf_op jit(solution)/shard_map/all_to_all | solution.py:601
  27.2 3.1 %collective-permute-start.2 = (f32[8,192]{1,0:T(8,128)S(1)}, f32[8,192]{1,0:T(8,128)S(1)}, u32[]{:S(2)}, u32[]{:S(2)}) collective-permute-start(f32[8,192]{1,0:T(8,128)S(1)} %get-tuple-element.61.refs_1_), channel_id=1, source_target_pairs={{0,3},{1,2},{2,1},{3,0},{4,7},{5,6},{6,5},{7,4},{8,11},{9,10},{10,... | collective-permute-start | bytes 18440 | tf_op jit(solution)/shard_map/ppermute | solution.py:696
  27.2 3.7 %collective-permute-start.1 = (f32[8,192]{1,0:T(8,128)S(1)}, f32[8,192]{1,0:T(8,128)S(1)}, u32[]{:S(2)}, u32[]{:S(2)}) collective-permute-start(f32[8,192]{1,0:T(8,128)S(1)} %get-tuple-element.61.refs_1_), channel_id=1, source_target_pairs={{0,2},{1,3},{2,0},{3,1},{4,6},{5,7},{6,4},{7,5},{8,10},{9,11},{10,... | collective-permute-start | bytes 18440 | tf_op jit(solution)/shard_map/ppermute | solution.py:696
  28.7 2.2 %collective-permute-start = (f32[8,192]{1,0:T(8,128)S(1)}, f32[8,192]{1,0:T(8,128)S(1)}, u32[]{:S(2)}, u32[]{:S(2)}) collective-permute-start(f32[8,192]{1,0:T(8,128)S(1)} %get-tuple-element.61.refs_1_), channel_id=1, source_target_pairs={{0,1},{1,0},{2,3},{3,2},{4,5},{5,4},{6,7},{7,6},{8,9},{9,8},{10,11... | collective-permute-start | bytes 18440 | tf_op jit(solution)/shard_map/ppermute | solution.py:696
  34.0 19.6 %all-to-all-start.1 = ((bf16[8,272,128]{2,1,0:T(8,128)(2,1)}), bf16[8,272,128]{2,1,0:T(8,128)(2,1)S(1)}, u32[]{:S(2)}, u32[]{:S(2)}) async-start(bf16[8,272,128]{2,1,0:T(8,128)(2,1)} %bitcast.36), calls=%async_computation.1 | async-start | bytes 1114112 | tf_op jit(solution)/shard_map/all_to_all | solution.py:601
  39.9 1.9 %collective-permute-start.3 = (bf16[32,512]{1,0:T(8,128)(2,1)S(1)}, bf16[32,512]{1,0:T(8,128)(2,1)S(1)}, u32[]{:S(2)}, u32[]{:S(2)}) collective-permute-start(bf16[32,512]{1,0:T(8,128)(2,1)S(1)} %get-tuple-element.69), channel_id=1, source_target_pairs={{0,1},{1,0},{2,3},{3,2},{4,5},{5,4},{6,7},{7,6},{8,9},{9,8},{10,11... | collective-permute-start | bytes 98312 | tf_op jit(solution)/shard_map/ppermute | solution.py:734
  40.0 4.3 %collective-permute-start.4 = (bf16[32,512]{1,0:T(8,128)(2,1)S(1)}, bf16[32,512]{1,0:T(8,128)(2,1)S(1)}, u32[]{:S(2)}, u32[]{:S(2)}) collective-permute-start(bf16[32,512]{1,0:T(8,128)(2,1)S(1)} %get-tuple-element.70), channel_id=1, source_target_pairs={{0,2},{1,3},{2,0},{3,1},{4,6},{5,7},{6,4},{7,5},{8,10},{9,11},{10,... | collective-permute-start | bytes 98312 | tf_op jit(solution)/shard_map/ppermute | solution.py:734
  40.6 3.7 %collective-permute-start.5 = (bf16[32,512]{1,0:T(8,128)(2,1)S(1)}, bf16[32,512]{1,0:T(8,128)(2,1)S(1)}, u32[]{:S(2)}, u32[]{:S(2)}) collective-permute-start(bf16[32,512]{1,0:T(8,128)(2,1)S(1)} %get-tuple-element.71), channel_id=1, source_target_pairs={{0,3},{1,2},{2,1},{3,0},{4,7},{5,6},{6,5},{7,4},{8,11},{9,10},{10,... | collective-permute-start | bytes 98312 | tf_op jit(solution)/shard_map/ppermute | solution.py:734

commit v3 on v2

--- a/solution.py
+++ b/solution.py
@@ -17,7 +17,7 @@
 NN = (((1,), (0,)), ((), ()))
 
 
-def call(kernel, outs, scalars=(), near=(), far=(), raw=(), held=(), scratch=(), vmem=16):
+def call(kernel, outs, scalars=(), near=(), far=(), raw=(), held=(), scratch=(), raw_outs=(), vmem=16):
     reads = len(scalars) + len(near) + len(far) + len(raw)
 
     def body(*refs):
@@ -33,7 +33,9 @@
         body,
         out_shape=outs,
         in_specs=specs,
-        out_specs=jax.tree.map(lambda _: pl.BlockSpec(memory_space=pltpu.VMEM), outs),
+        out_specs=tuple(
+            pl.BlockSpec(memory_space=pltpu.HBM if i in raw_outs else pltpu.VMEM) for i in range(len(outs))
+        ),
         scratch_shapes=list(scratch),
         compiler_params=pltpu.CompilerParams(vmem_limit_bytes=vmem * 1024 * 1024),
         cost_estimate=pl.CostEstimate(flops=1 << 20, bytes_accessed=1 << 20, transcendentals=0),
@@ -64,6 +66,20 @@
     return jnp.concatenate(parts, axis=1)
 
 
+def order_of(blocks):
+    return (2, 3, 1, 0, 4, 5, 7, 6) if blocks == 8 else tuple(range(blocks))
+
+
+def seat_of(block, blocks):
+    order = order_of(blocks)
+    if order == tuple(range(blocks)):
+        return block
+    seat = jnp.zeros_like(block)
+    for i, b in enumerate(order):
+        seat = jnp.where(block == b, i, seat)
+    return seat
+
+
 def positions(seq_ref, count):
     lane = lax.broadcasted_iota(I32, (1, count), 1)
 
@@ -82,7 +98,7 @@
     for h in range(heads):
         for c in range(halves):
             named = jnp.where(table_ref[h, c : c + 1, :] == slot, 1.0, named)
-    other_of = jnp.broadcast_to(position // requests, (16, count)).astype(F32).astype(BF16)
+    other_of = jnp.broadcast_to(seat_of(position // requests, blocks), (16, count)).astype(F32).astype(BF16)
     other = dot(other_of, named.astype(BF16), NT)[0:1, :].astype(I32)
     rows = max(16, blocks)
     mask = other == lax.broadcasted_iota(I32, (rows, slot_dev), 0)
@@ -95,7 +111,7 @@
     return other * per_peer + rank
 
 
-def place_of_item(table_ref, lines_ref, position, first, requests):
+def place_of_item(table_ref, lines_ref, position, first, blocks, requests, slot_dev):
     heads, halves, count = table_ref.shape
     per_item = heads * halves
     items = requests * per_item
@@ -110,9 +126,10 @@
     of_item = (
         lax.broadcasted_iota(I32, (per_item, items), 0) == lax.broadcasted_iota(I32, (per_item, items), 1) % per_item
     ).astype(F32).astype(BF16)
-    high = dot(dot(mine, (lines // 128).astype(F32).astype(BF16), NT).astype(BF16), of_item)
-    low = dot(dot(mine, (lines % 128).astype(F32).astype(BF16), NT).astype(BF16), of_item)
-    slots = high * 128.0 + low
+    seats = seat_of(lines // slot_dev, blocks)
+    high = dot(dot(mine, seats.astype(F32).astype(BF16), NT).astype(BF16), of_item)
+    low = dot(dot(mine, (lines % slot_dev).astype(F32).astype(BF16), NT).astype(BF16), of_item)
+    slots = high * slot_dev + low
     row = jnp.sum(jnp.where(owner, slots, 0.0), axis=0, keepdims=True)
     diagonal = lax.broadcasted_iota(I32, (items, items), 0) == lax.broadcasted_iota(I32, (items, items), 1)
     column = jnp.sum(jnp.where(diagonal, row, 0.0), axis=1, keepdims=True)
@@ -120,18 +137,26 @@
 
 
 def send_kernel(
-    blocks, requests, per_peer,
+    blocks, requests, per_peer, pieces,
     seq_hbm, read_hbm, state_hbm, edge_hbm,
-    out_ref,
-    seq_ref, read_ref, state_ref, edge_ref, scratch, edge_scratch, sems,
+    out_hbm,
+    seq_ref, read_ref, state_ref, edge_ref, scratch, edge_scratch, out_ref, sems, state_sems, out_sems,
 ):
-    slot_dev = state_ref.shape[0]
+    slot_dev, slot_width = state_ref.shape
     pack = out_ref.shape[1]
     me = lax.axis_index("blk")
-    sources = (seq_hbm, read_hbm, state_hbm, edge_hbm)
-    targets = (seq_ref, read_ref, state_ref, edge_ref)
+    sources = (seq_hbm, read_hbm, edge_hbm)
+    targets = (seq_ref, read_ref, edge_ref)
     copies = [pltpu.make_async_copy(a, b, sems.at[i]) for i, (a, b) in enumerate(zip(sources, targets))]
-    for copy in copies:
+    state_copies = []
+    piece = slot_width // 2 // pieces
+    for i in range(pieces):
+        for start in (i * piece, slot_width // 2 + i * piece):
+            cut = (slice(None), pl.ds(start, piece))
+            state_copies.append(
+                pltpu.make_async_copy(state_hbm.at[cut], state_ref.at[cut], state_sems.at[len(state_copies)])
+            )
+    for copy in (*copies[:2], *state_copies, copies[2]):
         copy.start()
     copies[0].wait()
     copies[1].wait()
@@ -139,17 +164,20 @@
     place = place_of_slot(read_ref, position, me * slot_dev, blocks, per_peer, requests, slot_dev)
     pick = (place == lax.broadcasted_iota(I32, (slot_dev, slot_dev), 0)).astype(F32).astype(BF16)
     left = lax.broadcasted_iota(I32, (slot_dev, 128), 1) < 64
-    copies[3].wait()
-    edge_rows = edge_ref.shape[0]
-    edges = jnp.concatenate([edge_ref[...], jnp.zeros((slot_dev - edge_rows, slot_dev), F32)], axis=0)
-    edge_scratch[...] = dot(pick, edges.astype(BF16), NT)
     half = pack // 2
-    copies[2].wait()
     for b in range(half):
+        if b % (half // pieces) == 0:
+            state_copies[b // (half // pieces) * 2].wait()
+            state_copies[b // (half // pieces) * 2 + 1].wait()
         x = dot(pick, state_ref[:, b * 128 : (b + 1) * 128].astype(BF16))
         y = dot(pick, state_ref[:, (half + b) * 128 : (half + b + 1) * 128].astype(BF16))
         scratch[:, 2 * b, :] = jnp.where(left, x, pltpu.roll(y, 64, 1))
         scratch[:, 2 * b + 1, :] = jnp.where(left, pltpu.roll(x, 64, 1), y)
+    copies[2].wait()
+    edge_rows = edge_ref.shape[0]
+    edges = jnp.concatenate([edge_ref[...], jnp.zeros((slot_dev - edge_rows, slot_dev), F32)], axis=0)
+    edge_scratch[...] = dot(pick, edges.astype(BF16), NT)
+    out_copies = []
     for b in range(blocks):
         at = b * (per_peer + 1)
         out_ref[at : at + per_peer] = scratch[b * per_peer : (b + 1) * per_peer].astype(BF16)
@@ -157,17 +185,22 @@
         if per_peer < pack:
             block = jnp.concatenate([block, jnp.zeros((pack - per_peer, 128), F32)], axis=0)
         out_ref[at + per_peer] = block.astype(BF16)
-
-
-def early_kernel(blocks, requests, per_peer, lines, *refs):
+        if (b + 1) % (blocks // 8) == 0:
+            cut = pl.ds((b + 1 - blocks // 8) * (per_peer + 1), blocks // 8 * (per_peer + 1))
+            out_copies.append(pltpu.make_async_copy(out_ref.at[cut], out_hbm.at[cut], out_sems.at[len(out_copies)]))
+            out_copies[-1].start()
+    for copy in out_copies:
+        copy.wait()
+
+
+def shift_kernel(requests, lines, *refs):
     scalars_hbm, refs = refs[:2], refs[2:]
-    tables_hbm, refs = refs[:2], refs[2:]
     vectors_hbm, refs = refs[:lines], refs[lines:]
     arrays_hbm, refs = refs[:5], refs[5:]
-    index_ref, partial_ref, first_ref, picked_ref, vector_ref = refs[:5]
-    arrays, refs = refs[5:9], refs[9:]
-    seq_ref, count_ref, read_ref, write_ref, layer_ref, line_scratch, lines_ref, sems, line_sem, array_sem = refs
-    pairs = list(zip((*scalars_hbm, *tables_hbm, arrays_hbm[0]), (seq_ref, count_ref, read_ref, write_ref, layer_ref)))
+    partial_ref, first_ref, picked_ref, vector_ref = refs[:4]
+    arrays, refs = refs[4:8], refs[8:]
+    seq_ref, count_ref, layer_ref, line_scratch, sems, line_sem, array_sem = refs
+    pairs = zip((*scalars_hbm, arrays_hbm[0]), (seq_ref, count_ref, layer_ref))
     copies = [pltpu.make_async_copy(a, b, sems.at[i]) for i, (a, b) in enumerate(pairs)]
     line_copies = [
         pltpu.make_async_copy(a, vector_ref.at[pl.ds(i, 1)], line_sem.at[i]) for i, a in enumerate(vectors_hbm)
@@ -175,7 +208,35 @@
     array_copies = [
         pltpu.make_async_copy(a, b, array_sem.at[i]) for i, (a, b) in enumerate(zip(arrays_hbm[1:], arrays))
     ]
-    for copy in (*copies, *line_copies, *array_copies):
+    for copy in (copies[2], *line_copies[:2], *array_copies, *copies[:2], *line_copies[2:]):
+        copy.start()
+    copies[2].wait()
+    steps = layer_ref.shape[0] // requests
+    line = layer_ref[...].astype(F32)
+    line_scratch[...] = line
+    delta = pltpu.roll(line, 1, 0) - line
+    left_decay_ref, left_rate_ref = arrays[:2]
+    rank = left_decay_ref.shape[0]
+    for copy in (*line_copies, *array_copies, *copies[:2]):
+        copy.wait()
+    mixed_decay = (line + delta * vector_ref[0:1, :]).astype(BF16)
+    mixed_rate = (line + delta * vector_ref[1:2, :]).astype(BF16)
+    partial_ref[:, :rank] = dot(mixed_decay, left_decay_ref[...], NT).astype(BF16)
+    partial_ref[:, rank:] = dot(mixed_rate, left_rate_ref[...], NT).astype(BF16)
+    first = lax.axis_index("blk") * requests
+    for p in range(requests):
+        first_ref[p : p + 1, :] = line_scratch[p * steps : p * steps + 1, :]
+        n = count_ref[seq_ref[first + p]]
+        picked_ref[p : p + 1, :] = line_scratch[pl.ds(p * steps + jnp.maximum(n - 1, 0), 1), :]
+
+
+def index_kernel(blocks, requests, per_peer, heads, vector_ref, *refs):
+    hbm, refs = refs[:6], refs[6:]
+    index_ref, key_ref, unit_ref, value_t_ref, unit_first_ref, key_first_ref, value_first_ref, *refs = refs
+    seq_ref, count_ref, read_ref, write_ref, value_ref, lines_ref, sems = refs
+    targets = (seq_ref, count_ref, read_ref, write_ref, key_ref, value_ref)
+    copies = [pltpu.make_async_copy(a, b, sems.at[i]) for i, (a, b) in enumerate(zip(hbm, targets))]
+    for copy in copies:
         copy.start()
     for copy in copies[:4]:
         copy.wait()
@@ -183,8 +244,8 @@
     me = lax.axis_index("blk")
     first = me * requests
     position = positions(seq_ref, read_ref.shape[2])
-    place_in = place_of_item(read_ref, lines_ref, position, first, requests)
-    place_out = place_of_item(write_ref, lines_ref, position, first, requests)
+    place_in = place_of_item(read_ref, lines_ref, position, first, blocks, requests, slot_dev)
+    place_out = place_of_item(write_ref, lines_ref, position, first, blocks, requests, slot_dev)
     target = place_of_slot(write_ref, position, me * slot_dev, blocks, per_peer, requests, slot_dev)
     lane = lax.broadcasted_iota(I32, (1, slot_dev), 1)
     counts = jnp.zeros((1, slot_dev), I32)
@@ -199,22 +260,20 @@
     index_ref[6:7, :] = target + target // per_peer
     index_ref[7:8, :] = jnp.zeros((1, slot_dev), I32)
     copies[4].wait()
-    for copy in (*line_copies, *array_copies):
-        copy.wait()
-    steps = layer_ref.shape[0] // requests
-    line = layer_ref[...].astype(F32)
-    line_scratch[...] = line
-    delta = pltpu.roll(line, 1, 0) - line
-    left_decay_ref, left_rate_ref = arrays[:2]
-    rank = left_decay_ref.shape[0]
-    mixed_decay = (line + delta * vector_ref[0:1, :]).astype(BF16)
-    mixed_rate = (line + delta * vector_ref[1:2, :]).astype(BF16)
-    partial_ref[:, :rank] = dot(mixed_decay, left_decay_ref[...], NT).astype(BF16)
-    partial_ref[:, rank:] = dot(mixed_rate, left_rate_ref[...], NT).astype(BF16)
-    for p in range(requests):
-        first_ref[p : p + 1, :] = line_scratch[p * steps : p * steps + 1, :]
-        n = count_ref[seq_ref[first + p]]
-        picked_ref[p : p + 1, :] = line_scratch[pl.ds(p * steps + jnp.maximum(n - 1, 0), 1), :]
+    copies[5].wait()
+    rows, width = key_ref.shape
+    steps = rows // requests
+    head_width = width // heads
+    u = key_ref[...].astype(F32) * vector_ref[4:5, :]
+    unit_ref[...] = u * lax.rsqrt(group_sum(u * u, head_width) + EPSILON)
+    ident = ident_of(head_width, width)
+    for p in range(requests):
+        cut = slice(p * steps, (p + 1) * steps)
+        line = slice(p, p + 1)
+        unit_first_ref[line, :] = unit_ref[p * steps : p * steps + 1, :]
+        key_first_ref[line, :] = key_ref[cut, :].astype(F32)[0:1, :]
+        value_first_ref[line, :] = value_ref[cut, :].astype(F32)[0:1, :]
+        value_t_ref[p] = dot(ident, expand(value_ref[cut, :], head_width), NT).astype(BF16)
 
 
 def first_kernel(
@@ -268,19 +327,22 @@
 
 
 def prepare_kernel(
-    requests, heads,
-    index_ref, parts_ref, vector_ref, right_decay_ref, right_rate_ref, key_ref, value_ref,
-    a_ref, k_ref, b_ref, scale_ref, key_mod_ref, last_ref, value_t_ref, solve_ref,
-    unit_first_ref, key_first_ref, value_first_ref, through_ref, added_ref,
-    cross, compact, unit_scratch, cum_ref,
+    requests, heads, groups,
+    index_ref, *refs,
 ):
+    parts_refs = refs[:groups]
+    (
+        vector_ref, right_decay_ref, right_rate_ref, key_ref, unit_ref, value_t_ref,
+        a_ref, k_ref, b_ref, scale_ref, key_mod_ref, last_ref, solve_ref, through_ref, added_ref,
+        cross, compact, cum_ref,
+    ) = refs[groups:]
     rows, width = key_ref.shape
     steps = rows // requests
     head_width = width // heads
     rank = right_decay_ref.shape[0]
-    total = parts_ref[0].astype(F32)
-    for g in range(1, parts_ref.shape[0]):
-        total = total + parts_ref[g].astype(F32)
+    total = parts_refs[0][...].astype(F32)
+    for ref in parts_refs[1:]:
+        total = total + ref[...].astype(F32)
     hidden = jnp.tanh(total[:, :rank]).astype(BF16)
     rate_hidden = total[:, rank:].astype(BF16)
     decay = vector_ref[2:3, :] + dot(hidden, right_decay_ref[...])
@@ -289,9 +351,7 @@
     log_forget = jnp.where(later, -DECAY_SCALE * jax.nn.sigmoid(decay), 0.0)
     rate = jax.nn.sigmoid(vector_ref[3:4, :] + dot(rate_hidden, right_rate_ref[...]))
     key = key_ref[...].astype(F32)
-    u = key * vector_ref[4:5, :]
-    unit = u * lax.rsqrt(group_sum(u * u, head_width) + EPSILON)
-    unit_scratch[...] = unit
+    unit = unit_ref[...]
     key_mod = key * (1.0 + (rate - 1.0) * vector_ref[5:6, :])
     key_mod_ref[...] = key_mod.astype(BF16)
     cum = log_forget
@@ -312,12 +372,8 @@
         n = index_ref[3, p]
         at_n = cum_ref[pl.ds(p * steps + jnp.maximum(n - 1, 0), 1), :]
         last_ref[p : p + 1, :] = jnp.where(n > 0, jnp.exp(at_n), 1.0)
-        unit_first_ref[p : p + 1, :] = unit_scratch[p * steps : p * steps + 1, :]
-        key_first_ref[p : p + 1, :] = key_ref[cut, :].astype(F32)[0:1, :]
-        value_first_ref[p : p + 1, :] = value_ref[cut, :].astype(F32)[0:1, :]
         right = jnp.concatenate([expand(k_ref[cut, :], head_width), expand(b_ref[cut, :], head_width)], axis=0)
         cross[p] = dot(a_ref[cut, :], right, NT)
-        value_t_ref[p] = dot(ident, expand(value_ref[cut, :], head_width), NT).astype(BF16)
     lane = lax.broadcasted_iota(I32, (requests, lanes), 1)
     source = lane % steps
     group = lane - source
@@ -413,6 +469,7 @@
         state_ref, change_ref, edge_blocks_ref, unit_first_ref, key_first_ref, last_ref, through_ref, added_ref,
         vector_ref, right_decay_ref, right_rate_ref,
         send_ref, after_ref, key_mod_first_ref,
+        kept_ref,
     ) = refs[groups:]
     width = unit_first_ref.shape[1]
     head_width = width // heads
@@ -432,23 +489,22 @@
     for b in range(edge_blocks_ref.shape[0]):
         send_ref[b * (per_peer + 1) + per_peer] = edge_blocks_ref[b]
     for p in range(requests):
-        n = index_ref[3, p]
         line = slice(p, p + 1)
         written = head_rows(removal[line, :], heads, head_width, 0) + head_rows(key_mod[line, :], heads, head_width, heads)
-        start = state_ref[p].astype(F32)
         change = dot(change_ref[p], written.astype(BF16))
-        after = start * forget[line, :] + change
-        after_b = after.astype(BF16)
-        after_ref[p] = after_b
+        after = state_ref[p].astype(F32) * forget[line, :] + change
+        after_ref[p] = after.astype(BF16)
+        kept_ref[p] = after * last_ref[line, :] + added_ref[p].astype(F32)
+    for p in range(requests):
         parts = []
         for pair in range(heads // 2):
             lanes = slice(pair * 128, (pair + 1) * 128)
             through = through_ref[p, :, lanes]
             zero = jnp.zeros_like(through)
             through = jnp.concatenate([jnp.where(own, through, zero), jnp.where(own, zero, through)], axis=0)
-            parts.append(dot(after_b[:, lanes], through))
-        kept = after * last_ref[line, :] + jnp.concatenate(parts, axis=1) + added_ref[p].astype(F32)
-        kept = jnp.where(n > 0, kept, start)
+            parts.append(dot(after_ref[p, :, lanes], through))
+        kept = kept_ref[p] + jnp.concatenate(parts, axis=1)
+        kept = jnp.where(index_ref[3, p] > 0, kept, state_ref[p].astype(F32))
         for c in range(halves):
             for pair in range(heads // 2):
                 top = kept[(2 * c) * pack : (2 * c + 1) * pack, pair * 128 : (pair + 1) * 128]
@@ -543,12 +599,8 @@
 def place_kernel(per_peer, index_ref, back_ref, out_ref, edge_ref, scratch, edge_scratch, edge_placed):
     slot_dev = out_ref.shape[0]
     pack = back_ref.shape[1]
-    for b in range(slot_dev // per_peer):
-        block = back_ref[b * (per_peer + 1) + per_peer].astype(F32)
-        edge_scratch[b * per_peer : (b + 1) * per_peer, :] = block[:per_peer, :]
     for s in range(slot_dev):
         scratch[s] = back_ref[index_ref[6, s]].astype(F32)
-        edge_placed[s : s + 1, :] = edge_scratch[pl.ds(index_ref[5, s], 1), :]
     left = lax.broadcasted_iota(I32, (slot_dev, 128), 1) < 64
     half = pack // 2
     for b in range(half):
@@ -556,6 +608,11 @@
         odd = scratch[:, 2 * b + 1, :]
         out_ref[:, b * 128 : (b + 1) * 128] = jnp.where(left, even, pltpu.roll(odd, 64, 1))
         out_ref[:, (half + b) * 128 : (half + b + 1) * 128] = jnp.where(left, pltpu.roll(even, 64, 1), odd)
+    for b in range(slot_dev // per_peer):
+        block = back_ref[b * (per_peer + 1) + per_peer].astype(F32)
+        edge_scratch[b * per_peer : (b + 1) * per_peer, :] = block[:per_peer, :]
+    for s in range(slot_dev):
+        edge_placed[s : s + 1, :] = edge_scratch[pl.ds(index_ref[5, s], 1), :]
     edge_ref[...] = jnp.transpose(edge_placed[...])[: edge_ref.shape[0], :]
 
 
@@ -598,14 +655,18 @@
     sds = jax.ShapeDtypeStruct
 
     def exchange(x, axis):
-        return lax.all_to_all(x, axis, split_axis=0, concat_axis=0, tiled=True)
+        return lax.all_to_all(
+            x, axis, split_axis=0, concat_axis=0, tiled=True, axis_index_groups=[list(order_of(blocks))]
+        )
 
     read_table = caller_memory_directory.transpose(1, 2, 0)
     write_table = kept_target_place.transpose(1, 2, 0)
-    sent = call(
-        functools.partial(send_kernel, blocks, requests, per_peer),
-        pltpu.HBM((blocks * (per_peer + 1), pack, 128), BF16),
+    pieces = 1
+    (sent,) = call(
+        functools.partial(send_kernel, blocks, requests, per_peer, pieces),
+        (pltpu.HBM((blocks * (per_peer + 1), pack, 128), BF16),),
         raw=(caller_sequence, read_table, lane_memory_store[0], prior_step_store[0].T),
+        raw_outs=(0,),
         scratch=[
             pltpu.SMEM(caller_sequence.shape, I32),
             pltpu.VMEM(read_table.shape, I32),
@@ -613,7 +674,10 @@
             pltpu.VMEM((edge_rows, slot_dev), F32),
             pltpu.VMEM((slot_dev, pack, 128), F32),
             pltpu.VMEM((slot_dev, slot_dev), F32),
-            pltpu.SemaphoreType.DMA((4,)),
+            pltpu.VMEM((blocks * (per_peer + 1), pack, 128), BF16),
+            pltpu.SemaphoreType.DMA((3,)),
+            pltpu.SemaphoreType.DMA((2 * pieces,)),
+            pltpu.SemaphoreType.DMA((8,)),
         ],
     )
     got = exchange(sent.reshape(blocks, (per_peer + 1) * pack, 128), "blk")
@@ -630,55 +694,61 @@
     wide = sds((rows, width), BF16)
     left = sds((rank, width), BF16)
     (
-        index, partial_sums, first_lines, picked, vector,
-        left_decay, left_rate, right_decay, right_rate,
+        partial_sums, first_lines, picked, vector, left_decay, left_rate, right_decay, right_rate,
     ) = call(
-        functools.partial(early_kernel, blocks, requests, per_peer, len(vectors)),
+        functools.partial(shift_kernel, requests, len(vectors)),
+        (sds((rows, 2 * rank), BF16), one, one, sds((16, width), F32), left, left, left, left),
+        raw=(caller_sequence, approved_guesses, *(x.reshape(1, width) for x in vectors), layer, *arrays),
+        scratch=[
+            pltpu.SMEM(caller_sequence.shape, I32),
+            pltpu.SMEM(approved_guesses.shape, I32),
+            pltpu.VMEM((rows, width), BF16),
+            pltpu.VMEM((rows, width), F32),
+            pltpu.SemaphoreType.DMA((3,)),
+            pltpu.SemaphoreType.DMA((len(vectors),)),
+            pltpu.SemaphoreType.DMA((len(arrays),)),
+        ],
+    )
+
+    def from_group(x):
+        return [x] + [lax.ppermute(x, "head", [(g, g ^ d) for g in range(groups)]) for d in range(1, groups)]
+
+    parts = from_group(partial_sums)
+    head_width = width // heads
+    index, key_near, unit, value_t, unit_first, key_first, value_first = call(
+        functools.partial(index_kernel, blocks, requests, per_peer, heads),
         (
-            sds((8, slot_dev), I32), sds((rows, 2 * rank), BF16), one, one,
-            sds((16, width), F32), left, left, left, left,
+            sds((8, slot_dev), I32), wide, sds((rows, width), F32),
+            sds((requests, head_width, heads * steps), BF16),
+            one, one, one,
         ),
-        raw=(
-            caller_sequence, approved_guesses, read_table, write_table,
-            *(x.reshape(1, width) for x in vectors), layer, *arrays,
-        ),
+        near=(vector,),
+        raw=(caller_sequence, approved_guesses, read_table, write_table, key, value),
+        held=(first_lines, picked, left_decay, left_rate, right_decay, right_rate),
         scratch=[
             pltpu.SMEM(caller_sequence.shape, I32),
             pltpu.SMEM(approved_guesses.shape, I32),
             pltpu.VMEM(read_table.shape, I32),
             pltpu.VMEM(write_table.shape, I32),
             pltpu.VMEM((rows, width), BF16),
-            pltpu.VMEM((rows, width), F32),
             pltpu.VMEM((heads * halves, write_table.shape[2]), I32),
-            pltpu.SemaphoreType.DMA((5,)),
-            pltpu.SemaphoreType.DMA((len(vectors),)),
-            pltpu.SemaphoreType.DMA((len(arrays),)),
+            pltpu.SemaphoreType.DMA((6,)),
         ],
     )
-    parts = lax.all_gather(partial_sums, "head", axis=0)
-
-    head_width = width // heads
-    (
-        a_lines, k_lines, b_lines, scale, key_mod, last, value_t, solve,
-        unit_first, key_first, value_first, through, added,
-    ) = call(
-        functools.partial(prepare_kernel, requests, heads),
+    a_lines, k_lines, b_lines, scale, key_mod, last, solve, through, added = call(
+        functools.partial(prepare_kernel, requests, heads, groups),
         (
             wide, wide, wide, wide, wide, one,
-            sds((requests, head_width, heads * steps), BF16),
             sds((2, steps, requests, heads * steps), F32),
-            one, one, one,
             sds((requests, head_width, width), BF16),
             sds((requests, head_width, width), BF16),
         ),
         scalars=(index,),
-        near=(parts, vector, right_decay, right_rate),
-        far=(key, value),
-        held=(first_lines, picked, left_decay, left_rate),
+        near=(*parts, vector, right_decay, right_rate, key_near, unit, value_t),
+        held=(first_lines, picked, left_decay, left_rate, unit_first, key_first, value_first),
         scratch=[
             pltpu.VMEM((requests, steps, 2 * heads * steps), F32),
             pltpu.VMEM((2, requests, steps, heads * steps), F32),
-            pltpu.VMEM((rows, width), F32),
             pltpu.VMEM((rows, width), F32),
         ],
     )
@@ -692,9 +762,7 @@
         held=(unit_first, value_first, picked, *state_later[1:], *read_later),
         scratch=[pltpu.VMEM((slot_dev, 128), F32)],
     )
-    first_parts = [first_sums] + [
-        lax.ppermute(first_sums, "head", [(g, g ^ d) for g in range(groups)]) for d in range(1, groups)
-    ]
+    first_parts = from_group(first_sums)
     state, change, edge_blocks = call(
         functools.partial(layout_kernel, requests, heads, halves, per_peer),
         (
@@ -720,6 +788,7 @@
             vector, right_decay, right_rate,
         ),
         held=read_later,
+        scratch=[pltpu.VMEM((requests, head_width, width), F32)],
     )
     back = exchange(back.reshape(blocks, (per_peer + 1) * pack, 128), "blk")
     back = back.reshape(blocks * (per_peer + 1), pack, 128)
@@ -733,9 +802,9 @@
     recept = [recept[0]] + [
         lax.ppermute(recept[d], "head", [(g, g ^ d) for g in range(groups)]) for d in range(1, groups)
     ]
-    result = call(
+    (result,) = call(
         functools.partial(read_kernel, requests, heads, groups),
-        pltpu.HBM((rows, width), BF16),
+        (pltpu.HBM((rows, width), BF16),),
         near=(*recept, scale, key_mod, key_mod_first, a_lines, k_lines, b_lines, solve, after, value_t, vector),
         far=(value,),
         held=(index,),

time: 56.4 us -> 52.1 us (0.924)
  blocking collectives: 5.79 us -> 0 us
  starting transfers between devices: 16.1 us -> 18.3 us
  waiting for transfers between devices: 10.7 us -> 9.79 us
    all_gather x1 -> x0, blocking collectives: 5.79 us -> none  [local(): parts = lax.all_gather(partial_sums, 'head', axis=0)]
    all_to_all x2, waiting for transfers between devices: 7.55 us -> 3.98 us  [exchange(): lax.all_to_all(x, axis, split_axis=0, concat_axis=0, tiled=True, axis_ind...]
    ppermute x3 -> x6, waiting for transfers between devices: 0.68 us -> 2.75 us  [from_group(): lax.ppermute(x, 'head', [(g, g ^ d) for g in range(groups)])]
    ppermute x3 -> x6, starting transfers between devices: 1.86 us -> 3.79 us  [from_group(): lax.ppermute(x, 'head', [(g, g ^ d) for g in range(groups)])]
    ppermute x3, waiting for transfers between devices: 2.42 us -> 3.06 us  [local(): lax.ppermute(recept[d], 'head', [(g, g ^ d) for g in range(groups)])]
    pallas_call x9 -> x10, Pallas kernels: 22.8 us -> 23 us  [call(): pl.pallas_call(body, out_shape=outs, in_specs=specs, out_specs=tuple((pl....]
  transfers between devices with their start and end apart: 8 -> 11, of which waited for: 5 -> 8; matrix products, arithmetic and copies ran while one was open for 0% -> 0% of each run, Pallas kernels for 24% -> 27%
where the time goes in v3:
time: 52.1 us; the launch traced here: 51.7 us
  Pallas kernels  23 us (44%)
  starting transfers between devices  18.3 us (35%)
  waiting for transfers between devices  9.79 us (19%)
  between operations  0.68 us (1%)
    pallas_call x10, Pallas kernels, call(): pl.pallas_call(body, out_shape=outs, in_specs=specs, out_specs=tuple((pl....  23 us
    all_to_all x2, starting transfers between devices, exchange(): lax.all_to_all(x, axis, split_axis=0, concat_axis=0, tiled=True, axis_ind...  12.5 us
    all_to_all x2, waiting for transfers between devices, exchange(): lax.all_to_all(x, axis, split_axis=0, concat_axis=0, tiled=True, axis_ind...  3.98 us
    ppermute x6, starting transfers between devices, from_group(): lax.ppermute(x, 'head', [(g, g ^ d) for g in range(groups)])  3.79 us
    ppermute x3, waiting for transfers between devices, local(): lax.ppermute(recept[d], 'head', [(g, g ^ d) for g in range(groups)])  3.06 us
    ppermute x6, waiting for transfers between devices, from_group(): lax.ppermute(x, 'head', [(g, g ^ d) for g in range(groups)])  2.75 us
    ppermute x3, starting transfers between devices, local(): lax.ppermute(recept[d], 'head', [(g, g ^ d) for g in range(groups)])  1.93 us
  transfers between devices with their start and end apart: 11, of which 8 were waited for; matrix products, arithmetic and copies ran while one was open for 0% of the time, Pallas kernels for 27%

profile of v3, /device:TPU:0, one launch (start us, length us, event | category | flops | bytes accessed | tf_op | source)
XLA Modules:
  0.0 51.7 jit_solution(3734740611775580797)
XLA Ops:
  0.6 3.1 %shard_map.240 = bf16[136,16,128]{2,1,0:T(8,128)(2,1)} custom-call(s32[64]{0:T(128)} %refs_0_.4, s32[8,2,64]{2,1,0:T(2,128)} %bitcast.42, f32[128,2048]{1,0:T(8,128)} %bitcast.33, f32[32,128]{1,0:T(8,128)} %bitcast.44), custom_call_target="tpu_custom_call" | custom-call | flops 1048576 | bytes 1048576 | tf_op jit(solution)/shard_map/pallas_call | solution.py:32
  3.8 7.9 %all-to-all-start = ((bf16[8,272,128]{2,1,0:T(8,128)(2,1)}), bf16[8,272,128]{2,1,0:T(8,128)(2,1)S(1)}, u32[]{:S(2)}, u32[]{:S(2)}) async-start(bf16[8,272,128]{2,1,0:T(8,128)(2,1)} %bitcast.32), calls=%async_computation | async-start | bytes 1114112 | tf_op jit(solution)/shard_map/all_to_all | solution.py:658
  11.6 1.7 %shard_map.238 = (bf16[128,192]{1,0:T(8,128)(2,1)S(1)}, f32[8,512]{1,0:T(8,128)S(1)}, f32[8,512]{1,0:T(8,128)S(1)}, f32[16,512]{1,0:T(8,128)S(1)}, bf16[96,512]{...) custom-call(s32[64]{0:T(128)} %refs_0_.4, ...), custom_call_target="tpu_custom_call" | custom-call | flops 1048576 | bytes 1048576 | tf_op jit(solution)/shard_map/pallas_call | solution.py:32
  13.3 0.4 collective-permute-start.2
  13.7 1.2 %collective-permute-start.1 = (bf16[128,192]{1,0:T(8,128)(2,1)S(1)}, bf16[128,192]{1,0:T(8,128)(2,1)S(1)}, u32[]{:S(2)}, u32[]{:S(2)}) collective-permute-start(bf16[128,192]{1,0:T(8,128)(2,1)S(1)} %get-tuple-element.52.refs_1_), channel_id=1, source_target_pairs={{0,2},{1,3},{2,0},{3,1},{4,6},{5,7},{6,4},{7,5},{8,10},{9,11},{10,... | collective-permute-start | bytes 147464 | tf_op jit(solution)/shard_map/ppermute | solution.py:714
  14.9 0.3 collective-permute-start
  15.2 1.9 %shard_map.239 = (s32[8,128]{1,0:T(8,128)S(1)}, bf16[128,512]{1,0:T(8,128)(2,1)S(1)}, f32[128,512]{1,0:T(8,128)S(1)}, bf16[8,64,128]{2,1,0:T(8,128)(2,1)S(1)}, f...) custom-call(f32[16,512]{1,0:T(8,128)S(1)} %get-tuple-element.41.refs_0_.refs_5_.refs_3_.refs_6_.refs_13_.refs_2_, ...), custom_call_target="tpu_custom_call" | custom-call | flops 1048576 | bytes 1048576 | tf_op jit(solution)/shard_map/pallas_call | solution.py:32
  17.1 0.6 %collective-permute-done.2.refs_4_ = bf16[128,192]{1,0:T(8,128)(2,1)S(1)} collective-permute-done((bf16[128,192]{1,0:T(8,128)(2,1)S(1)}, bf16[128,192]{1,0:T(8,128)(2,1)S(1)}, u32[]{:S(2)}, u32[]{:S(2)}) %collective-permute-start.2) | collective-permute-done | bytes 49184 | tf_op jit(solution)/shard_map/ppermute | solution.py:714
  17.7 1.5 %collective-permute-done.1.refs_3_ = bf16[128,192]{1,0:T(8,128)(2,1)S(1)} collective-permute-done((bf16[128,192]{1,0:T(8,128)(2,1)S(1)}, bf16[128,192]{1,0:T(8,128)(2,1)S(1)}, u32[]{:S(2)}, u32[]{:S(2)}) %collective-permute-start.1) | collective-permute-done | bytes 49184 | tf_op jit(solution)/shard_map/ppermute | solution.py:714
  19.1 0.0 collective-permute-done.refs_2_
  19.1 4.2 %shard_map.241 = (bf16[128,512]{1,0:T(8,128)(2,1)S(1)}, bf16[128,512]{1,0:T(8,128)(2,1)S(1)}, bf16[128,512]{1,0:T(8,128)(2,1)S(1)}, bf16[128,512]{1,0:T(8,128)(2...) custom-call(s32[8,128]{1,0:T(8,128)S(1)} %get-tuple-element.48.refs_, ...), custom_call_target="tpu_custom_call" | custom-call | flops 1048576 | bytes 1048576 | tf_op jit(solution)/shard_map/pallas_call | solution.py:32
  23.4 1.3 %all-to-all-done = bf16[8,272,128]{2,1,0:T(8,128)(2,1)S(1)} async-done(((bf16[8,272,128]{2,1,0:T(8,128)(2,1)}), bf16[8,272,128]{2,1,0:T(8,128)(2,1)S(1)}, u32[]{:S(2)}, u32[]{:S(2)}) %all-to-all-start) | async-done | bytes 557088 | tf_op jit(solution)/shard_map/all_to_all | solution.py:658
  24.7 1.0 %shard_map.242 = (f32[8,192]{1,0:T(8,128)S(1)}, f32[8,512]{1,0:T(8,128)S(1)}) custom-call(s32[8,128]{1,0:T(8,128)S(1)} %get-tuple-element.48.refs_0_.refs_1_.refs_15_, bf16[136,16,128]{2,1,0:T(8,128)(2,1)S(1)} %bitcast.29, f32[8,512]{1,0:T(8,128)S(1)} %get-tuple-element.42.refs_7_.refs_11_.refs_2_, ...), custom_call_target="tpu_custom_call" | custom-call | flops 1048576 | bytes 1048576 | tf_op jit(solution)/shard_map/pallas_call | solution.py:32
  25.7 0.0 collective-permute-start.5
  25.7 1.5 %collective-permute-start.4 = (f32[8,192]{1,0:T(8,128)S(1)}, f32[8,192]{1,0:T(8,128)S(1)}, u32[]{:S(2)}, u32[]{:S(2)}) collective-permute-start(f32[8,192]{1,0:T(8,128)S(1)} %get-tuple-element.65.refs_1_), channel_id=1, source_target_pairs={{0,2},{1,3},{2,0},{3,1},{4,6},{5,7},{6,4},{7,5},{8,10},{9,11},{10,... | collective-permute-start | bytes 18440 | tf_op jit(solution)/shard_map/ppermute | solution.py:714
  27.2 0.3 collective-permute-start.3
  27.6 1.1 %shard_map.243 = (bf16[8,64,512]{2,1,0:T(8,128)(2,1)S(1)}, bf16[8,64,16]{2,1,0:T(8,128)(2,1)S(1)}, bf16[8,16,128]{2,1,0:T(8,128)(2,1)S(1)}) custom-call(s32[8,128]{1,0:T(8,128)S(1)} %get-tuple-element.48.refs_0_.refs_1_.refs_15_, bf16[136,16,128]{2,1,0:T(8,128)(2,1)S(1)} %bitcast.30, f32[8,512]{1,0:T(8,128)S(1)} %get-tuple-element.49.refs_15_.refs_6_.refs_2_.refs_8_, ...), custom_call_target="tpu_custom_call" | custom-call | flops 1048576 | bytes 1048576 | tf_op jit(solution)/shard_map/pallas_call | solution.py:32
  28.7 0.1 collective-permute-done.5.refs_4_
  28.8 0.6 %collective-permute-done.4.refs_3_ = f32[8,192]{1,0:T(8,128)S(1)} collective-permute-done((f32[8,192]{1,0:T(8,128)S(1)}, f32[8,192]{1,0:T(8,128)S(1)}, u32[]{:S(2)}, u32[]{:S(2)}) %collective-permute-start.4) | collective-permute-done | bytes 6176 | tf_op jit(solution)/shard_map/ppermute | solution.py:714
  29.4 0.0 collective-permute-done.3.refs_2_
  29.4 2.5 %shard_map.244 = (bf16[136,16,128]{2,1,0:T(8,128)(2,1)}, bf16[8,64,512]{2,1,0:T(8,128)(2,1)S(1)}, f32[8,512]{1,0:T(8,128)S(1)}) custom-call(s32[8,128]{1,0:T(8,128)S(1)} %get-tuple-element.48.refs_0_.refs_1_.refs_15_, f32[8,192]{1,0:T(8,128)S(1)} %get-tuple-element.65.refs_1_, f32[8,192]{1,0:T(8,128)S(1)} %collective-permute-done.3.refs_2_, ...), custom_call_target="tpu_custom_call" | custom-call | flops 1048576 | bytes 1048576 | tf_op jit(solution)/shard_map/pallas_call | solution.py:32
  31.9 4.7 %all-to-all-start.1 = ((bf16[8,272,128]{2,1,0:T(8,128)(2,1)}), bf16[8,272,128]{2,1,0:T(8,128)(2,1)S(1)}, u32[]{:S(2)}, u32[]{:S(2)}) async-start(bf16[8,272,128]{2,1,0:T(8,128)(2,1)} %bitcast.34), calls=%async_computation.1 | async-start | bytes 1114112 | tf_op jit(solution)/shard_map/all_to_all | solution.py:658
  36.5 1.0 %shard_map.245 = (bf16[32,512]{1,0:T(8,128)(2,1)S(1)}, bf16[32,512]{1,0:T(8,128)(2,1)S(1)}, bf16[32,512]{1,0:T(8,128)(2,1)S(1)}, bf16[32,512]{1,0:T(8,128)(2,1)S(1)}) custom-call(bf16[8,4,2048]{2,1,0:T(4,128)(2,1)} %refs_0_.5, s32[8,128]{1,0:T(8,128)S(1)} %get-tuple-element.48.refs_0_.refs_1_.refs_15_, ...), custom_call_target="tpu_custom_call" | custom-call | flops 1048576 | bytes 1048576 | tf_op jit(solution)/shard_map/pallas_call | solution.py:32
  37.5 0.2 collective-permute-start.6
  37.7 1.4 %collective-permute-start.7 = (bf16[32,512]{1,0:T(8,128)(2,1)S(1)}, bf16[32,512]{1,0:T(8,128)(2,1)S(1)}, u32[]{:S(2)}, u32[]{:S(2)}) collective-permute-start(bf16[32,512]{1,0:T(8,128)(2,1)S(1)} %get-tuple-element.74), channel_id=1, source_target_pairs={{0,2},{1,3},{2,0},{3,1},{4,6},{5,7},{6,4},{7,5},{8,10},{9,11},{10,... | collective-permute-start | bytes 98312 | tf_op jit(solution)/shard_map/ppermute | solution.py:803
  39.2 0.3 collective-permute-start.8
  39.4 0.0 collective-permute-done.6.refs_1_
  39.4 2.2 %collective-permute-done.7.refs_2_ = bf16[32,512]{1,0:T(8,128)(2,1)S(1)} collective-permute-done((bf16[32,512]{1,0:T(8,128)(2,1)S(1)}, bf16[32,512]{1,0:T(8,128)(2,1)S(1)}, u32[]{:S(2)}, u32[]{:S(2)}) %collective-permute-start.7) | collective-permute-done | bytes 32800 | tf_op jit(solution)/shard_map/ppermute | solution.py:803
  41.7 0.8 %collective-permute-done.8.refs_3_ = bf16[32,512]{1,0:T(8,128)(2,1)S(1)} collective-permute-done((bf16[32,512]{1,0:T(8,128)(2,1)S(1)}, bf16[32,512]{1,0:T(8,128)(2,1)S(1)}, u32[]{:S(2)}, u32[]{:S(2)}) %collective-permute-start.8) | collective-permute-done | bytes 32800 | tf_op jit(solution)/shard_map/ppermute | solution.py:803
  42.5 4.1 %shard_map.246 = bf16[128,512]{1,0:T(8,128)(2,1)} custom-call(bf16[32,512]{1,0:T(8,128)(2,1)S(1)} %get-tuple-element.72.refs_0_, bf16[32,512]{1,0:T(8,128)(2,1)S(1)} %collective-permute-done.6.refs_1_, bf16[32,512]{1,0:T(8,128)(2,1)S(1)} %collective-permute-done.7.refs_2_, bf16[32,512]{1,0:T(8,128)(2,1)S(1)} %collective-permute-done.8.refs_3_, ...), custom_call_target="tpu_custom_call" | custom-call | flops 1048576 | bytes 1048576 | tf_op jit(solution)/shard_map/pallas_call | solution.py:32
  46.7 2.6 %all-to-all-done.1 = bf16[8,272,128]{2,1,0:T(8,128)(2,1)S(1)} async-done(((bf16[8,272,128]{2,1,0:T(8,128)(2,1)}), bf16[8,272,128]{2,1,0:T(8,128)(2,1)S(1)}, u32[]{:S(2)}, u32[]{:S(2)}) %all-to-all-start.1) | async-done | bytes 557088 | tf_op jit(solution)/shard_map/all_to_all | solution.py:658
  49.3 2.4 %shard_map.247 = (f32[128,2048]{1,0:T(8,128)}, f32[32,128]{1,0:T(8,128)}) custom-call(s32[8,128]{1,0:T(8,128)S(1)} %get-tuple-element.48.refs_0_.refs_1_.refs_15_, bf16[136,16,128]{2,1,0:T(8,128)(2,1)S(1)} %bitcast.31), custom_call_target="tpu_custom_call" | custom-call | flops 1048576 | bytes 1048576 | tf_op jit(solution)/shard_map/pallas_call | solution.py:32
Async XLA Ops:
  3.8 21.0 %all-to-all-start = ((bf16[8,272,128]{2,1,0:T(8,128)(2,1)}), bf16[8,272,128]{2,1,0:T(8,128)(2,1)S(1)}, u32[]{:S(2)}, u32[]{:S(2)}) async-start(bf16[8,272,128]{2,1,0:T(8,128)(2,1)} %bitcast.32), calls=%async_computation | async-start | bytes 1114112 | tf_op jit(solution)/shard_map/all_to_all | solution.py:658
  13.3 4.4 %collective-permute-start.2 = (bf16[128,192]{1,0:T(8,128)(2,1)S(1)}, bf16[128,192]{1,0:T(8,128)(2,1)S(1)}, u32[]{:S(2)}, u32[]{:S(2)}) collective-permute-start(bf16[128,192]{1,0:T(8,128)(2,1)S(1)} %get-tuple-element.52.refs_1_), channel_id=1, source_target_pairs={{0,3},{1,2},{2,1},{3,0},{4,7},{5,6},{6,5},{7,4},{8,11},{9,10},{10,... | collective-permute-start | bytes 147464 | tf_op jit(solution)/shard_map/ppermute | solution.py:714
  13.7 5.4 %collective-permute-start.1 = (bf16[128,192]{1,0:T(8,128)(2,1)S(1)}, bf16[128,192]{1,0:T(8,128)(2,1)S(1)}, u32[]{:S(2)}, u32[]{:S(2)}) collective-permute-start(bf16[128,192]{1,0:T(8,128)(2,1)S(1)} %get-tuple-element.52.refs_1_), channel_id=1, source_target_pairs={{0,2},{1,3},{2,0},{3,1},{4,6},{5,7},{6,4},{7,5},{8,10},{9,11},{10,... | collective-permute-start | bytes 147464 | tf_op jit(solution)/shard_map/ppermute | solution.py:714
  14.9 4.2 %collective-permute-start = (bf16[128,192]{1,0:T(8,128)(2,1)S(1)}, bf16[128,192]{1,0:T(8,128)(2,1)S(1)}, u32[]{:S(2)}, u32[]{:S(2)}) collective-permute-start(bf16[128,192]{1,0:T(8,128)(2,1)S(1)} %get-tuple-element.52.refs_1_), channel_id=1, source_target_pairs={{0,1},{1,0},{2,3},{3,2},{4,5},{5,4},{6,7},{7,6},{8,9},{9,8},{10,11... | collective-permute-start | bytes 147464 | tf_op jit(solution)/shard_map/ppermute | solution.py:714
  25.7 3.1 %collective-permute-start.5 = (f32[8,192]{1,0:T(8,128)S(1)}, f32[8,192]{1,0:T(8,128)S(1)}, u32[]{:S(2)}, u32[]{:S(2)}) collective-permute-start(f32[8,192]{1,0:T(8,128)S(1)} %get-tuple-element.65.refs_1_), channel_id=1, source_target_pairs={{0,3},{1,2},{2,1},{3,0},{4,7},{5,6},{6,5},{7,4},{8,11},{9,10},{10,... | collective-permute-start | bytes 18440 | tf_op jit(solution)/shard_map/ppermute | solution.py:714
  25.7 3.7 %collective-permute-start.4 = (f32[8,192]{1,0:T(8,128)S(1)}, f32[8,192]{1,0:T(8,128)S(1)}, u32[]{:S(2)}, u32[]{:S(2)}) collective-permute-start(f32[8,192]{1,0:T(8,128)S(1)} %get-tuple-element.65.refs_1_), channel_id=1, source_target_pairs={{0,2},{1,3},{2,0},{3,1},{4,6},{5,7},{6,4},{7,5},{8,10},{9,11},{10,... | collective-permute-start | bytes 18440 | tf_op jit(solution)/shard_map/ppermute | solution.py:714
  27.2 2.2 %collective-permute-start.3 = (f32[8,192]{1,0:T(8,128)S(1)}, f32[8,192]{1,0:T(8,128)S(1)}, u32[]{:S(2)}, u32[]{:S(2)}) collective-permute-start(f32[8,192]{1,0:T(8,128)S(1)} %get-tuple-element.65.refs_1_), channel_id=1, source_target_pairs={{0,1},{1,0},{2,3},{3,2},{4,5},{5,4},{6,7},{7,6},{8,9},{9,8},{10,11... | collective-permute-start | bytes 18440 | tf_op jit(solution)/shard_map/ppermute | solution.py:714
  31.9 17.4 %all-to-all-start.1 = ((bf16[8,272,128]{2,1,0:T(8,128)(2,1)}), bf16[8,272,128]{2,1,0:T(8,128)(2,1)S(1)}, u32[]{:S(2)}, u32[]{:S(2)}) async-start(bf16[8,272,128]{2,1,0:T(8,128)(2,1)} %bitcast.34), calls=%async_computation.1 | async-start | bytes 1114112 | tf_op jit(solution)/shard_map/all_to_all | solution.py:658
  37.5 1.9 %collective-permute-start.6 = (bf16[32,512]{1,0:T(8,128)(2,1)S(1)}, bf16[32,512]{1,0:T(8,128)(2,1)S(1)}, u32[]{:S(2)}, u32[]{:S(2)}) collective-permute-start(bf16[32,512]{1,0:T(8,128)(2,1)S(1)} %get-tuple-element.73), channel_id=1, source_target_pairs={{0,1},{1,0},{2,3},{3,2},{4,5},{5,4},{6,7},{7,6},{8,9},{9,8},{10,11... | collective-permute-start | bytes 98312 | tf_op jit(solution)/shard_map/ppermute | solution.py:803
  37.7 3.9 %collective-permute-start.7 = (bf16[32,512]{1,0:T(8,128)(2,1)S(1)}, bf16[32,512]{1,0:T(8,128)(2,1)S(1)}, u32[]{:S(2)}, u32[]{:S(2)}) collective-permute-start(bf16[32,512]{1,0:T(8,128)(2,1)S(1)} %get-tuple-element.74), channel_id=1, source_target_pairs={{0,2},{1,3},{2,0},{3,1},{4,6},{5,7},{6,4},{7,5},{8,10},{9,11},{10,... | collective-permute-start | bytes 98312 | tf_op jit(solution)/shard_map/ppermute | solution.py:803
  39.2 3.3 %collective-permute-start.8 = (bf16[32,512]{1,0:T(8,128)(2,1)S(1)}, bf16[32,512]{1,0:T(8,128)(2,1)S(1)}, u32[]{:S(2)}, u32[]{:S(2)}) collective-permute-start(bf16[32,512]{1,0:T(8,128)(2,1)S(1)} %get-tuple-element.75), channel_id=1, source_target_pairs={{0,3},{1,2},{2,1},{3,0},{4,7},{5,6},{6,5},{7,4},{8,11},{9,10},{10,... | collective-permute-start | bytes 98312 | tf_op jit(solution)/shard_map/ppermute | solution.py:803

commit v4 on v3

--- a/solution.py
+++ b/solution.py
@@ -17,8 +17,8 @@
 NN = (((1,), (0,)), ((), ()))
 
 
-def call(kernel, outs, scalars=(), near=(), far=(), raw=(), held=(), scratch=(), raw_outs=(), vmem=16):
-    reads = len(scalars) + len(near) + len(far) + len(raw)
+def call(kernel, outs, scalars=(), near=(), far=(), raw=(), loose=(), held=(), scratch=(), raw_outs=(), vmem=16):
+    reads = len(scalars) + len(near) + len(far) + len(raw) + len(loose)
 
     def body(*refs):
         kernel(*refs[:reads], *refs[reads + len(held) :])
@@ -28,7 +28,7 @@
     args += [pltpu.with_memory_space_constraint(x, pltpu.HBM) for x in (*far, *raw)]
     specs = [pl.BlockSpec(memory_space=pltpu.SMEM)] * len(scalars)
     specs += [pl.BlockSpec(memory_space=pltpu.VMEM)] * (len(near) + len(far))
-    specs += [pl.BlockSpec(memory_space=pltpu.HBM)] * (len(raw) + len(held))
+    specs += [pl.BlockSpec(memory_space=pltpu.HBM)] * (len(raw) + len(loose) + len(held))
     return pl.pallas_call(
         body,
         out_shape=outs,
@@ -39,7 +39,7 @@
         scratch_shapes=list(scratch),
         compiler_params=pltpu.CompilerParams(vmem_limit_bytes=vmem * 1024 * 1024),
         cost_estimate=pl.CostEstimate(flops=1 << 20, bytes_accessed=1 << 20, transcendentals=0),
-    )(*args, *held)
+    )(*args, *loose, *held)
 
 
 def dot(a, b, dims=NN):
@@ -140,7 +140,7 @@
     blocks, requests, per_peer, pieces,
     seq_hbm, read_hbm, state_hbm, edge_hbm,
     out_hbm,
-    seq_ref, read_ref, state_ref, edge_ref, scratch, edge_scratch, out_ref, sems, state_sems, out_sems,
+    seq_ref, read_ref, state_ref, edge_ref, flat, scratch, edge_scratch, out_ref, sems, state_sems, out_sems,
 ):
     slot_dev, slot_width = state_ref.shape
     pack = out_ref.shape[1]
@@ -171,8 +171,12 @@
             state_copies[b // (half // pieces) * 2 + 1].wait()
         x = dot(pick, state_ref[:, b * 128 : (b + 1) * 128].astype(BF16))
         y = dot(pick, state_ref[:, (half + b) * 128 : (half + b + 1) * 128].astype(BF16))
-        scratch[:, 2 * b, :] = jnp.where(left, x, pltpu.roll(y, 64, 1))
-        scratch[:, 2 * b + 1, :] = jnp.where(left, pltpu.roll(x, 64, 1), y)
+        flat[:, 2 * b * 128 : (2 * b + 1) * 128] = jnp.where(left, x, pltpu.roll(y, 64, 1))
+        flat[:, (2 * b + 1) * 128 : (2 * b + 2) * 128] = jnp.where(left, pltpu.roll(x, 64, 1), y)
+    for row in range(0, slot_dev, 8):
+        for j in range(0, pack, 8):
+            tiles = [flat[row : row + 8, i * 128 : (i + 1) * 128] for i in range(j, j + 8)]
+            scratch[row : row + 8, j : j + 8, :] = jnp.swapaxes(jnp.stack(tiles), 0, 1)
     copies[2].wait()
     edge_rows = edge_ref.shape[0]
     edges = jnp.concatenate([edge_ref[...], jnp.zeros((slot_dev - edge_rows, slot_dev), F32)], axis=0)
@@ -191,6 +195,14 @@
             out_copies[-1].start()
     for copy in out_copies:
         copy.wait()
+
+
+def pick_of(place):
+    count = place.shape[1]
+    row = lax.broadcasted_iota(I32, (count, count), 0)
+    lane = lax.broadcasted_iota(I32, (count, count), 1)
+    column = jnp.sum(jnp.where(row == lane, place, 0).astype(F32), axis=1, keepdims=True).astype(I32)
+    return (column == lane).astype(F32).astype(BF16)
 
 
 def shift_kernel(requests, lines, *refs):
@@ -232,7 +244,8 @@
 
 def index_kernel(blocks, requests, per_peer, heads, vector_ref, *refs):
     hbm, refs = refs[:6], refs[6:]
-    index_ref, key_ref, unit_ref, value_t_ref, unit_first_ref, key_first_ref, value_first_ref, *refs = refs
+    index_ref, pick_in_ref, pick_out_ref, key_ref, unit_ref, value_t_ref, *refs = refs
+    unit_first_ref, key_first_ref, value_first_ref, *refs = refs
     seq_ref, count_ref, read_ref, write_ref, value_ref, lines_ref, sems = refs
     targets = (seq_ref, count_ref, read_ref, write_ref, key_ref, value_ref)
     copies = [pltpu.make_async_copy(a, b, sems.at[i]) for i, (a, b) in enumerate(zip(hbm, targets))]
@@ -256,9 +269,9 @@
     index_ref[2:3, :] = place_in + place_in // per_peer
     index_ref[3:4, :] = counts
     index_ref[4:5, :] = place_out + place_out // per_peer
-    index_ref[5:6, :] = target
-    index_ref[6:7, :] = target + target // per_peer
-    index_ref[7:8, :] = jnp.zeros((1, slot_dev), I32)
+    index_ref[5:8, :] = jnp.zeros((3, slot_dev), I32)
+    pick_in_ref[...] = pick_of(place_in)
+    pick_out_ref[...] = pick_of(target)
     copies[4].wait()
     copies[5].wait()
     rows, width = key_ref.shape
@@ -278,18 +291,18 @@
 
 def first_kernel(
     requests, heads, halves, per_peer,
-    index_ref, got_ref, first_ref, vector_ref, left_decay_ref, left_rate_ref,
-    out_ref, edge_ref, pool_scratch,
+    pick_ref, got_ref, first_ref, vector_ref, left_decay_ref, left_rate_ref,
+    out_ref, edge_ref, pool_scratch, item_scratch,
 ):
     slot_dev = pool_scratch.shape[0]
-    rows = first_ref.shape[1] // (heads * halves)
+    per_item = heads * halves
+    rows = first_ref.shape[1] // per_item
     for b in range(slot_dev // per_peer):
         block = got_ref[b * (per_peer + 1) + per_peer].astype(F32)
         pool_scratch[b * per_peer : (b + 1) * per_peer, :] = block[:per_peer, :]
-    for p in range(requests):
-        for k in range(heads * halves):
-            place = index_ref[0, p * heads * halves + k]
-            edge_ref[p : p + 1, k * rows : (k + 1) * rows] = pool_scratch[pl.ds(place, 1), :rows]
+    item_scratch[...] = dot(pick_ref[...], pool_scratch[...].astype(BF16))
+    for k in range(per_item):
+        edge_ref[:, k * rows : (k + 1) * rows] = item_scratch[pl.ds(k, requests, per_item), :rows]
     line = first_ref[...]
     delta = edge_ref[...] - line
     rank = left_decay_ref.shape[0]
@@ -328,14 +341,16 @@
 
 def prepare_kernel(
     requests, heads, groups,
-    index_ref, *refs,
+    *refs,
 ):
     parts_refs = refs[:groups]
     (
-        vector_ref, right_decay_ref, right_rate_ref, key_ref, unit_ref, value_t_ref,
+        vector_ref, right_decay_ref, right_rate_ref, key_ref, unit_ref, value_t_ref, index_near_ref,
         a_ref, k_ref, b_ref, scale_ref, key_mod_ref, last_ref, solve_ref, through_ref, added_ref,
-        cross, compact, cum_ref,
+        cross, compact, cum_ref, k_low_ref, b_low_ref, index_ref, index_sem,
     ) = refs[groups:]
+    index_copy = pltpu.make_async_copy(index_near_ref, index_ref, index_sem)
+    index_copy.start()
     rows, width = key_ref.shape
     steps = rows // requests
     head_width = width // heads
@@ -363,10 +378,11 @@
     cum_ref[...] = cum
     scale_ref[...] = jnp.exp(cum).astype(BF16)
     a_ref[...] = jnp.where(later, unit * jnp.exp(cum - log_forget), 0.0).astype(BF16)
-    k_ref[...] = (key_mod * grow).astype(BF16)
-    b_ref[...] = (rate * unit * grow).astype(BF16)
+    k_ref[...], k_low_ref[...] = split(key_mod * grow)
+    b_ref[...], b_low_ref[...] = split(rate * unit * grow)
     ident = ident_of(head_width, width)
     lanes = heads * steps
+    index_copy.wait()
     for p in range(requests):
         cut = slice(p * steps, (p + 1) * steps)
         n = index_ref[3, p]
@@ -398,7 +414,8 @@
         a_t = dot(ident, expand(a_ref[cut, :], head_width), NT).astype(BF16)
         value_t = value_t_ref[p]
         reach = dot(a_t, spread(compact[0, p].astype(BF16), steps), NT)
-        removed = dot(value_t, spread(compact[1, p].astype(BF16), steps), NT)
+        high, low = split(compact[1, p])
+        removed = dot(value_t, spread(high, steps), NT) + dot(value_t, spread(low, steps), NT)
         left = jnp.concatenate(
             [
                 jnp.concatenate([-reach, jnp.zeros_like(reach)], axis=1),
@@ -407,9 +424,10 @@
             axis=0,
         )
         at = lax.broadcasted_iota(I32, left.shape, 1) % steps
-        left = jnp.where(at < n, left, 0.0).astype(BF16)
+        left, left_low = split(jnp.where(at < n, left, 0.0))
         right = jnp.concatenate([expand(b_ref[cut, :], head_width), expand(k_ref[cut, :], head_width)], axis=0)
-        both = dot(left, right) * last_ref[p : p + 1, :]
+        right_low = jnp.concatenate([expand(b_low_ref[cut, :], head_width), expand(k_low_ref[cut, :], head_width)], axis=0)
+        both = (dot(left, right) + dot(left_low, right) + dot(left, right_low)) * last_ref[p : p + 1, :]
         added_ref[p] = both[head_width:, :].astype(BF16)
         through_ref[p] = both[:head_width, :].astype(BF16)
 
@@ -462,15 +480,17 @@
 
 def state_kernel(
     requests, heads, halves, per_peer, groups,
-    index_ref, *refs,
+    *refs,
 ):
     parts_refs = refs[:groups]
     (
         state_ref, change_ref, edge_blocks_ref, unit_first_ref, key_first_ref, last_ref, through_ref, added_ref,
-        vector_ref, right_decay_ref, right_rate_ref,
+        vector_ref, right_decay_ref, right_rate_ref, index_near_ref,
         send_ref, after_ref, key_mod_first_ref,
-        kept_ref,
+        kept_ref, index_ref, index_sem,
     ) = refs[groups:]
+    index_copy = pltpu.make_async_copy(index_near_ref, index_ref, index_sem)
+    index_copy.start()
     width = unit_first_ref.shape[1]
     head_width = width // heads
     pack = send_ref.shape[1]
@@ -495,6 +515,7 @@
         after = state_ref[p].astype(F32) * forget[line, :] + change
         after_ref[p] = after.astype(BF16)
         kept_ref[p] = after * last_ref[line, :] + added_ref[p].astype(F32)
+    index_copy.wait()
     for p in range(requests):
         parts = []
         for pair in range(heads // 2):
@@ -596,24 +617,27 @@
     result_ref[...] = (line + bonus * value_ref[...].astype(F32)).astype(BF16)
 
 
-def place_kernel(per_peer, index_ref, back_ref, out_ref, edge_ref, scratch, edge_scratch, edge_placed):
+def place_kernel(per_peer, pick_ref, back_ref, out_ref, edge_ref, scratch, flat, edge_scratch):
     slot_dev = out_ref.shape[0]
     pack = back_ref.shape[1]
-    for s in range(slot_dev):
-        scratch[s] = back_ref[index_ref[6, s]].astype(F32)
-    left = lax.broadcasted_iota(I32, (slot_dev, 128), 1) < 64
+    for b in range(slot_dev // per_peer):
+        at = b * (per_peer + 1)
+        scratch[b * per_peer : (b + 1) * per_peer] = back_ref[at : at + per_peer].astype(F32)
+        edge_scratch[b * per_peer : (b + 1) * per_peer, :] = back_ref[at + per_peer].astype(F32)[:per_peer, :]
+    left = lax.broadcasted_iota(I32, (8, 128), 1) < 64
     half = pack // 2
-    for b in range(half):
-        even = scratch[:, 2 * b, :]
-        odd = scratch[:, 2 * b + 1, :]
-        out_ref[:, b * 128 : (b + 1) * 128] = jnp.where(left, even, pltpu.roll(odd, 64, 1))
-        out_ref[:, (half + b) * 128 : (half + b + 1) * 128] = jnp.where(left, pltpu.roll(even, 64, 1), odd)
-    for b in range(slot_dev // per_peer):
-        block = back_ref[b * (per_peer + 1) + per_peer].astype(F32)
-        edge_scratch[b * per_peer : (b + 1) * per_peer, :] = block[:per_peer, :]
-    for s in range(slot_dev):
-        edge_placed[s : s + 1, :] = edge_scratch[pl.ds(index_ref[5, s], 1), :]
-    edge_ref[...] = jnp.transpose(edge_placed[...])[: edge_ref.shape[0], :]
+    for row in range(0, slot_dev, 8):
+        for j in range(0, pack, 8):
+            tiles = jnp.swapaxes(scratch[row : row + 8, j : j + 8, :], 0, 1)
+            for i in range(4):
+                even, odd = tiles[2 * i], tiles[2 * i + 1]
+                b = j // 2 + i
+                flat[row : row + 8, b * 128 : (b + 1) * 128] = jnp.where(left, even, pltpu.roll(odd, 64, 1))
+                flat[row : row + 8, (half + b) * 128 : (half + b + 1) * 128] = jnp.where(left, pltpu.roll(even, 64, 1), odd)
+    pick = pick_ref[...]
+    for start in range(0, pack * 128, 256):
+        out_ref[:, start : start + 256] = dot(pick, flat[:, start : start + 256].astype(BF16))
+    edge_ref[...] = jnp.transpose(dot(pick, edge_scratch[...].astype(BF16)))[: edge_ref.shape[0], :]
 
 
 def local(
@@ -672,6 +696,7 @@
             pltpu.VMEM(read_table.shape, I32),
             pltpu.VMEM((slot_dev, slot_width), F32),
             pltpu.VMEM((edge_rows, slot_dev), F32),
+            pltpu.VMEM((slot_dev, slot_width), F32),
             pltpu.VMEM((slot_dev, pack, 128), F32),
             pltpu.VMEM((slot_dev, slot_dev), F32),
             pltpu.VMEM((blocks * (per_peer + 1), pack, 128), BF16),
@@ -715,10 +740,11 @@
 
     parts = from_group(partial_sums)
     head_width = width // heads
-    index, key_near, unit, value_t, unit_first, key_first, value_first = call(
+    square = sds((slot_dev, slot_dev), BF16)
+    index, pick_in, pick_out, key_near, unit, value_t, unit_first, key_first, value_first = call(
         functools.partial(index_kernel, blocks, requests, per_peer, heads),
         (
-            sds((8, slot_dev), I32), wide, sds((rows, width), F32),
+            sds((8, slot_dev), I32), square, square, wide, sds((rows, width), F32),
             sds((requests, head_width, heads * steps), BF16),
             one, one, one,
         ),
@@ -743,24 +769,27 @@
             sds((requests, head_width, width), BF16),
             sds((requests, head_width, width), BF16),
         ),
-        scalars=(index,),
         near=(*parts, vector, right_decay, right_rate, key_near, unit, value_t),
-        held=(first_lines, picked, left_decay, left_rate, unit_first, key_first, value_first),
+        loose=(index,),
+        held=(pick_in, pick_out, first_lines, picked, left_decay, left_rate, unit_first, key_first, value_first),
         scratch=[
             pltpu.VMEM((requests, steps, 2 * heads * steps), F32),
             pltpu.VMEM((2, requests, steps, heads * steps), F32),
             pltpu.VMEM((rows, width), F32),
+            pltpu.VMEM((rows, width), BF16),
+            pltpu.VMEM((rows, width), BF16),
+            pltpu.SMEM((8, slot_dev), I32),
+            pltpu.SemaphoreType.DMA,
         ],
     )
-    read_later = (scale, key_mod, a_lines, k_lines, b_lines, solve, value_t)
+    read_later = (scale, key_mod, a_lines, k_lines, b_lines, solve, value_t, pick_out)
     state_later = (vector, right_decay, right_rate, key_first, last, through, added)
     first_sums, edge = call(
         functools.partial(first_kernel, requests, heads, halves, per_peer),
         (sds((requests, 2 * rank), F32), one),
-        scalars=(index,),
-        near=(got, first_lines, vector, left_decay, left_rate),
-        held=(unit_first, value_first, picked, *state_later[1:], *read_later),
-        scratch=[pltpu.VMEM((slot_dev, 128), F32)],
+        near=(pick_in, got, first_lines, vector, left_decay, left_rate),
+        held=(index, unit_first, value_first, picked, *state_later[1:], *read_later),
+        scratch=[pltpu.VMEM((slot_dev, 128), F32), pltpu.VMEM((slot_dev, 128), F32)],
     )
     first_parts = from_group(first_sums)
     state, change, edge_blocks = call(
@@ -782,13 +811,17 @@
             sds((requests, head_width, width), BF16),
             one,
         ),
-        scalars=(index,),
         near=(
             *first_parts, state, change, edge_blocks, unit_first, key_first, last, through, added,
             vector, right_decay, right_rate,
         ),
+        loose=(index,),
         held=read_later,
-        scratch=[pltpu.VMEM((requests, head_width, width), F32)],
+        scratch=[
+            pltpu.VMEM((requests, head_width, width), F32),
+            pltpu.SMEM((8, slot_dev), I32),
+            pltpu.SemaphoreType.DMA,
+        ],
     )
     back = exchange(back.reshape(blocks, (per_peer + 1) * pack, 128), "blk")
     back = back.reshape(blocks * (per_peer + 1), pack, 128)
@@ -796,7 +829,7 @@
         lines_kernel,
         (sds((rows // groups, width), BF16),) * groups,
         far=(gating_query,),
-        held=(index, vector, after, key_mod_first, *read_later),
+        held=(vector, after, key_mod_first, *read_later),
         scratch=[pltpu.VMEM((rows // groups, width), F32)],
     )
     recept = [recept[0]] + [
@@ -807,7 +840,7 @@
         (pltpu.HBM((rows, width), BF16),),
         near=(*recept, scale, key_mod, key_mod_first, a_lines, k_lines, b_lines, solve, after, value_t, vector),
         far=(value,),
-        held=(index,),
+        held=(pick_out,),
         scratch=[
             pltpu.VMEM((rows, width), BF16),
             pltpu.VMEM((requests, steps, 2 * heads * steps), F32),
@@ -818,11 +851,10 @@
     new_states, new_edges = call(
         functools.partial(place_kernel, per_peer),
         (pltpu.HBM((slot_dev, slot_width), F32), pltpu.HBM((edge_rows, slot_dev), F32)),
-        scalars=(index,),
-        near=(back,),
+        near=(pick_out, back),
         scratch=[
             pltpu.VMEM((slot_dev, pack, 128), F32),
-            pltpu.VMEM((slot_dev, 128), F32),
+            pltpu.VMEM((slot_dev, slot_width), F32),
             pltpu.VMEM((slot_dev, 128), F32),
         ],
     )

time: 52.1 us -> 49.9 us (0.958)
  Pallas kernels: 23 us -> 20.9 us
    pallas_call x10, Pallas kernels: 23 us -> 20.9 us  [call(): pl.pallas_call(body, out_shape=outs, in_specs=specs, out_specs=tuple((pl....]
  transfers between devices with their start and end apart: 11 -> 11, of which waited for: 8 -> 8; matrix products, arithmetic and copies ran while one was open for 0% -> 0% of each run, Pallas kernels for 27% -> 29%
where the time goes in v4:
time: 49.9 us; the launch traced here: 49.5 us
  Pallas kernels  20.9 us (42%)
  starting transfers between devices  18.3 us (37%)
  waiting for transfers between devices  9.56 us (19%)
  between operations  0.69 us (1%)
    pallas_call x10, Pallas kernels, call(): pl.pallas_call(body, out_shape=outs, in_specs=specs, out_specs=tuple((pl....  20.9 us
    all_to_all x2, starting transfers between devices, exchange(): lax.all_to_all(x, axis, split_axis=0, concat_axis=0, tiled=True, axis_ind...  12.5 us
    all_to_all x2, waiting for transfers between devices, exchange(): lax.all_to_all(x, axis, split_axis=0, concat_axis=0, tiled=True, axis_ind...  3.82 us
    ppermute x6, starting transfers between devices, from_group(): lax.ppermute(x, 'head', [(g, g ^ d) for g in range(groups)])  3.81 us
    ppermute x3, waiting for transfers between devices, local(): lax.ppermute(recept[d], 'head', [(g, g ^ d) for g in range(groups)])  3.05 us
    ppermute x6, waiting for transfers between devices, from_group(): lax.ppermute(x, 'head', [(g, g ^ d) for g in range(groups)])  2.69 us
    ppermute x3, starting transfers between devices, local(): lax.ppermute(recept[d], 'head', [(g, g ^ d) for g in range(groups)])  1.93 us
  transfers between devices with their start and end apart: 11, of which 8 were waited for; matrix products, arithmetic and copies ran while one was open for 0% of the time, Pallas kernels for 29%

profile of v4, /device:TPU:0, one launch (start us, length us, event | category | flops | bytes accessed | tf_op | source)
XLA Modules:
  0.0 49.5 jit_solution(16643194897811107785)
XLA Ops:
  0.6 2.8 %shard_map.240 = bf16[136,16,128]{2,1,0:T(8,128)(2,1)} custom-call(s32[64]{0:T(128)} %refs_0_.4, s32[8,2,64]{2,1,0:T(2,128)} %bitcast.42, f32[128,2048]{1,0:T(8,128)} %bitcast.33, f32[32,128]{1,0:T(8,128)} %bitcast.44), custom_call_target="tpu_custom_call" | custom-call | flops 1048576 | bytes 1048576 | tf_op jit(solution)/shard_map/pallas_call | solution.py:32
  3.4 7.9 %all-to-all-start = ((bf16[8,272,128]{2,1,0:T(8,128)(2,1)}), bf16[8,272,128]{2,1,0:T(8,128)(2,1)S(1)}, u32[]{:S(2)}, u32[]{:S(2)}) async-start(bf16[8,272,128]{2,1,0:T(8,128)(2,1)} %bitcast.32), calls=%async_computation | async-start | bytes 1114112 | tf_op jit(solution)/shard_map/all_to_all | solution.py:682
  11.3 1.7 %shard_map.238 = (bf16[128,192]{1,0:T(8,128)(2,1)S(1)}, f32[8,512]{1,0:T(8,128)S(1)}, f32[8,512]{1,0:T(8,128)S(1)}, f32[16,512]{1,0:T(8,128)S(1)}, bf16[96,512]{...) custom-call(s32[64]{0:T(128)} %refs_0_.4, ...), custom_call_target="tpu_custom_call" | custom-call | flops 1048576 | bytes 1048576 | tf_op jit(solution)/shard_map/pallas_call | solution.py:32
  13.0 0.4 collective-permute-start.2
  13.4 1.2 %collective-permute-start.1 = (bf16[128,192]{1,0:T(8,128)(2,1)S(1)}, bf16[128,192]{1,0:T(8,128)(2,1)S(1)}, u32[]{:S(2)}, u32[]{:S(2)}) collective-permute-start(bf16[128,192]{1,0:T(8,128)(2,1)S(1)} %get-tuple-element.55.refs_0_), channel_id=1, source_target_pairs={{0,2},{1,3},{2,0},{3,1},{4,6},{5,7},{6,4},{7,5},{8,10},{9,11},{10,... | collective-permute-start | bytes 147464 | tf_op jit(solution)/shard_map/ppermute | solution.py:739
  14.6 0.3 collective-permute-start
  14.9 1.9 %shard_map.239 = (s32[8,128]{1,0:T(8,128)S(1)}, bf16[128,128]{1,0:T(8,128)(2,1)S(1)}, bf16[128,128]{1,0:T(8,128)(2,1)S(1)}, bf16[128,512]{1,0:T(8,128)(2,1)S(1)}...) custom-call(f32[16,512]{1,0:T(8,128)S(1)} %get-tuple-element.43.refs, ...), custom_call_target="tpu_custom_call" | custom-call | flops 1048576 | bytes 1048576 | tf_op jit(solution)/shard_map/pallas_call | solution.py:32
  16.8 0.6 %collective-permute-done.2.refs_3_ = bf16[128,192]{1,0:T(8,128)(2,1)S(1)} collective-permute-done((bf16[128,192]{1,0:T(8,128)(2,1)S(1)}, bf16[128,192]{1,0:T(8,128)(2,1)S(1)}, u32[]{:S(2)}, u32[]{:S(2)}) %collective-permute-start.2) | collective-permute-done | bytes 49184 | tf_op jit(solution)/shard_map/ppermute | solution.py:739
  17.4 1.4 %collective-permute-done.1.refs_2_ = bf16[128,192]{1,0:T(8,128)(2,1)S(1)} collective-permute-done((bf16[128,192]{1,0:T(8,128)(2,1)S(1)}, bf16[128,192]{1,0:T(8,128)(2,1)S(1)}, u32[]{:S(2)}, u32[]{:S(2)}) %collective-permute-start.1) | collective-permute-done | bytes 49184 | tf_op jit(solution)/shard_map/ppermute | solution.py:739
  18.8 0.0 collective-permute-done.refs_1_
  18.8 4.4 %shard_map.241 = (bf16[128,512]{1,0:T(8,128)(2,1)S(1)}, bf16[128,512]{1,0:T(8,128)(2,1)S(1)}, bf16[128,512]{1,0:T(8,128)(2,1)S(1)}, bf16[128,512]{1,0:T(8,128)(2...) custom-call(bf16[128,192]{1,0:T(8,128)(2,1)S(1)} %get-tuple-element., ...), custom_call_target="tpu_custom_call" | custom-call | flops 1048576 | bytes 1048576 | tf_op jit(solution)/shard_map/pallas_call | solution.py:32
  23.2 1.2 %all-to-all-done = bf16[8,272,128]{2,1,0:T(8,128)(2,1)S(1)} async-done(((bf16[8,272,128]{2,1,0:T(8,128)(2,1)}), bf16[8,272,128]{2,1,0:T(8,128)(2,1)S(1)}, u32[]{:S(2)}, u32[]{:S(2)}) %all-to-all-start) | async-done | bytes 557088 | tf_op jit(solution)/shard_map/all_to_all | solution.py:682
  24.4 0.4 shard_map.242
  24.8 0.0 collective-permute-start.5
  24.8 1.5 %collective-permute-start.4 = (f32[8,192]{1,0:T(8,128)S(1)}, f32[8,192]{1,0:T(8,128)S(1)}, u32[]{:S(2)}, u32[]{:S(2)}) collective-permute-start(f32[8,192]{1,0:T(8,128)S(1)} %get-tuple-element.69.refs_0_), channel_id=1, source_target_pairs={{0,2},{1,3},{2,0},{3,1},{4,6},{5,7},{6,4},{7,5},{8,10},{9,11},{10,... | collective-permute-start | bytes 18440 | tf_op jit(solution)/shard_map/ppermute | solution.py:739
  26.4 0.3 collective-permute-start.3
  26.7 1.1 %shard_map.243 = (bf16[8,64,512]{2,1,0:T(8,128)(2,1)S(1)}, bf16[8,64,16]{2,1,0:T(8,128)(2,1)S(1)}, bf16[8,16,128]{2,1,0:T(8,128)(2,1)S(1)}) custom-call(s32[8,128]{1,0:T(8,128)S(1)} %get-tuple-element.51.refs_10_.refs_6_.refs_0_.refs_15_, bf16[136,16,128]{2,1,0:T(8,128)(2,1)S(1)} %bitcast.30, f32[8,512]{1,0:T(8,128)S(1)} %get-tuple-element.52.refs_17_.refs_7_.refs_2_, ...), custom_call_target="tpu_custom_call" | custom-call | flops 1048576 | bytes 1048576 | tf_op jit(solution)/shard_map/pallas_call | solution.py:32
  27.9 0.1 collective-permute-done.5.refs_3_
  28.0 0.6 %collective-permute-done.4.refs_2_ = f32[8,192]{1,0:T(8,128)S(1)} collective-permute-done((f32[8,192]{1,0:T(8,128)S(1)}, f32[8,192]{1,0:T(8,128)S(1)}, u32[]{:S(2)}, u32[]{:S(2)}) %collective-permute-start.4) | collective-permute-done | bytes 6176 | tf_op jit(solution)/shard_map/ppermute | solution.py:739
  28.6 0.0 collective-permute-done.3.refs_1_
  28.6 2.0 %shard_map.244 = (bf16[136,16,128]{2,1,0:T(8,128)(2,1)}, bf16[8,64,512]{2,1,0:T(8,128)(2,1)S(1)}, f32[8,512]{1,0:T(8,128)S(1)}) custom-call(f32[8,192]{1,0:T(8,128)S(1)} %get-tuple-element.69.refs_0_, f32[8,192]{1,0:T(8,128)S(1)} %collective-permute-done.3.refs_1_, f32[8,192]{1,0:T(8,128)S(1)} %collective-permute-done.4.refs_2_, ...), custom_call_target="tpu_custom_call" | custom-call | flops 1048576 | bytes 1048576 | tf_op jit(solution)/shard_map/pallas_call | solution.py:32
  30.5 4.7 %all-to-all-start.1 = ((bf16[8,272,128]{2,1,0:T(8,128)(2,1)}), bf16[8,272,128]{2,1,0:T(8,128)(2,1)S(1)}, u32[]{:S(2)}, u32[]{:S(2)}) async-start(bf16[8,272,128]{2,1,0:T(8,128)(2,1)} %bitcast.34), calls=%async_computation.1 | async-start | bytes 1114112 | tf_op jit(solution)/shard_map/all_to_all | solution.py:682
  35.2 1.0 %shard_map.245 = (bf16[32,512]{1,0:T(8,128)(2,1)S(1)}, bf16[32,512]{1,0:T(8,128)(2,1)S(1)}, bf16[32,512]{1,0:T(8,128)(2,1)S(1)}, bf16[32,512]{1,0:T(8,128)(2,1)S(1)}) custom-call(bf16[8,4,2048]{2,1,0:T(4,128)(2,1)} %refs_0_.5, f32[16,512]{1,0:T(8,128)S(1)} %get-tuple-element.43.refs_0_.refs_4_.refs_3_.refs_6_.refs_12_.refs_1_.refs_13_, ...), custom_call_target="tpu_custom_call" | custom-call | flops 1048576 | bytes 1048576 | tf_op jit(solution)/shard_map/pallas_call | solution.py:32
  36.2 0.2 collective-permute-start.6
  36.4 1.4 %collective-permute-start.7 = (bf16[32,512]{1,0:T(8,128)(2,1)S(1)}, bf16[32,512]{1,0:T(8,128)(2,1)S(1)}, u32[]{:S(2)}, u32[]{:S(2)}) collective-permute-start(bf16[32,512]{1,0:T(8,128)(2,1)S(1)} %get-tuple-element.78), channel_id=1, source_target_pairs={{0,2},{1,3},{2,0},{3,1},{4,6},{5,7},{6,4},{7,5},{8,10},{9,11},{10,... | collective-permute-start | bytes 98312 | tf_op jit(solution)/shard_map/ppermute | solution.py:836
  37.8 0.3 collective-permute-start.8
  38.1 0.0 collective-permute-done.6.refs_1_
  38.1 2.2 %collective-permute-done.7.refs_2_ = bf16[32,512]{1,0:T(8,128)(2,1)S(1)} collective-permute-done((bf16[32,512]{1,0:T(8,128)(2,1)S(1)}, bf16[32,512]{1,0:T(8,128)(2,1)S(1)}, u32[]{:S(2)}, u32[]{:S(2)}) %collective-permute-start.7) | collective-permute-done | bytes 32800 | tf_op jit(solution)/shard_map/ppermute | solution.py:836
  40.3 0.8 %collective-permute-done.8.refs_3_ = bf16[32,512]{1,0:T(8,128)(2,1)S(1)} collective-permute-done((bf16[32,512]{1,0:T(8,128)(2,1)S(1)}, bf16[32,512]{1,0:T(8,128)(2,1)S(1)}, u32[]{:S(2)}, u32[]{:S(2)}) %collective-permute-start.8) | collective-permute-done | bytes 32800 | tf_op jit(solution)/shard_map/ppermute | solution.py:836
  41.2 4.1 %shard_map.246 = bf16[128,512]{1,0:T(8,128)(2,1)} custom-call(bf16[32,512]{1,0:T(8,128)(2,1)S(1)} %get-tuple-element.76.refs_0_, bf16[32,512]{1,0:T(8,128)(2,1)S(1)} %collective-permute-done.6.refs_1_, bf16[32,512]{1,0:T(8,128)(2,1)S(1)} %collective-permute-done.7.refs_2_, bf16[32,512]{1,0:T(8,128)(2,1)S(1)} %collective-permute-done.8.refs_3_, ...), custom_call_target="tpu_custom_call" | custom-call | flops 1048576 | bytes 1048576 | tf_op jit(solution)/shard_map/pallas_call | solution.py:32
  45.3 2.7 %all-to-all-done.1 = bf16[8,272,128]{2,1,0:T(8,128)(2,1)S(1)} async-done(((bf16[8,272,128]{2,1,0:T(8,128)(2,1)}), bf16[8,272,128]{2,1,0:T(8,128)(2,1)S(1)}, u32[]{:S(2)}, u32[]{:S(2)}) %all-to-all-start.1) | async-done | bytes 557088 | tf_op jit(solution)/shard_map/all_to_all | solution.py:682
  47.9 1.5 %shard_map.247 = (f32[128,2048]{1,0:T(8,128)}, f32[32,128]{1,0:T(8,128)}) custom-call(bf16[128,128]{1,0:T(8,128)(2,1)S(1)} %get-tuple-element.59.refs_12_.refs_23_.refs_20_.refs_11_.refs_15_.refs_0_, bf16[136,16,128]{2,1,0:T(8,128)(2,1)S(1)} %bitcast.31), custom_call_target="tpu_custom_call" | custom-call | flops 1048576 | bytes 1048576 | tf_op jit(solution)/shard_map/pallas_call | solution.py:32
Async XLA Ops:
  3.4 21.0 %all-to-all-start = ((bf16[8,272,128]{2,1,0:T(8,128)(2,1)}), bf16[8,272,128]{2,1,0:T(8,128)(2,1)S(1)}, u32[]{:S(2)}, u32[]{:S(2)}) async-start(bf16[8,272,128]{2,1,0:T(8,128)(2,1)} %bitcast.32), calls=%async_computation | async-start | bytes 1114112 | tf_op jit(solution)/shard_map/all_to_all | solution.py:682
  13.0 4.4 %collective-permute-start.2 = (bf16[128,192]{1,0:T(8,128)(2,1)S(1)}, bf16[128,192]{1,0:T(8,128)(2,1)S(1)}, u32[]{:S(2)}, u32[]{:S(2)}) collective-permute-start(bf16[128,192]{1,0:T(8,128)(2,1)S(1)} %get-tuple-element.55.refs_0_), channel_id=1, source_target_pairs={{0,3},{1,2},{2,1},{3,0},{4,7},{5,6},{6,5},{7,4},{8,11},{9,10},{10,... | collective-permute-start | bytes 147464 | tf_op jit(solution)/shard_map/ppermute | solution.py:739
  13.4 5.4 %collective-permute-start.1 = (bf16[128,192]{1,0:T(8,128)(2,1)S(1)}, bf16[128,192]{1,0:T(8,128)(2,1)S(1)}, u32[]{:S(2)}, u32[]{:S(2)}) collective-permute-start(bf16[128,192]{1,0:T(8,128)(2,1)S(1)} %get-tuple-element.55.refs_0_), channel_id=1, source_target_pairs={{0,2},{1,3},{2,0},{3,1},{4,6},{5,7},{6,4},{7,5},{8,10},{9,11},{10,... | collective-permute-start | bytes 147464 | tf_op jit(solution)/shard_map/ppermute | solution.py:739
  14.6 4.2 %collective-permute-start = (bf16[128,192]{1,0:T(8,128)(2,1)S(1)}, bf16[128,192]{1,0:T(8,128)(2,1)S(1)}, u32[]{:S(2)}, u32[]{:S(2)}) collective-permute-start(bf16[128,192]{1,0:T(8,128)(2,1)S(1)} %get-tuple-element.55.refs_0_), channel_id=1, source_target_pairs={{0,1},{1,0},{2,3},{3,2},{4,5},{5,4},{6,7},{7,6},{8,9},{9,8},{10,11... | collective-permute-start | bytes 147464 | tf_op jit(solution)/shard_map/ppermute | solution.py:739
  24.8 3.1 %collective-permute-start.5 = (f32[8,192]{1,0:T(8,128)S(1)}, f32[8,192]{1,0:T(8,128)S(1)}, u32[]{:S(2)}, u32[]{:S(2)}) collective-permute-start(f32[8,192]{1,0:T(8,128)S(1)} %get-tuple-element.69.refs_0_), channel_id=1, source_target_pairs={{0,3},{1,2},{2,1},{3,0},{4,7},{5,6},{6,5},{7,4},{8,11},{9,10},{10,... | collective-permute-start | bytes 18440 | tf_op jit(solution)/shard_map/ppermute | solution.py:739
  24.8 3.7 %collective-permute-start.4 = (f32[8,192]{1,0:T(8,128)S(1)}, f32[8,192]{1,0:T(8,128)S(1)}, u32[]{:S(2)}, u32[]{:S(2)}) collective-permute-start(f32[8,192]{1,0:T(8,128)S(1)} %get-tuple-element.69.refs_0_), channel_id=1, source_target_pairs={{0,2},{1,3},{2,0},{3,1},{4,6},{5,7},{6,4},{7,5},{8,10},{9,11},{10,... | collective-permute-start | bytes 18440 | tf_op jit(solution)/shard_map/ppermute | solution.py:739
  26.4 2.2 %collective-permute-start.3 = (f32[8,192]{1,0:T(8,128)S(1)}, f32[8,192]{1,0:T(8,128)S(1)}, u32[]{:S(2)}, u32[]{:S(2)}) collective-permute-start(f32[8,192]{1,0:T(8,128)S(1)} %get-tuple-element.69.refs_0_), channel_id=1, source_target_pairs={{0,1},{1,0},{2,3},{3,2},{4,5},{5,4},{6,7},{7,6},{8,9},{9,8},{10,11... | collective-permute-start | bytes 18440 | tf_op jit(solution)/shard_map/ppermute | solution.py:739
  30.5 17.4 %all-to-all-start.1 = ((bf16[8,272,128]{2,1,0:T(8,128)(2,1)}), bf16[8,272,128]{2,1,0:T(8,128)(2,1)S(1)}, u32[]{:S(2)}, u32[]{:S(2)}) async-start(bf16[8,272,128]{2,1,0:T(8,128)(2,1)} %bitcast.34), calls=%async_computation.1 | async-start | bytes 1114112 | tf_op jit(solution)/shard_map/all_to_all | solution.py:682
  36.2 1.9 %collective-permute-start.6 = (bf16[32,512]{1,0:T(8,128)(2,1)S(1)}, bf16[32,512]{1,0:T(8,128)(2,1)S(1)}, u32[]{:S(2)}, u32[]{:S(2)}) collective-permute-start(bf16[32,512]{1,0:T(8,128)(2,1)S(1)} %get-tuple-element.77), channel_id=1, source_target_pairs={{0,1},{1,0},{2,3},{3,2},{4,5},{5,4},{6,7},{7,6},{8,9},{9,8},{10,11... | collective-permute-start | bytes 98312 | tf_op jit(solution)/shard_map/ppermute | solution.py:836
  36.4 3.9 %collective-permute-start.7 = (bf16[32,512]{1,0:T(8,128)(2,1)S(1)}, bf16[32,512]{1,0:T(8,128)(2,1)S(1)}, u32[]{:S(2)}, u32[]{:S(2)}) collective-permute-start(bf16[32,512]{1,0:T(8,128)(2,1)S(1)} %get-tuple-element.78), channel_id=1, source_target_pairs={{0,2},{1,3},{2,0},{3,1},{4,6},{5,7},{6,4},{7,5},{8,10},{9,11},{10,... | collective-permute-start | bytes 98312 | tf_op jit(solution)/shard_map/ppermute | solution.py:836
  37.8 3.3 %collective-permute-start.8 = (bf16[32,512]{1,0:T(8,128)(2,1)S(1)}, bf16[32,512]{1,0:T(8,128)(2,1)S(1)}, u32[]{:S(2)}, u32[]{:S(2)}) collective-permute-start(bf16[32,512]{1,0:T(8,128)(2,1)S(1)} %get-tuple-element.79), channel_id=1, source_target_pairs={{0,3},{1,2},{2,1},{3,0},{4,7},{5,6},{6,5},{7,4},{8,11},{9,10},{10,... | collective-permute-start | bytes 98312 | tf_op jit(solution)/shard_map/ppermute | solution.py:836

commit v5 on v4

--- a/solution.py
+++ b/solution.py
@@ -67,7 +67,7 @@
 
 
 def order_of(blocks):
-    return (2, 3, 1, 0, 4, 5, 7, 6) if blocks == 8 else tuple(range(blocks))
+    return (4, 5, 7, 6, 2, 3, 1, 0) if blocks == 8 else tuple(range(blocks))
 
 
 def seat_of(block, blocks):
@@ -347,7 +347,7 @@
     (
         vector_ref, right_decay_ref, right_rate_ref, key_ref, unit_ref, value_t_ref, index_near_ref,
         a_ref, k_ref, b_ref, scale_ref, key_mod_ref, last_ref, solve_ref, through_ref, added_ref,
-        cross, compact, cum_ref, k_low_ref, b_low_ref, index_ref, index_sem,
+        cross, compact, cum_ref, k_low_ref, b_low_ref, a_t_ref, left_ref, left_low_ref, index_ref, index_sem,
     ) = refs[groups:]
     index_copy = pltpu.make_async_copy(index_near_ref, index_ref, index_sem)
     index_copy.start()
@@ -376,8 +376,9 @@
         shift *= 2
     grow = jnp.where(later, jnp.exp(-cum), 0.0)
     cum_ref[...] = cum
-    scale_ref[...] = jnp.exp(cum).astype(BF16)
-    a_ref[...] = jnp.where(later, unit * jnp.exp(cum - log_forget), 0.0).astype(BF16)
+    scale = jnp.exp(cum)
+    scale_ref[...] = scale.astype(BF16)
+    a_ref[...] = jnp.where(later, unit * pltpu.roll(scale, 1, 0), 0.0).astype(BF16)
     k_ref[...], k_low_ref[...] = split(key_mod * grow)
     b_ref[...], b_low_ref[...] = split(rate * unit * grow)
     ident = ident_of(head_width, width)
@@ -390,6 +391,7 @@
         last_ref[p : p + 1, :] = jnp.where(n > 0, jnp.exp(at_n), 1.0)
         right = jnp.concatenate([expand(k_ref[cut, :], head_width), expand(b_ref[cut, :], head_width)], axis=0)
         cross[p] = dot(a_ref[cut, :], right, NT)
+        a_t_ref[p] = dot(ident, expand(a_ref[cut, :], head_width), NT).astype(BF16)
     lane = lax.broadcasted_iota(I32, (requests, lanes), 1)
     source = lane % steps
     group = lane - source
@@ -409,11 +411,9 @@
         solve_ref[0, t] = solve_t
         solve_ref[1, t] = carry_t
     for p in range(requests):
-        cut = slice(p * steps, (p + 1) * steps)
         n = index_ref[3, p]
-        a_t = dot(ident, expand(a_ref[cut, :], head_width), NT).astype(BF16)
         value_t = value_t_ref[p]
-        reach = dot(a_t, spread(compact[0, p].astype(BF16), steps), NT)
+        reach = dot(a_t_ref[p], spread(compact[0, p].astype(BF16), steps), NT)
         high, low = split(compact[1, p])
         removed = dot(value_t, spread(high, steps), NT) + dot(value_t, spread(low, steps), NT)
         left = jnp.concatenate(
@@ -424,7 +424,10 @@
             axis=0,
         )
         at = lax.broadcasted_iota(I32, left.shape, 1) % steps
-        left, left_low = split(jnp.where(at < n, left, 0.0))
+        left_ref[p], left_low_ref[p] = split(jnp.where(at < n, left, 0.0))
+    for p in range(requests):
+        cut = slice(p * steps, (p + 1) * steps)
+        left, left_low = left_ref[p], left_low_ref[p]
         right = jnp.concatenate([expand(b_ref[cut, :], head_width), expand(k_ref[cut, :], head_width)], axis=0)
         right_low = jnp.concatenate([expand(b_low_ref[cut, :], head_width), expand(k_low_ref[cut, :], head_width)], axis=0)
         both = (dot(left, right) + dot(left_low, right) + dot(left, right_low)) * last_ref[p : p + 1, :]
@@ -778,6 +781,9 @@
             pltpu.VMEM((rows, width), F32),
             pltpu.VMEM((rows, width), BF16),
             pltpu.VMEM((rows, width), BF16),
+            pltpu.VMEM((requests, head_width, heads * steps), BF16),
+            pltpu.VMEM((requests, 2 * head_width, 2 * heads * steps), BF16),
+            pltpu.VMEM((requests, 2 * head_width, 2 * heads * steps), BF16),
             pltpu.SMEM((8, slot_dev), I32),
             pltpu.SemaphoreType.DMA,
         ],

time: 49.9 us -> 48.9 us (0.980)
  Pallas kernels: 20.9 us -> 19.9 us
  starting transfers between devices: 18.3 us -> 19.2 us
  waiting for transfers between devices: 9.56 us -> 8.72 us
    pallas_call x10, Pallas kernels: 20.9 us -> 19.9 us  [call(): pl.pallas_call(body, out_shape=outs, in_specs=specs, out_specs=tuple((pl....]
    all_to_all x2, starting transfers between devices: 12.5 us -> 13.5 us  [exchange(): lax.all_to_all(x, axis, split_axis=0, concat_axis=0, tiled=True, axis_ind...]
    all_to_all x2, waiting for transfers between devices: 3.82 us -> 2.98 us  [exchange(): lax.all_to_all(x, axis, split_axis=0, concat_axis=0, tiled=True, axis_ind...]
  transfers between devices with their start and end apart: 11 -> 11, of which waited for: 8 -> 8; matrix products, arithmetic and copies ran while one was open for 0% -> 0% of each run, Pallas kernels for 29% -> 27%
where the time goes in v5:
time: 48.9 us; the launch traced here: 48.5 us
  Pallas kernels  19.9 us (41%)
  starting transfers between devices  19.2 us (39%)
  waiting for transfers between devices  8.72 us (18%)
  between operations  0.69 us (1%)
    pallas_call x10, Pallas kernels, call(): pl.pallas_call(body, out_shape=outs, in_specs=specs, out_specs=tuple((pl....  19.9 us
    all_to_all x2, starting transfers between devices, exchange(): lax.all_to_all(x, axis, split_axis=0, concat_axis=0, tiled=True, axis_ind...  13.5 us
    ppermute x6, starting transfers between devices, from_group(): lax.ppermute(x, 'head', [(g, g ^ d) for g in range(groups)])  3.81 us
    ppermute x3, waiting for transfers between devices, local(): lax.ppermute(recept[d], 'head', [(g, g ^ d) for g in range(groups)])  3.05 us
    all_to_all x2, waiting for transfers between devices, exchange(): lax.all_to_all(x, axis, split_axis=0, concat_axis=0, tiled=True, axis_ind...  2.98 us
    ppermute x6, waiting for transfers between devices, from_group(): lax.ppermute(x, 'head', [(g, g ^ d) for g in range(groups)])  2.69 us
    ppermute x3, starting transfers between devices, local(): lax.ppermute(recept[d], 'head', [(g, g ^ d) for g in range(groups)])  1.93 us
  transfers between devices with their start and end apart: 11, of which 8 were waited for; matrix products, arithmetic and copies ran while one was open for 0% of the time, Pallas kernels for 27%

profile of v5, /device:TPU:0, one launch (start us, length us, event | category | flops | bytes accessed | tf_op | source)
XLA Modules:
  0.0 48.5 jit_solution(8818012615309298785)
XLA Ops:
  0.6 2.8 %shard_map.240 = bf16[136,16,128]{2,1,0:T(8,128)(2,1)} custom-call(s32[64]{0:T(128)} %refs_0_.4, s32[8,2,64]{2,1,0:T(2,128)} %bitcast.42, f32[128,2048]{1,0:T(8,128)} %bitcast.33, f32[32,128]{1,0:T(8,128)} %bitcast.44), custom_call_target="tpu_custom_call" | custom-call | flops 1048576 | bytes 1048576 | tf_op jit(solution)/shard_map/pallas_call | solution.py:32
  3.4 7.9 %all-to-all-start = ((bf16[8,272,128]{2,1,0:T(8,128)(2,1)}), bf16[8,272,128]{2,1,0:T(8,128)(2,1)S(1)}, u32[]{:S(2)}, u32[]{:S(2)}) async-start(bf16[8,272,128]{2,1,0:T(8,128)(2,1)} %bitcast.32), calls=%async_computation | async-start | bytes 1114112 | tf_op jit(solution)/shard_map/all_to_all | solution.py:685
  11.3 1.7 %shard_map.238 = (bf16[128,192]{1,0:T(8,128)(2,1)S(1)}, f32[8,512]{1,0:T(8,128)S(1)}, f32[8,512]{1,0:T(8,128)S(1)}, f32[16,512]{1,0:T(8,128)S(1)}, bf16[96,512]{...) custom-call(s32[64]{0:T(128)} %refs_0_.4, ...), custom_call_target="tpu_custom_call" | custom-call | flops 1048576 | bytes 1048576 | tf_op jit(solution)/shard_map/pallas_call | solution.py:32
  13.0 0.4 collective-permute-start.2
  13.4 1.2 %collective-permute-start.1 = (bf16[128,192]{1,0:T(8,128)(2,1)S(1)}, bf16[128,192]{1,0:T(8,128)(2,1)S(1)}, u32[]{:S(2)}, u32[]{:S(2)}) collective-permute-start(bf16[128,192]{1,0:T(8,128)(2,1)S(1)} %get-tuple-element.55.refs_0_), channel_id=1, source_target_pairs={{0,2},{1,3},{2,0},{3,1},{4,6},{5,7},{6,4},{7,5},{8,10},{9,11},{10,... | collective-permute-start | bytes 147464 | tf_op jit(solution)/shard_map/ppermute | solution.py:742
  14.6 0.3 collective-permute-start
  14.9 1.9 %shard_map.239 = (s32[8,128]{1,0:T(8,128)S(1)}, bf16[128,128]{1,0:T(8,128)(2,1)S(1)}, bf16[128,128]{1,0:T(8,128)(2,1)S(1)}, bf16[128,512]{1,0:T(8,128)(2,1)S(1)}...) custom-call(f32[16,512]{1,0:T(8,128)S(1)} %get-tuple-element.43.refs, ...), custom_call_target="tpu_custom_call" | custom-call | flops 1048576 | bytes 1048576 | tf_op jit(solution)/shard_map/pallas_call | solution.py:32
  16.8 0.6 %collective-permute-done.2.refs_3_ = bf16[128,192]{1,0:T(8,128)(2,1)S(1)} collective-permute-done((bf16[128,192]{1,0:T(8,128)(2,1)S(1)}, bf16[128,192]{1,0:T(8,128)(2,1)S(1)}, u32[]{:S(2)}, u32[]{:S(2)}) %collective-permute-start.2) | collective-permute-done | bytes 49184 | tf_op jit(solution)/shard_map/ppermute | solution.py:742
  17.4 1.4 %collective-permute-done.1.refs_2_ = bf16[128,192]{1,0:T(8,128)(2,1)S(1)} collective-permute-done((bf16[128,192]{1,0:T(8,128)(2,1)S(1)}, bf16[128,192]{1,0:T(8,128)(2,1)S(1)}, u32[]{:S(2)}, u32[]{:S(2)}) %collective-permute-start.1) | collective-permute-done | bytes 49184 | tf_op jit(solution)/shard_map/ppermute | solution.py:742
  18.8 0.0 collective-permute-done.refs_1_
  18.8 3.3 %shard_map.241 = (bf16[128,512]{1,0:T(8,128)(2,1)S(1)}, bf16[128,512]{1,0:T(8,128)(2,1)S(1)}, bf16[128,512]{1,0:T(8,128)(2,1)S(1)}, bf16[128,512]{1,0:T(8,128)(2...) custom-call(bf16[128,192]{1,0:T(8,128)(2,1)S(1)} %get-tuple-element., ...), custom_call_target="tpu_custom_call" | custom-call | flops 1048576 | bytes 1048576 | tf_op jit(solution)/shard_map/pallas_call | solution.py:32
  22.2 1.3 %all-to-all-done = bf16[8,272,128]{2,1,0:T(8,128)(2,1)S(1)} async-done(((bf16[8,272,128]{2,1,0:T(8,128)(2,1)}), bf16[8,272,128]{2,1,0:T(8,128)(2,1)S(1)}, u32[]{:S(2)}, u32[]{:S(2)}) %all-to-all-start) | async-done | bytes 557088 | tf_op jit(solution)/shard_map/all_to_all | solution.py:685
  23.5 0.4 shard_map.242
  23.9 0.0 collective-permute-start.5
  23.9 1.5 %collective-permute-start.4 = (f32[8,192]{1,0:T(8,128)S(1)}, f32[8,192]{1,0:T(8,128)S(1)}, u32[]{:S(2)}, u32[]{:S(2)}) collective-permute-start(f32[8,192]{1,0:T(8,128)S(1)} %get-tuple-element.69.refs_0_), channel_id=1, source_target_pairs={{0,2},{1,3},{2,0},{3,1},{4,6},{5,7},{6,4},{7,5},{8,10},{9,11},{10,... | collective-permute-start | bytes 18440 | tf_op jit(solution)/shard_map/ppermute | solution.py:742
  25.5 0.3 collective-permute-start.3
  25.8 1.1 %shard_map.243 = (bf16[8,64,512]{2,1,0:T(8,128)(2,1)S(1)}, bf16[8,64,16]{2,1,0:T(8,128)(2,1)S(1)}, bf16[8,16,128]{2,1,0:T(8,128)(2,1)S(1)}) custom-call(s32[8,128]{1,0:T(8,128)S(1)} %get-tuple-element.51.refs_10_.refs_6_.refs_0_.refs_15_, bf16[136,16,128]{2,1,0:T(8,128)(2,1)S(1)} %bitcast.30, f32[8,512]{1,0:T(8,128)S(1)} %get-tuple-element.52.refs_17_.refs_7_.refs_2_, ...), custom_call_target="tpu_custom_call" | custom-call | flops 1048576 | bytes 1048576 | tf_op jit(solution)/shard_map/pallas_call | solution.py:32
  27.0 0.1 collective-permute-done.5.refs_3_
  27.1 0.6 %collective-permute-done.4.refs_2_ = f32[8,192]{1,0:T(8,128)S(1)} collective-permute-done((f32[8,192]{1,0:T(8,128)S(1)}, f32[8,192]{1,0:T(8,128)S(1)}, u32[]{:S(2)}, u32[]{:S(2)}) %collective-permute-start.4) | collective-permute-done | bytes 6176 | tf_op jit(solution)/shard_map/ppermute | solution.py:742
  27.6 0.0 collective-permute-done.3.refs_1_
  27.7 2.0 %shard_map.244 = (bf16[136,16,128]{2,1,0:T(8,128)(2,1)}, bf16[8,64,512]{2,1,0:T(8,128)(2,1)S(1)}, f32[8,512]{1,0:T(8,128)S(1)}) custom-call(f32[8,192]{1,0:T(8,128)S(1)} %get-tuple-element.69.refs_0_, f32[8,192]{1,0:T(8,128)S(1)} %collective-permute-done.3.refs_1_, f32[8,192]{1,0:T(8,128)S(1)} %collective-permute-done.4.refs_2_, ...), custom_call_target="tpu_custom_call" | custom-call | flops 1048576 | bytes 1048576 | tf_op jit(solution)/shard_map/pallas_call | solution.py:32
  29.6 5.6 %all-to-all-start.1 = ((bf16[8,272,128]{2,1,0:T(8,128)(2,1)}), bf16[8,272,128]{2,1,0:T(8,128)(2,1)S(1)}, u32[]{:S(2)}, u32[]{:S(2)}) async-start(bf16[8,272,128]{2,1,0:T(8,128)(2,1)} %bitcast.34), calls=%async_computation.1 | async-start | bytes 1114112 | tf_op jit(solution)/shard_map/all_to_all | solution.py:685
  35.2 1.0 %shard_map.245 = (bf16[32,512]{1,0:T(8,128)(2,1)S(1)}, bf16[32,512]{1,0:T(8,128)(2,1)S(1)}, bf16[32,512]{1,0:T(8,128)(2,1)S(1)}, bf16[32,512]{1,0:T(8,128)(2,1)S(1)}) custom-call(bf16[8,4,2048]{2,1,0:T(4,128)(2,1)} %refs_0_.5, f32[16,512]{1,0:T(8,128)S(1)} %get-tuple-element.43.refs_0_.refs_4_.refs_3_.refs_6_.refs_12_.refs_1_.refs_13_, ...), custom_call_target="tpu_custom_call" | custom-call | flops 1048576 | bytes 1048576 | tf_op jit(solution)/shard_map/pallas_call | solution.py:32
  36.2 0.2 collective-permute-start.6
  36.4 1.4 %collective-permute-start.7 = (bf16[32,512]{1,0:T(8,128)(2,1)S(1)}, bf16[32,512]{1,0:T(8,128)(2,1)S(1)}, u32[]{:S(2)}, u32[]{:S(2)}) collective-permute-start(bf16[32,512]{1,0:T(8,128)(2,1)S(1)} %get-tuple-element.78), channel_id=1, source_target_pairs={{0,2},{1,3},{2,0},{3,1},{4,6},{5,7},{6,4},{7,5},{8,10},{9,11},{10,... | collective-permute-start | bytes 98312 | tf_op jit(solution)/shard_map/ppermute | solution.py:842
  37.8 0.3 collective-permute-start.8
  38.1 0.0 collective-permute-done.6.refs_1_
  38.1 2.2 %collective-permute-done.7.refs_2_ = bf16[32,512]{1,0:T(8,128)(2,1)S(1)} collective-permute-done((bf16[32,512]{1,0:T(8,128)(2,1)S(1)}, bf16[32,512]{1,0:T(8,128)(2,1)S(1)}, u32[]{:S(2)}, u32[]{:S(2)}) %collective-permute-start.7) | collective-permute-done | bytes 32800 | tf_op jit(solution)/shard_map/ppermute | solution.py:842
  40.4 0.8 %collective-permute-done.8.refs_3_ = bf16[32,512]{1,0:T(8,128)(2,1)S(1)} collective-permute-done((bf16[32,512]{1,0:T(8,128)(2,1)S(1)}, bf16[32,512]{1,0:T(8,128)(2,1)S(1)}, u32[]{:S(2)}, u32[]{:S(2)}) %collective-permute-start.8) | collective-permute-done | bytes 32800 | tf_op jit(solution)/shard_map/ppermute | solution.py:842
  41.2 4.1 %shard_map.246 = bf16[128,512]{1,0:T(8,128)(2,1)} custom-call(bf16[32,512]{1,0:T(8,128)(2,1)S(1)} %get-tuple-element.76.refs_0_, bf16[32,512]{1,0:T(8,128)(2,1)S(1)} %collective-permute-done.6.refs_1_, bf16[32,512]{1,0:T(8,128)(2,1)S(1)} %collective-permute-done.7.refs_2_, bf16[32,512]{1,0:T(8,128)(2,1)S(1)} %collective-permute-done.8.refs_3_, ...), custom_call_target="tpu_custom_call" | custom-call | flops 1048576 | bytes 1048576 | tf_op jit(solution)/shard_map/pallas_call | solution.py:32
  45.3 1.7 %all-to-all-done.1 = bf16[8,272,128]{2,1,0:T(8,128)(2,1)S(1)} async-done(((bf16[8,272,128]{2,1,0:T(8,128)(2,1)}), bf16[8,272,128]{2,1,0:T(8,128)(2,1)S(1)}, u32[]{:S(2)}, u32[]{:S(2)}) %all-to-all-start.1) | async-done | bytes 557088 | tf_op jit(solution)/shard_map/all_to_all | solution.py:685
  47.0 1.5 %shard_map.247 = (f32[128,2048]{1,0:T(8,128)}, f32[32,128]{1,0:T(8,128)}) custom-call(bf16[128,128]{1,0:T(8,128)(2,1)S(1)} %get-tuple-element.59.refs_12_.refs_23_.refs_20_.refs_11_.refs_15_.refs_0_, bf16[136,16,128]{2,1,0:T(8,128)(2,1)S(1)} %bitcast.31), custom_call_target="tpu_custom_call" | custom-call | flops 1048576 | bytes 1048576 | tf_op jit(solution)/shard_map/pallas_call | solution.py:32
Async XLA Ops:
  3.4 20.1 %all-to-all-start = ((bf16[8,272,128]{2,1,0:T(8,128)(2,1)}), bf16[8,272,128]{2,1,0:T(8,128)(2,1)S(1)}, u32[]{:S(2)}, u32[]{:S(2)}) async-start(bf16[8,272,128]{2,1,0:T(8,128)(2,1)} %bitcast.32), calls=%async_computation | async-start | bytes 1114112 | tf_op jit(solution)/shard_map/all_to_all | solution.py:685
  13.0 4.4 %collective-permute-start.2 = (bf16[128,192]{1,0:T(8,128)(2,1)S(1)}, bf16[128,192]{1,0:T(8,128)(2,1)S(1)}, u32[]{:S(2)}, u32[]{:S(2)}) collective-permute-start(bf16[128,192]{1,0:T(8,128)(2,1)S(1)} %get-tuple-element.55.refs_0_), channel_id=1, source_target_pairs={{0,3},{1,2},{2,1},{3,0},{4,7},{5,6},{6,5},{7,4},{8,11},{9,10},{10,... | collective-permute-start | bytes 147464 | tf_op jit(solution)/shard_map/ppermute | solution.py:742
  13.4 5.4 %collective-permute-start.1 = (bf16[128,192]{1,0:T(8,128)(2,1)S(1)}, bf16[128,192]{1,0:T(8,128)(2,1)S(1)}, u32[]{:S(2)}, u32[]{:S(2)}) collective-permute-start(bf16[128,192]{1,0:T(8,128)(2,1)S(1)} %get-tuple-element.55.refs_0_), channel_id=1, source_target_pairs={{0,2},{1,3},{2,0},{3,1},{4,6},{5,7},{6,4},{7,5},{8,10},{9,11},{10,... | collective-permute-start | bytes 147464 | tf_op jit(solution)/shard_map/ppermute | solution.py:742
  14.6 4.2 %collective-permute-start = (bf16[128,192]{1,0:T(8,128)(2,1)S(1)}, bf16[128,192]{1,0:T(8,128)(2,1)S(1)}, u32[]{:S(2)}, u32[]{:S(2)}) collective-permute-start(bf16[128,192]{1,0:T(8,128)(2,1)S(1)} %get-tuple-element.55.refs_0_), channel_id=1, source_target_pairs={{0,1},{1,0},{2,3},{3,2},{4,5},{5,4},{6,7},{7,6},{8,9},{9,8},{10,11... | collective-permute-start | bytes 147464 | tf_op jit(solution)/shard_map/ppermute | solution.py:742
  23.9 3.1 %collective-permute-start.5 = (f32[8,192]{1,0:T(8,128)S(1)}, f32[8,192]{1,0:T(8,128)S(1)}, u32[]{:S(2)}, u32[]{:S(2)}) collective-permute-start(f32[8,192]{1,0:T(8,128)S(1)} %get-tuple-element.69.refs_0_), channel_id=1, source_target_pairs={{0,3},{1,2},{2,1},{3,0},{4,7},{5,6},{6,5},{7,4},{8,11},{9,10},{10,... | collective-permute-start | bytes 18440 | tf_op jit(solution)/shard_map/ppermute | solution.py:742
  23.9 3.7 %collective-permute-start.4 = (f32[8,192]{1,0:T(8,128)S(1)}, f32[8,192]{1,0:T(8,128)S(1)}, u32[]{:S(2)}, u32[]{:S(2)}) collective-permute-start(f32[8,192]{1,0:T(8,128)S(1)} %get-tuple-element.69.refs_0_), channel_id=1, source_target_pairs={{0,2},{1,3},{2,0},{3,1},{4,6},{5,7},{6,4},{7,5},{8,10},{9,11},{10,... | collective-permute-start | bytes 18440 | tf_op jit(solution)/shard_map/ppermute | solution.py:742
  25.5 2.2 %collective-permute-start.3 = (f32[8,192]{1,0:T(8,128)S(1)}, f32[8,192]{1,0:T(8,128)S(1)}, u32[]{:S(2)}, u32[]{:S(2)}) collective-permute-start(f32[8,192]{1,0:T(8,128)S(1)} %get-tuple-element.69.refs_0_), channel_id=1, source_target_pairs={{0,1},{1,0},{2,3},{3,2},{4,5},{5,4},{6,7},{7,6},{8,9},{9,8},{10,11... | collective-permute-start | bytes 18440 | tf_op jit(solution)/shard_map/ppermute | solution.py:742
  29.6 17.4 %all-to-all-start.1 = ((bf16[8,272,128]{2,1,0:T(8,128)(2,1)}), bf16[8,272,128]{2,1,0:T(8,128)(2,1)S(1)}, u32[]{:S(2)}, u32[]{:S(2)}) async-start(bf16[8,272,128]{2,1,0:T(8,128)(2,1)} %bitcast.34), calls=%async_computation.1 | async-start | bytes 1114112 | tf_op jit(solution)/shard_map/all_to_all | solution.py:685
  36.2 1.9 %collective-permute-start.6 = (bf16[32,512]{1,0:T(8,128)(2,1)S(1)}, bf16[32,512]{1,0:T(8,128)(2,1)S(1)}, u32[]{:S(2)}, u32[]{:S(2)}) collective-permute-start(bf16[32,512]{1,0:T(8,128)(2,1)S(1)} %get-tuple-element.77), channel_id=1, source_target_pairs={{0,1},{1,0},{2,3},{3,2},{4,5},{5,4},{6,7},{7,6},{8,9},{9,8},{10,11... | collective-permute-start | bytes 98312 | tf_op jit(solution)/shard_map/ppermute | solution.py:842
  36.4 3.9 %collective-permute-start.7 = (bf16[32,512]{1,0:T(8,128)(2,1)S(1)}, bf16[32,512]{1,0:T(8,128)(2,1)S(1)}, u32[]{:S(2)}, u32[]{:S(2)}) collective-permute-start(bf16[32,512]{1,0:T(8,128)(2,1)S(1)} %get-tuple-element.78), channel_id=1, source_target_pairs={{0,2},{1,3},{2,0},{3,1},{4,6},{5,7},{6,4},{7,5},{8,10},{9,11},{10,... | collective-permute-start | bytes 98312 | tf_op jit(solution)/shard_map/ppermute | solution.py:842
  37.8 3.3 %collective-permute-start.8 = (bf16[32,512]{1,0:T(8,128)(2,1)S(1)}, bf16[32,512]{1,0:T(8,128)(2,1)S(1)}, u32[]{:S(2)}, u32[]{:S(2)}) collective-permute-start(bf16[32,512]{1,0:T(8,128)(2,1)S(1)} %get-tuple-element.79), channel_id=1, source_target_pairs={{0,3},{1,2},{2,1},{3,0},{4,7},{5,6},{6,5},{7,4},{8,11},{9,10},{10,... | collective-permute-start | bytes 98312 | tf_op jit(solution)/shard_map/ppermute | solution.py:842

commit v6 on v5

--- a/solution.py
+++ b/solution.py
@@ -140,7 +140,7 @@
     blocks, requests, per_peer, pieces,
     seq_hbm, read_hbm, state_hbm, edge_hbm,
     out_hbm,
-    seq_ref, read_ref, state_ref, edge_ref, flat, scratch, edge_scratch, out_ref, sems, state_sems, out_sems,
+    seq_ref, read_ref, state_ref, edge_ref, flat, edge_scratch, out_ref, sems, state_sems, out_sems,
 ):
     slot_dev, slot_width = state_ref.shape
     pack = out_ref.shape[1]
@@ -173,24 +173,28 @@
         y = dot(pick, state_ref[:, (half + b) * 128 : (half + b + 1) * 128].astype(BF16))
         flat[:, 2 * b * 128 : (2 * b + 1) * 128] = jnp.where(left, x, pltpu.roll(y, 64, 1))
         flat[:, (2 * b + 1) * 128 : (2 * b + 2) * 128] = jnp.where(left, pltpu.roll(x, 64, 1), y)
-    for row in range(0, slot_dev, 8):
-        for j in range(0, pack, 8):
-            tiles = [flat[row : row + 8, i * 128 : (i + 1) * 128] for i in range(j, j + 8)]
-            scratch[row : row + 8, j : j + 8, :] = jnp.swapaxes(jnp.stack(tiles), 0, 1)
     copies[2].wait()
     edge_rows = edge_ref.shape[0]
     edges = jnp.concatenate([edge_ref[...], jnp.zeros((slot_dev - edge_rows, slot_dev), F32)], axis=0)
     edge_scratch[...] = dot(pick, edges.astype(BF16), NT)
     out_copies = []
-    for b in range(blocks):
-        at = b * (per_peer + 1)
-        out_ref[at : at + per_peer] = scratch[b * per_peer : (b + 1) * per_peer].astype(BF16)
-        block = edge_scratch[b * per_peer : (b + 1) * per_peer, :]
-        if per_peer < pack:
-            block = jnp.concatenate([block, jnp.zeros((pack - per_peer, 128), F32)], axis=0)
-        out_ref[at + per_peer] = block.astype(BF16)
-        if (b + 1) % (blocks // 8) == 0:
-            cut = pl.ds((b + 1 - blocks // 8) * (per_peer + 1), blocks // 8 * (per_peer + 1))
+    for row in range(0, slot_dev, 8):
+        parts = []
+        for j in range(0, pack, 8):
+            tiles = [flat[row : row + 8, i * 128 : (i + 1) * 128] for i in range(j, j + 8)]
+            parts.append(jnp.swapaxes(jnp.stack(tiles), 0, 1))
+        for i in range(8):
+            place = row + i
+            block = jnp.concatenate([part[i] for part in parts], axis=0)
+            out_ref[place + place // per_peer] = block.astype(BF16)
+        if (row + 8) % (slot_dev // 8) == 0:
+            first, last = (row + 8) * 8 // slot_dev * (blocks // 8) - blocks // 8, (row + 8) * 8 // slot_dev * (blocks // 8)
+            for b in range(first, last):
+                block = edge_scratch[b * per_peer : (b + 1) * per_peer, :]
+                if per_peer < pack:
+                    block = jnp.concatenate([block, jnp.zeros((pack - per_peer, 128), F32)], axis=0)
+                out_ref[b * (per_peer + 1) + per_peer] = block.astype(BF16)
+            cut = pl.ds(first * (per_peer + 1), (last - first) * (per_peer + 1))
             out_copies.append(pltpu.make_async_copy(out_ref.at[cut], out_hbm.at[cut], out_sems.at[len(out_copies)]))
             out_copies[-1].start()
     for copy in out_copies:
@@ -377,7 +381,7 @@
     grow = jnp.where(later, jnp.exp(-cum), 0.0)
     cum_ref[...] = cum
     scale = jnp.exp(cum)
-    scale_ref[...] = scale.astype(BF16)
+    scale_ref[...] = scale
     a_ref[...] = jnp.where(later, unit * pltpu.roll(scale, 1, 0), 0.0).astype(BF16)
     k_ref[...], k_low_ref[...] = split(key_mod * grow)
     b_ref[...], b_low_ref[...] = split(rate * unit * grow)
@@ -444,15 +448,21 @@
 
 def layout_kernel(
     requests, heads, halves, per_peer,
-    index_ref, got_ref, unit_first_ref, value_first_ref, edge_ref, picked_ref,
-    state_ref, change_ref, edge_out_ref, edge_scratch,
+    got_ref, unit_first_ref, value_first_ref, edge_ref, picked_ref, index_near_ref,
+    state_ref, change_ref, edge_out_ref, edge_scratch, value_scratch, index_ref, index_sem,
 ):
+    index_copy = pltpu.make_async_copy(index_near_ref, index_ref, index_sem)
+    index_copy.start()
     width = unit_first_ref.shape[1]
     head_width = width // heads
     pack = got_ref.shape[1]
     edge_rows = head_width // halves
     ident = ident_of(head_width, width)
     low = lax.broadcasted_iota(I32, (pack, 128), 1) < head_width
+    for p in range(requests):
+        value = head_rows(value_first_ref[p : p + 1, :], heads, head_width, heads).astype(BF16)
+        value_scratch[p] = dot(ident, value, NT)
+    index_copy.wait()
     for p in range(requests):
         for c in range(halves):
             for pair in range(heads // 2):
@@ -465,8 +475,7 @@
                 state_ref[p, 2 * c * pack : (2 * c + 1) * pack, lanes] = top.astype(BF16)
                 state_ref[p, (2 * c + 1) * pack : (2 * c + 2) * pack, lanes] = bottom.astype(BF16)
         unit = head_rows(unit_first_ref[p : p + 1, :], heads, head_width, 0).astype(BF16)
-        value = head_rows(value_first_ref[p : p + 1, :], heads, head_width, heads).astype(BF16)
-        change_ref[p] = (dot(ident, value, NT) - dot(state_ref[p], unit, NT)).astype(BF16)
+        change_ref[p] = (value_scratch[p] - dot(state_ref[p], unit, NT)).astype(BF16)
         new_edge = jnp.where(index_ref[3, p] > 0, picked_ref[p : p + 1, :], edge_ref[p : p + 1, :])
         for k in range(heads * halves):
             lane = k * edge_rows
@@ -563,7 +572,7 @@
     requests, heads,
     recept_refs, scale_ref, key_mod_ref, key_mod_first_ref, a_ref, k_ref, b_ref, solve_ref, state_ref, value_t_ref,
     vector_ref, value_ref,
-    result_ref, line_scratch, cross, compact, out_scratch,
+    result_ref, line_scratch, low_scratch, cross, compact, out_scratch,
 ):
     rows, width = value_ref.shape
     steps = rows // requests
@@ -579,11 +588,13 @@
     first = lax.broadcasted_iota(I32, (rows, width), 0) % steps == 0
     key_mod = jnp.where(first, key_mod_first, key_mod_ref[...].astype(F32))
     bonus = group_sum(recept * key_mod * vector_ref[6:7, :], head_width)
-    line_scratch[...] = (recept * scale_ref[...].astype(F32)).astype(BF16)
+    line_scratch[...], line_low = split(recept * scale_ref[...])
+    low_scratch[...] = line_low
     for p in range(requests):
         cut = slice(p * steps, (p + 1) * steps)
         right = jnp.concatenate([expand(k_ref[cut, :], head_width), expand(b_ref[cut, :], head_width)], axis=0)
-        cross[p] = dot(line_scratch[cut, :], right, NT)
+        both_parts = dot(jnp.concatenate([line_scratch[cut, :], low_scratch[cut, :]], axis=0), right, NT)
+        cross[p] = both_parts[:steps, :] + both_parts[steps:, :]
     lane = lax.broadcasted_iota(I32, (requests, lanes), 1)
     source = lane % steps
     group = lane - source
@@ -608,6 +619,7 @@
         both = jnp.concatenate([along, value_t_ref[p]], axis=1)
         out = dot(read, jnp.concatenate([both, both], axis=0), NT)
         out = out + dot(expand(line_scratch[cut, :], head_width), jnp.concatenate([state, state], axis=0), NT)
+        out = out + dot(expand(low_scratch[cut, :], head_width), jnp.concatenate([state, state], axis=0), NT)
         for pair in range(heads // 2):
             at = 2 * pair * steps
             out_scratch[cut, pair * 128 : (pair + 1) * 128] = jnp.where(
@@ -700,7 +712,6 @@
             pltpu.VMEM((slot_dev, slot_width), F32),
             pltpu.VMEM((edge_rows, slot_dev), F32),
             pltpu.VMEM((slot_dev, slot_width), F32),
-            pltpu.VMEM((slot_dev, pack, 128), F32),
             pltpu.VMEM((slot_dev, slot_dev), F32),
             pltpu.VMEM((blocks * (per_peer + 1), pack, 128), BF16),
             pltpu.SemaphoreType.DMA((3,)),
@@ -767,7 +778,7 @@
     a_lines, k_lines, b_lines, scale, key_mod, last, solve, through, added = call(
         functools.partial(prepare_kernel, requests, heads, groups),
         (
-            wide, wide, wide, wide, wide, one,
+            wide, wide, wide, sds((rows, width), F32), wide, one,
             sds((2, steps, requests, heads * steps), F32),
             sds((requests, head_width, width), BF16),
             sds((requests, head_width, width), BF16),
@@ -805,10 +816,15 @@
             sds((requests, head_width, 2 * heads), BF16),
             sds((blocks, pack, 128), BF16),
         ),
-        scalars=(index,),
         near=(got, unit_first, value_first, edge, picked),
+        loose=(index,),
         held=(*state_later, *read_later),
-        scratch=[pltpu.VMEM((slot_dev, 128), F32)],
+        scratch=[
+            pltpu.VMEM((slot_dev, 128), F32),
+            pltpu.VMEM((requests, head_width, 2 * heads), F32),
+            pltpu.SMEM((8, slot_dev), I32),
+            pltpu.SemaphoreType.DMA,
+        ],
     )
     back, after, key_mod_first = call(
         functools.partial(state_kernel, requests, heads, halves, per_peer, groups),
@@ -848,6 +864,7 @@
         far=(value,),
         held=(pick_out,),
         scratch=[
+            pltpu.VMEM((rows, width), BF16),
             pltpu.VMEM((rows, width), BF16),
             pltpu.VMEM((requests, steps, 2 * heads * steps), F32),
             pltpu.VMEM((2, requests, steps, heads * steps), F32),

time: 48.9 us -> 48.8 us (level)
  transfers between devices with their start and end apart: 11 -> 11, of which waited for: 8 -> 8; matrix products, arithmetic and copies ran while one was open for 0% -> 0% of each run, Pallas kernels for 27% -> 28%
where the time goes in v6:
time: 48.8 us; the launch traced here: 48.5 us
  Pallas kernels  20.1 us (41%)
  starting transfers between devices  19.2 us (39%)
  waiting for transfers between devices  8.43 us (17%)
  between operations  0.69 us (1%)
    pallas_call x10, Pallas kernels, call(): pl.pallas_call(body, out_shape=outs, in_specs=specs, out_specs=tuple((pl....  20.1 us
    all_to_all x2, starting transfers between devices, exchange(): lax.all_to_all(x, axis, split_axis=0, concat_axis=0, tiled=True, axis_ind...  13.5 us
    ppermute x6, starting transfers between devices, from_group(): lax.ppermute(x, 'head', [(g, g ^ d) for g in range(groups)])  3.81 us
    ppermute x3, waiting for transfers between devices, local(): lax.ppermute(recept[d], 'head', [(g, g ^ d) for g in range(groups)])  3.05 us
    ppermute x6, waiting for transfers between devices, from_group(): lax.ppermute(x, 'head', [(g, g ^ d) for g in range(groups)])  2.76 us
    all_to_all x2, waiting for transfers between devices, exchange(): lax.all_to_all(x, axis, split_axis=0, concat_axis=0, tiled=True, axis_ind...  2.62 us
    ppermute x3, starting transfers between devices, local(): lax.ppermute(recept[d], 'head', [(g, g ^ d) for g in range(groups)])  1.93 us
  transfers between devices with their start and end apart: 11, of which 8 were waited for; matrix products, arithmetic and copies ran while one was open for 0% of the time, Pallas kernels for 28%

profile of v6, /device:TPU:0, one launch (start us, length us, event | category | flops | bytes accessed | tf_op | source)
XLA Modules:
  0.0 48.5 jit_solution(15598045656793021828)
XLA Ops:
  0.6 2.8 %shard_map.240 = bf16[136,16,128]{2,1,0:T(8,128)(2,1)} custom-call(s32[64]{0:T(128)} %refs_0_.4, s32[8,2,64]{2,1,0:T(2,128)} %bitcast.42, f32[128,2048]{1,0:T(8,128)} %bitcast.33, f32[32,128]{1,0:T(8,128)} %bitcast.44), custom_call_target="tpu_custom_call" | custom-call | flops 1048576 | bytes 1048576 | tf_op jit(solution)/shard_map/pallas_call | solution.py:32
  3.4 7.9 %all-to-all-start = ((bf16[8,272,128]{2,1,0:T(8,128)(2,1)}), bf16[8,272,128]{2,1,0:T(8,128)(2,1)S(1)}, u32[]{:S(2)}, u32[]{:S(2)}) async-start(bf16[8,272,128]{2,1,0:T(8,128)(2,1)} %bitcast.32), calls=%async_computation | async-start | bytes 1114112 | tf_op jit(solution)/shard_map/all_to_all | solution.py:697
  11.2 1.7 %shard_map.238 = (bf16[128,192]{1,0:T(8,128)(2,1)S(1)}, f32[8,512]{1,0:T(8,128)S(1)}, f32[8,512]{1,0:T(8,128)S(1)}, f32[16,512]{1,0:T(8,128)S(1)}, bf16[96,512]{...) custom-call(s32[64]{0:T(128)} %refs_0_.4, ...), custom_call_target="tpu_custom_call" | custom-call | flops 1048576 | bytes 1048576 | tf_op jit(solution)/shard_map/pallas_call | solution.py:32
  12.9 0.4 collective-permute-start.2
  13.3 1.2 %collective-permute-start.1 = (bf16[128,192]{1,0:T(8,128)(2,1)S(1)}, bf16[128,192]{1,0:T(8,128)(2,1)S(1)}, u32[]{:S(2)}, u32[]{:S(2)}) collective-permute-start(bf16[128,192]{1,0:T(8,128)(2,1)S(1)} %get-tuple-element.55.refs_0_), channel_id=1, source_target_pairs={{0,2},{1,3},{2,0},{3,1},{4,6},{5,7},{6,4},{7,5},{8,10},{9,11},{10,... | collective-permute-start | bytes 147464 | tf_op jit(solution)/shard_map/ppermute | solution.py:753
  14.5 0.3 collective-permute-start
  14.8 1.9 %shard_map.239 = (s32[8,128]{1,0:T(8,128)S(1)}, bf16[128,128]{1,0:T(8,128)(2,1)S(1)}, bf16[128,128]{1,0:T(8,128)(2,1)S(1)}, bf16[128,512]{1,0:T(8,128)(2,1)S(1)}...) custom-call(f32[16,512]{1,0:T(8,128)S(1)} %get-tuple-element.43.refs, ...), custom_call_target="tpu_custom_call" | custom-call | flops 1048576 | bytes 1048576 | tf_op jit(solution)/shard_map/pallas_call | solution.py:32
  16.8 0.6 %collective-permute-done.2.refs_3_ = bf16[128,192]{1,0:T(8,128)(2,1)S(1)} collective-permute-done((bf16[128,192]{1,0:T(8,128)(2,1)S(1)}, bf16[128,192]{1,0:T(8,128)(2,1)S(1)}, u32[]{:S(2)}, u32[]{:S(2)}) %collective-permute-start.2) | collective-permute-done | bytes 49184 | tf_op jit(solution)/shard_map/ppermute | solution.py:753
  17.3 1.4 %collective-permute-done.1.refs_2_ = bf16[128,192]{1,0:T(8,128)(2,1)S(1)} collective-permute-done((bf16[128,192]{1,0:T(8,128)(2,1)S(1)}, bf16[128,192]{1,0:T(8,128)(2,1)S(1)}, u32[]{:S(2)}, u32[]{:S(2)}) %collective-permute-start.1) | collective-permute-done | bytes 49184 | tf_op jit(solution)/shard_map/ppermute | solution.py:753
  18.8 0.0 collective-permute-done.refs_1_
  18.8 3.3 %shard_map.241 = (bf16[128,512]{1,0:T(8,128)(2,1)S(1)}, bf16[128,512]{1,0:T(8,128)(2,1)S(1)}, bf16[128,512]{1,0:T(8,128)(2,1)S(1)}, f32[128,512]{1,0:T(8,128)S(1...) custom-call(bf16[128,192]{1,0:T(8,128)(2,1)S(1)} %get-tuple-element., ...), custom_call_target="tpu_custom_call" | custom-call | flops 1048576 | bytes 1048576 | tf_op jit(solution)/shard_map/pallas_call | solution.py:32
  22.1 1.3 %all-to-all-done = bf16[8,272,128]{2,1,0:T(8,128)(2,1)S(1)} async-done(((bf16[8,272,128]{2,1,0:T(8,128)(2,1)}), bf16[8,272,128]{2,1,0:T(8,128)(2,1)S(1)}, u32[]{:S(2)}, u32[]{:S(2)}) %all-to-all-start) | async-done | bytes 557088 | tf_op jit(solution)/shard_map/all_to_all | solution.py:697
  23.5 0.4 shard_map.242
  23.9 0.0 collective-permute-start.5
  23.9 1.5 %collective-permute-start.4 = (f32[8,192]{1,0:T(8,128)S(1)}, f32[8,192]{1,0:T(8,128)S(1)}, u32[]{:S(2)}, u32[]{:S(2)}) collective-permute-start(f32[8,192]{1,0:T(8,128)S(1)} %get-tuple-element.69.refs_0_), channel_id=1, source_target_pairs={{0,2},{1,3},{2,0},{3,1},{4,6},{5,7},{6,4},{7,5},{8,10},{9,11},{10,... | collective-permute-start | bytes 18440 | tf_op jit(solution)/shard_map/ppermute | solution.py:753
  25.4 0.3 collective-permute-start.3
  25.8 1.1 %shard_map.243 = (bf16[8,64,512]{2,1,0:T(8,128)(2,1)S(1)}, bf16[8,64,16]{2,1,0:T(8,128)(2,1)S(1)}, bf16[8,16,128]{2,1,0:T(8,128)(2,1)S(1)}) custom-call(bf16[136,16,128]{2,1,0:T(8,128)(2,1)S(1)} %bitcast.30, f32[8,512]{1,0:T(8,128)S(1)} %get-tuple-element.52.refs_17_.refs_7_.refs_1_, f32[8,512]{1,0:T(8,128)S(1)} %get-tuple-element.53.refs_19_.refs_8_.refs_2_, ...), custom_call_target="tpu_custom_call" | custom-call | flops 1048576 | bytes 1048576 | tf_op jit(solution)/shard_map/pallas_call | solution.py:32
  26.8 0.2 collective-permute-done.5.refs_3_
  27.0 0.6 %collective-permute-done.4.refs_2_ = f32[8,192]{1,0:T(8,128)S(1)} collective-permute-done((f32[8,192]{1,0:T(8,128)S(1)}, f32[8,192]{1,0:T(8,128)S(1)}, u32[]{:S(2)}, u32[]{:S(2)}) %collective-permute-start.4) | collective-permute-done | bytes 6176 | tf_op jit(solution)/shard_map/ppermute | solution.py:753
  27.6 0.0 collective-permute-done.3.refs_1_
  27.6 2.0 %shard_map.244 = (bf16[136,16,128]{2,1,0:T(8,128)(2,1)}, bf16[8,64,512]{2,1,0:T(8,128)(2,1)S(1)}, f32[8,512]{1,0:T(8,128)S(1)}) custom-call(f32[8,192]{1,0:T(8,128)S(1)} %get-tuple-element.69.refs_0_, f32[8,192]{1,0:T(8,128)S(1)} %collective-permute-done.3.refs_1_, f32[8,192]{1,0:T(8,128)S(1)} %collective-permute-done.4.refs_2_, ...), custom_call_target="tpu_custom_call" | custom-call | flops 1048576 | bytes 1048576 | tf_op jit(solution)/shard_map/pallas_call | solution.py:32
  29.6 5.6 %all-to-all-start.1 = ((bf16[8,272,128]{2,1,0:T(8,128)(2,1)}), bf16[8,272,128]{2,1,0:T(8,128)(2,1)S(1)}, u32[]{:S(2)}, u32[]{:S(2)}) async-start(bf16[8,272,128]{2,1,0:T(8,128)(2,1)} %bitcast.34), calls=%async_computation.1 | async-start | bytes 1114112 | tf_op jit(solution)/shard_map/all_to_all | solution.py:697
  35.2 1.0 %shard_map.245 = (bf16[32,512]{1,0:T(8,128)(2,1)S(1)}, bf16[32,512]{1,0:T(8,128)(2,1)S(1)}, bf16[32,512]{1,0:T(8,128)(2,1)S(1)}, bf16[32,512]{1,0:T(8,128)(2,1)S(1)}) custom-call(bf16[8,4,2048]{2,1,0:T(4,128)(2,1)} %refs_0_.5, f32[16,512]{1,0:T(8,128)S(1)} %get-tuple-element.43.refs_0_.refs_4_.refs_3_.refs_6_.refs_12_.refs_1_.refs_13_, ...), custom_call_target="tpu_custom_call" | custom-call | flops 1048576 | bytes 1048576 | tf_op jit(solution)/shard_map/pallas_call | solution.py:32
  36.1 0.2 collective-permute-start.6
  36.4 1.4 %collective-permute-start.7 = (bf16[32,512]{1,0:T(8,128)(2,1)S(1)}, bf16[32,512]{1,0:T(8,128)(2,1)S(1)}, u32[]{:S(2)}, u32[]{:S(2)}) collective-permute-start(bf16[32,512]{1,0:T(8,128)(2,1)S(1)} %get-tuple-element.78), channel_id=1, source_target_pairs={{0,2},{1,3},{2,0},{3,1},{4,6},{5,7},{6,4},{7,5},{8,10},{9,11},{10,... | collective-permute-start | bytes 98312 | tf_op jit(solution)/shard_map/ppermute | solution.py:858
  37.8 0.3 collective-permute-start.8
  38.1 0.0 collective-permute-done.6.refs_1_
  38.1 2.2 %collective-permute-done.7.refs_2_ = bf16[32,512]{1,0:T(8,128)(2,1)S(1)} collective-permute-done((bf16[32,512]{1,0:T(8,128)(2,1)S(1)}, bf16[32,512]{1,0:T(8,128)(2,1)S(1)}, u32[]{:S(2)}, u32[]{:S(2)}) %collective-permute-start.7) | collective-permute-done | bytes 32800 | tf_op jit(solution)/shard_map/ppermute | solution.py:858
  40.3 0.8 %collective-permute-done.8.refs_3_ = bf16[32,512]{1,0:T(8,128)(2,1)S(1)} collective-permute-done((bf16[32,512]{1,0:T(8,128)(2,1)S(1)}, bf16[32,512]{1,0:T(8,128)(2,1)S(1)}, u32[]{:S(2)}, u32[]{:S(2)}) %collective-permute-start.8) | collective-permute-done | bytes 32800 | tf_op jit(solution)/shard_map/ppermute | solution.py:858
  41.1 4.5 %shard_map.246 = bf16[128,512]{1,0:T(8,128)(2,1)} custom-call(bf16[32,512]{1,0:T(8,128)(2,1)S(1)} %get-tuple-element.76.refs_0_, bf16[32,512]{1,0:T(8,128)(2,1)S(1)} %collective-permute-done.6.refs_1_, bf16[32,512]{1,0:T(8,128)(2,1)S(1)} %collective-permute-done.7.refs_2_, bf16[32,512]{1,0:T(8,128)(2,1)S(1)} %collective-permute-done.8.refs_3_, ...), custom_call_target="tpu_custom_call" | custom-call | flops 1048576 | bytes 1048576 | tf_op jit(solution)/shard_map/pallas_call | solution.py:32
  45.6 1.3 %all-to-all-done.1 = bf16[8,272,128]{2,1,0:T(8,128)(2,1)S(1)} async-done(((bf16[8,272,128]{2,1,0:T(8,128)(2,1)}), bf16[8,272,128]{2,1,0:T(8,128)(2,1)S(1)}, u32[]{:S(2)}, u32[]{:S(2)}) %all-to-all-start.1) | async-done | bytes 557088 | tf_op jit(solution)/shard_map/all_to_all | solution.py:697
  46.9 1.5 %shard_map.247 = (f32[128,2048]{1,0:T(8,128)}, f32[32,128]{1,0:T(8,128)}) custom-call(bf16[128,128]{1,0:T(8,128)(2,1)S(1)} %get-tuple-element.59.refs_12_.refs_23_.refs_20_.refs_11_.refs_15_.refs_0_, bf16[136,16,128]{2,1,0:T(8,128)(2,1)S(1)} %bitcast.31), custom_call_target="tpu_custom_call" | custom-call | flops 1048576 | bytes 1048576 | tf_op jit(solution)/shard_map/pallas_call | solution.py:32
Async XLA Ops:
  3.4 20.1 %all-to-all-start = ((bf16[8,272,128]{2,1,0:T(8,128)(2,1)}), bf16[8,272,128]{2,1,0:T(8,128)(2,1)S(1)}, u32[]{:S(2)}, u32[]{:S(2)}) async-start(bf16[8,272,128]{2,1,0:T(8,128)(2,1)} %bitcast.32), calls=%async_computation | async-start | bytes 1114112 | tf_op jit(solution)/shard_map/all_to_all | solution.py:697
  12.9 4.4 %collective-permute-start.2 = (bf16[128,192]{1,0:T(8,128)(2,1)S(1)}, bf16[128,192]{1,0:T(8,128)(2,1)S(1)}, u32[]{:S(2)}, u32[]{:S(2)}) collective-permute-start(bf16[128,192]{1,0:T(8,128)(2,1)S(1)} %get-tuple-element.55.refs_0_), channel_id=1, source_target_pairs={{0,3},{1,2},{2,1},{3,0},{4,7},{5,6},{6,5},{7,4},{8,11},{9,10},{10,... | collective-permute-start | bytes 147464 | tf_op jit(solution)/shard_map/ppermute | solution.py:753
  13.3 5.4 %collective-permute-start.1 = (bf16[128,192]{1,0:T(8,128)(2,1)S(1)}, bf16[128,192]{1,0:T(8,128)(2,1)S(1)}, u32[]{:S(2)}, u32[]{:S(2)}) collective-permute-start(bf16[128,192]{1,0:T(8,128)(2,1)S(1)} %get-tuple-element.55.refs_0_), channel_id=1, source_target_pairs={{0,2},{1,3},{2,0},{3,1},{4,6},{5,7},{6,4},{7,5},{8,10},{9,11},{10,... | collective-permute-start | bytes 147464 | tf_op jit(solution)/shard_map/ppermute | solution.py:753
  14.5 4.2 %collective-permute-start = (bf16[128,192]{1,0:T(8,128)(2,1)S(1)}, bf16[128,192]{1,0:T(8,128)(2,1)S(1)}, u32[]{:S(2)}, u32[]{:S(2)}) collective-permute-start(bf16[128,192]{1,0:T(8,128)(2,1)S(1)} %get-tuple-element.55.refs_0_), channel_id=1, source_target_pairs={{0,1},{1,0},{2,3},{3,2},{4,5},{5,4},{6,7},{7,6},{8,9},{9,8},{10,11... | collective-permute-start | bytes 147464 | tf_op jit(solution)/shard_map/ppermute | solution.py:753
  23.9 3.1 %collective-permute-start.5 = (f32[8,192]{1,0:T(8,128)S(1)}, f32[8,192]{1,0:T(8,128)S(1)}, u32[]{:S(2)}, u32[]{:S(2)}) collective-permute-start(f32[8,192]{1,0:T(8,128)S(1)} %get-tuple-element.69.refs_0_), channel_id=1, source_target_pairs={{0,3},{1,2},{2,1},{3,0},{4,7},{5,6},{6,5},{7,4},{8,11},{9,10},{10,... | collective-permute-start | bytes 18440 | tf_op jit(solution)/shard_map/ppermute | solution.py:753
  23.9 3.7 %collective-permute-start.4 = (f32[8,192]{1,0:T(8,128)S(1)}, f32[8,192]{1,0:T(8,128)S(1)}, u32[]{:S(2)}, u32[]{:S(2)}) collective-permute-start(f32[8,192]{1,0:T(8,128)S(1)} %get-tuple-element.69.refs_0_), channel_id=1, source_target_pairs={{0,2},{1,3},{2,0},{3,1},{4,6},{5,7},{6,4},{7,5},{8,10},{9,11},{10,... | collective-permute-start | bytes 18440 | tf_op jit(solution)/shard_map/ppermute | solution.py:753
  25.4 2.2 %collective-permute-start.3 = (f32[8,192]{1,0:T(8,128)S(1)}, f32[8,192]{1,0:T(8,128)S(1)}, u32[]{:S(2)}, u32[]{:S(2)}) collective-permute-start(f32[8,192]{1,0:T(8,128)S(1)} %get-tuple-element.69.refs_0_), channel_id=1, source_target_pairs={{0,1},{1,0},{2,3},{3,2},{4,5},{5,4},{6,7},{7,6},{8,9},{9,8},{10,11... | collective-permute-start | bytes 18440 | tf_op jit(solution)/shard_map/ppermute | solution.py:753
  29.6 17.4 %all-to-all-start.1 = ((bf16[8,272,128]{2,1,0:T(8,128)(2,1)}), bf16[8,272,128]{2,1,0:T(8,128)(2,1)S(1)}, u32[]{:S(2)}, u32[]{:S(2)}) async-start(bf16[8,272,128]{2,1,0:T(8,128)(2,1)} %bitcast.34), calls=%async_computation.1 | async-start | bytes 1114112 | tf_op jit(solution)/shard_map/all_to_all | solution.py:697
  36.1 1.9 %collective-permute-start.6 = (bf16[32,512]{1,0:T(8,128)(2,1)S(1)}, bf16[32,512]{1,0:T(8,128)(2,1)S(1)}, u32[]{:S(2)}, u32[]{:S(2)}) collective-permute-start(bf16[32,512]{1,0:T(8,128)(2,1)S(1)} %get-tuple-element.77), channel_id=1, source_target_pairs={{0,1},{1,0},{2,3},{3,2},{4,5},{5,4},{6,7},{7,6},{8,9},{9,8},{10,11... | collective-permute-start | bytes 98312 | tf_op jit(solution)/shard_map/ppermute | solution.py:858
  36.4 3.9 %collective-permute-start.7 = (bf16[32,512]{1,0:T(8,128)(2,1)S(1)}, bf16[32,512]{1,0:T(8,128)(2,1)S(1)}, u32[]{:S(2)}, u32[]{:S(2)}) collective-permute-start(bf16[32,512]{1,0:T(8,128)(2,1)S(1)} %get-tuple-element.78), channel_id=1, source_target_pairs={{0,2},{1,3},{2,0},{3,1},{4,6},{5,7},{6,4},{7,5},{8,10},{9,11},{10,... | collective-permute-start | bytes 98312 | tf_op jit(solution)/shard_map/ppermute | solution.py:858
  37.8 3.3 %collective-permute-start.8 = (bf16[32,512]{1,0:T(8,128)(2,1)S(1)}, bf16[32,512]{1,0:T(8,128)(2,1)S(1)}, u32[]{:S(2)}, u32[]{:S(2)}) collective-permute-start(bf16[32,512]{1,0:T(8,128)(2,1)S(1)} %get-tuple-element.79), channel_id=1, source_target_pairs={{0,3},{1,2},{2,1},{3,0},{4,7},{5,6},{6,5},{7,4},{8,11},{9,10},{10,... | collective-permute-start | bytes 98312 | tf_op jit(solution)/shard_map/ppermute | solution.py:858
